TPU v7x, 256 devices: a whole 4x4x8 slice. The times are simulated.
256 devices in a mesh: tm: 16 (over y_lo, x, core), space: 16 (over z, y_hi).
Axes of the slice: x: 4, y: 4 (y_hi: 2, y_lo: 2; y = y_hi * 2 + y_lo), z: 8, core: 2. Of those that a mesh axis runs over, the one named last changes fastest.
Arguments:
- states: bfloat16 [32, 64, 128, 256], P('tm', None, 'space'), may hold values from -6 to 6
- observed: bfloat16 [32, 64, 128, 256], P('tm', None, 'space'), may hold values from -6 to 6
- station_mask: int32 [32, 128, 256], P('tm', 'space'), may hold values 0 or 1
- noise: float32 [32, 64, 128, 256], P('tm', None, 'space'), may hold values from -6 to 6
- sigma_now: float32 [1], replicated, may hold values from 0.8 to 1.2
- sigma_next: float32 [1], replicated, may hold values from 0.3 to 0.6
- first_kernel: bfloat16 [3, 3, 96, 320], replicated, may hold values from -0.109375 to 0.109375
- second_kernel: bfloat16 [3, 3, 96, 96], replicated, may hold values from -0.21875 to 0.21875
- out_weight: bfloat16 [64, 96], replicated, may hold values from -0.625 to 0.625
Outputs:
- next_states: float32 [32, 64, 128, 256], P('tm', None, 'space')
All inputs are finite; a program needn't handle non-finite values. No bound on the sum of `station_mask` on one device may be relied on, other than what follows from the above.
Results may differ from a plain program's by a relative error of at most 0.00054.
Values may be sent and summed in bfloat16 or wider, within the bound.
No kernel may reach another device: no remote copies, remote signals or barrier semaphores. Data moves between devices by JAX's collectives and lax.ppermute only.
A program may use at most 64 MiB of HBM per device.

v0:
```python
import jax
import jax.numpy as jnp
from jax import lax
from jax.sharding import PartitionSpec as P


def padded_2(block, sides, width):
    for axis, dim in sides:
        count = lax.axis_size(axis)
        forward = [(i, i + 1) for i in range(count - 1)]
        backward = [(target, source) for source, target in forward]
        low = lax.ppermute(
            lax.slice_in_dim(block, block.shape[dim] - width, None, axis=dim), axis, forward
        )
        high = lax.ppermute(lax.slice_in_dim(block, 0, width, axis=dim), axis, backward)
        block = jnp.concatenate([low, block, high], axis=dim)
    return block


def conv_block(source, kernel):
    rows = source.shape[2] - 2
    width = source.shape[3]
    padded = jnp.pad(source, ((0, 0), (0, 0), (0, 0), (1, 1)))
    total = None
    for offa in range(3):
        for offb in range(3):
            piece = padded[:, :, offa : offa + rows, offb : offb + width]
            term = jnp.einsum(
                "oc,sclw->solw", kernel[offa, offb], piece, preferred_element_type=jnp.float32
            )
            total = term if total is None else total + term
    return total


def body(
    states,
    observed,
    station_mask,
    noise,
    sigma_now,
    sigma_next,
    first_kernel,
    second_kernel,
    out_weight,
):
    level = sigma_now[0]
    later = sigma_next[0]
    scale_in = 1.0 / jnp.sqrt(1.0 + level * level)
    count = states.shape[0]
    depth = 1
    timed = padded_2(states, (("tm", 0),), 2)
    extended = padded_2(timed, (("space", 2),), depth)
    window = jnp.concatenate([extended[k : k + count] for k in range(5)], axis=1)
    pre_one = conv_block(window, first_kernel)
    hidden_one = jax.nn.silu(pre_one * scale_in)
    hidden_one = hidden_one.astype(jnp.bfloat16)
    hidden_pad = padded_2(hidden_one, (("space", 2),), 1)
    hidden_two = jax.nn.silu(conv_block(hidden_pad, second_kernel)).astype(jnp.bfloat16)
    estimate = jnp.einsum(
        "co,solw->sclw", out_weight, hidden_two, preferred_element_type=jnp.float32
    )
    current = states.astype(jnp.float32)
    weight_obs = station_mask.astype(jnp.float32)[:, None, :, :]
    score = -estimate / level + weight_obs * (observed.astype(jnp.float32) - current) / (
        0.1 + level * level
    )
    drop = level * level - later * later
    return current + drop * score + jnp.sqrt(drop) * noise


def solution(mesh):
    in_specs = (
        P("tm", None, "space", None),
        P("tm", None, "space", None),
        P("tm", "space", None),
        P("tm", None, "space", None),
        P(),
        P(),
        P(),
        P(),
        P(),
    )
    out_specs = P("tm", None, "space", None)
    return jax.shard_map(body, mesh=mesh, in_specs=in_specs, out_specs=out_specs, check_vma=False)
```

profile of v0, /device:TPU:120, one launch (start us, length us, event | category | flops | bytes accessed | tf_op | source)
XLA Modules:
  0.0 77.7 jit_solution(3493887173999028996)
XLA Ops:
  0.0 1.2 %copy.10 = bf16[2,64,8,256]{3,1,2,0:T(8,128)(2,1)S(1)} copy(bf16[2,64,8,256]{3,2,1,0:T(8,128)(2,1)} %param.9) | data formatting | bytes 1048576 | tf_op args[0]
  1.2 1.9 %collective-permute-start = (bf16[2,64,8,256]{3,1,2,0:T(8,128)(2,1)S(1)}, bf16[2,64,8,256]{3,1,2,0:T(8,128)(2,1)S(1)}, u32[]{:S(2)}, u32[]{:S(2)}) collective-permute-start(bf16[2,64,8,256]{3,1,2,0:T(8,128)(2,1)S(1)} %copy.10), channel_id=1, source_target_pairs={{0,16},{16,32},{32,48},{48,64},{64,80},{80,96},{96,112},{112,128},... | collective-permute-start | bytes 1572872 | tf_op jit(solution)/shard_map/ppermute | solution.py:12
  3.2 5.8 %collective-permute-start.1 = (bf16[2,64,8,256]{3,1,2,0:T(8,128)(2,1)S(1)}, bf16[2,64,8,256]{3,1,2,0:T(8,128)(2,1)S(1)}, u32[]{:S(2)}, u32[]{:S(2)}) collective-permute-start(bf16[2,64,8,256]{3,1,2,0:T(8,128)(2,1)S(1)} %copy.10), channel_id=1, source_target_pairs={{16,0},{32,16},{48,32},{64,48},{80,64},{96,80},{112,96},{128,112},... | collective-permute-start | bytes 1572872 | tf_op jit(solution)/shard_map/ppermute | solution.py:15
  8.9 5.2 %collective-permute-done = bf16[2,64,8,256]{3,1,2,0:T(8,128)(2,1)S(1)} collective-permute-done((bf16[2,64,8,256]{3,1,2,0:T(8,128)(2,1)S(1)}, bf16[2,64,8,256]{3,1,2,0:T(8,128)(2,1)S(1)}, u32[]{:S(2)}, u32[]{:S(2)}) %collective-permute-start) | collective-permute-done | bytes 524320 | tf_op jit(solution)/shard_map/ppermute | solution.py:12
  14.3 2.7 %collective-permute-done.1 = bf16[2,64,8,256]{3,1,2,0:T(8,128)(2,1)S(1)} collective-permute-done((bf16[2,64,8,256]{3,1,2,0:T(8,128)(2,1)S(1)}, bf16[2,64,8,256]{3,1,2,0:T(8,128)(2,1)S(1)}, u32[]{:S(2)}, u32[]{:S(2)}) %collective-permute-start.1) | collective-permute-done | bytes 524320 | tf_op jit(solution)/shard_map/ppermute | solution.py:15
  17.1 4.3 %collective-permute-start.2 = (bf16[6,64,1,256]{3,1,2,0:T(8,128)(2,1)S(1)}, bf16[6,64,1,256]{3,1,2,0:T(8,128)(2,1)S(1)}, u32[]{:S(2)}, u32[]{:S(2)}) collective-permute-start(bf16[6,64,1,256]{3,1,2,0:T(8,128)(2,1)S(1)} %get-tuple-element.5), channel_id=1, source_target_pairs={{0,1},{1,2},{2,3},{3,4},{4,5},{5,6},{6,7},{7,8},{8,9},{9,10},{10,1... | collective-permute-start | bytes 589832 | tf_op jit(solution)/shard_map/ppermute | solution.py:12
  21.4 3.1 %collective-permute-start.3 = (bf16[6,64,1,256]{3,1,2,0:T(8,128)(2,1)S(1)}, bf16[6,64,1,256]{3,1,2,0:T(8,128)(2,1)S(1)}, u32[]{:S(2)}, u32[]{:S(2)}) collective-permute-start(bf16[6,64,1,256]{3,1,2,0:T(8,128)(2,1)S(1)} %get-tuple-element.6), channel_id=1, source_target_pairs={{1,0},{2,1},{3,2},{4,3},{5,4},{6,5},{7,6},{8,7},{9,8},{10,9},{11,1... | collective-permute-start | bytes 589832 | tf_op jit(solution)/shard_map/ppermute | solution.py:15
  26.2 6.9 %collective-permute-done.3 = bf16[6,64,1,256]{3,1,2,0:T(8,128)(2,1)S(1)} collective-permute-done((bf16[6,64,1,256]{3,1,2,0:T(8,128)(2,1)S(1)}, bf16[6,64,1,256]{3,1,2,0:T(8,128)(2,1)S(1)}, u32[]{:S(2)}, u32[]{:S(2)}) %collective-permute-start.3) | collective-permute-done | bytes 196640 | tf_op jit(solution)/shard_map/ppermute | solution.py:15
  33.6 1.0 %copy-done.2 = bf16[3,3,96,320]{3,2,1,0:T(8,128)(2,1)S(1)} copy-done((bf16[3,3,96,320]{3,2,1,0:T(8,128)(2,1)S(1)}, bf16[3,3,96,320]{3,2,1,0:T(8,128)(2,1)}, u32[]{:S(2)}) %copy-start.2) | copy-done | bytes 552984
  34.6 0.9 %fusion.1 = f32[2,8,256,96]{2,3,1,0:T(8,128)S(1)} fusion(bf16[2,320,10,256]{3,1,2,0:T(8,128)(2,1)S(1)} %slice_dynamic-update-slice_fusion, bf16[3,3,96,320]{3,2,1,0:T(8,128)(2,1)S(1)} %copy-done.2), kind=kOutput, calls=%fused_computation.9 | convolution fusion | flops 251658240 | bytes 4923392 | tf_op jit(solution)/shard_map/oc,sclw->solw/dot_general | solution.py:28
  35.5 0.7 fusion.11
  36.2 0.9 %fusion.2 = f32[2,8,256,96]{2,3,1,0:T(8,128)S(1)} fusion(bf16[2,320,10,256]{3,1,2,0:T(8,128)(2,1)S(1)} %slice_dynamic-update-slice_fusion, bf16[3,3,96,320]{3,2,1,0:T(8,128)(2,1)S(1)} %copy-done.2), kind=kOutput, calls=%fused_computation.10 | convolution fusion | flops 251658240 | bytes 4923392 | tf_op jit(solution)/shard_map/oc,sclw->solw/dot_general | solution.py:28
  37.2 0.9 %fusion.3 = f32[2,8,256,96]{2,3,1,0:T(8,128)S(1)} fusion(bf16[2,320,10,256]{3,1,2,0:T(8,128)(2,1)S(1)} %slice_dynamic-update-slice_fusion, bf16[3,3,96,320]{3,2,1,0:T(8,128)(2,1)S(1)} %copy-done.2), kind=kOutput, calls=%fused_computation.11 | convolution fusion | flops 251658240 | bytes 4923392 | tf_op jit(solution)/shard_map/oc,sclw->solw/dot_general | solution.py:28
  38.1 0.9 %fusion.4 = f32[2,8,256,96]{2,3,1,0:T(8,128)S(1)} fusion(bf16[2,320,10,256]{3,1,2,0:T(8,128)(2,1)S(1)} %slice_dynamic-update-slice_fusion, bf16[3,3,96,320]{3,2,1,0:T(8,128)(2,1)S(1)} %copy-done.2), kind=kOutput, calls=%fused_computation.12 | convolution fusion | flops 251658240 | bytes 4923392 | tf_op jit(solution)/shard_map/oc,sclw->solw/dot_general | solution.py:28
  39.1 0.9 %fusion.5 = f32[2,8,256,96]{2,3,1,0:T(8,128)S(1)} fusion(bf16[2,320,10,256]{3,1,2,0:T(8,128)(2,1)S(1)} %slice_dynamic-update-slice_fusion, bf16[3,3,96,320]{3,2,1,0:T(8,128)(2,1)S(1)} %copy-done.2), kind=kOutput, calls=%fused_computation.13 | convolution fusion | flops 251658240 | bytes 4923392 | tf_op jit(solution)/shard_map/oc,sclw->solw/dot_general | solution.py:28
  40.0 0.7 fusion.7
  40.7 0.7 fusion.9
  41.4 1.6 %fusion.23 = bf16[2,96,8,256]{3,1,2,0:T(8,128)(2,1)S(1)} fusion(f32[2,8,256,96]{2,3,1,0:T(8,128)S(1)} %fusion.7, f32[2,8,256,96]{2,3,1,0:T(8,128)S(1)} %fusion.5, f32[2,8,256,96]{2,3,1,0:T(8,128)S(1)} %fusion.4, f32[2,8,256,96]{2,3,1,0:T(8,128)S(1)} %fusion.9, f32[2,8,256,96]{2,3,1,0:T(8,128)S(1)} %fusion.3, f32[2,8,256,96]{2,3,1,0:T(8,128)S(1)} %fusion.2, ...), kind=kOutput, calls=%fused_computation.36 | convolution fusion | flops 257163264 | bytes 16719876 | tf_op jit(solution)/shard_map/oc,sclw->solw/dot_general | solution.py:28
  43.1 4.5 %collective-permute-start.4 = (bf16[2,96,1,256]{3,1,2,0:T(8,128)(2,1)S(1)}, bf16[2,96,1,256]{3,1,2,0:T(8,128)(2,1)S(1)}, u32[]{:S(2)}, u32[]{:S(2)}) collective-permute-start(bf16[2,96,1,256]{3,1,2,0:T(8,128)(2,1)S(1)} %get-tuple-element.7), channel_id=1, source_target_pairs={{0,1},{1,2},{2,3},{3,4},{4,5},{5,6},{6,7},{7,8},{8,9},{9,10},{10,1... | collective-permute-start | bytes 294920 | tf_op jit(solution)/shard_map/ppermute | solution.py:12
  47.6 3.0 %collective-permute-start.5 = (bf16[2,96,1,256]{3,1,2,0:T(8,128)(2,1)S(1)}, bf16[2,96,1,256]{3,1,2,0:T(8,128)(2,1)S(1)}, u32[]{:S(2)}, u32[]{:S(2)}) collective-permute-start(bf16[2,96,1,256]{3,1,2,0:T(8,128)(2,1)S(1)} %get-tuple-element.8), channel_id=1, source_target_pairs={{1,0},{2,1},{3,2},{4,3},{5,4},{6,5},{7,6},{8,7},{9,8},{10,9},{11,1... | collective-permute-start | bytes 294920 | tf_op jit(solution)/shard_map/ppermute | solution.py:15
  50.6 1.5 %fusion.77 = f32[2,8,256,96]{2,3,1,0:T(8,128)} fusion(bf16[2,96,8,256]{3,1,2,0:T(8,128)(2,1)S(1)} %fusion.23, bf16[3,3,96,96]{3,2,1,0:T(8,128)(2,1)S(1)} %copy-done.3), kind=kOutput, calls=%fused_computation.95 | convolution fusion | flops 75497472 | bytes 2383872 | tf_op jit(solution)/shard_map/oc,sclw->solw/dot_general | solution.py:28
  52.1 5.5 %collective-permute-done.5 = bf16[2,96,1,256]{3,1,2,0:T(8,128)(2,1)S(1)} collective-permute-done((bf16[2,96,1,256]{3,1,2,0:T(8,128)(2,1)S(1)}, bf16[2,96,1,256]{3,1,2,0:T(8,128)(2,1)S(1)}, u32[]{:S(2)}, u32[]{:S(2)}) %collective-permute-start.5) | collective-permute-done | bytes 98336 | tf_op jit(solution)/shard_map/ppermute | solution.py:15
  57.7 0.9 %fusion.25 = bf16[2,96,10,258]{3,1,2,0:T(8,128)(2,1)S(1)} fusion(bf16[2,96,1,256]{3,1,2,0:T(8,128)(2,1)S(1)} %collective-permute-done.5, bf16[2,96,8,256]{3,1,2,0:T(8,128)(2,1)S(1)} %fusion.23, bf16[2,96,1,256]{3,1,2,0:T(8,128)(2,1)S(1)} %collective-permute-done.4), kind=kLoop, calls=%fused_computation.38 | loop fusion | flops 5944320 | bytes 1973760 | tf_op jit(solution)/shard_map/concatenate | solution.py:16
  58.5 1.5 %fusion.40 = f32[2,8,256,96]{2,3,1,0:T(8,128)} fusion(bf16[2,96,10,258]{3,1,2,0:T(8,128)(2,1)S(1)} %fusion.25, bf16[3,3,96,96]{3,2,1,0:T(8,128)(2,1)S(1)} %copy-done.3), kind=kOutput, calls=%fused_computation.55 | convolution fusion | flops 75497472 | bytes 2383872 | tf_op jit(solution)/shard_map/oc,sclw->solw/dot_general | solution.py:28
  60.1 1.6 %fusion.42 = f32[2,8,256,96]{2,3,1,0:T(8,128)} fusion(bf16[2,96,10,258]{3,1,2,0:T(8,128)(2,1)S(1)} %fusion.25, bf16[3,3,96,96]{3,2,1,0:T(8,128)(2,1)S(1)} %copy-done.3), kind=kOutput, calls=%fused_computation.57 | convolution fusion | flops 75497472 | bytes 2383872 | tf_op jit(solution)/shard_map/oc,sclw->solw/dot_general | solution.py:28
  61.6 1.5 %fusion.44 = f32[2,8,256,96]{2,3,1,0:T(8,128)} fusion(bf16[2,96,10,258]{3,1,2,0:T(8,128)(2,1)S(1)} %fusion.25, bf16[3,3,96,96]{3,2,1,0:T(8,128)(2,1)S(1)} %copy-done.3), kind=kOutput, calls=%fused_computation.59 | convolution fusion | flops 75497472 | bytes 2383872 | tf_op jit(solution)/shard_map/oc,sclw->solw/dot_general | solution.py:28
  63.1 1.7 %fusion.46 = f32[2,8,256,96]{2,3,1,0:T(8,128)} fusion(bf16[2,96,10,258]{3,1,2,0:T(8,128)(2,1)S(1)} %fusion.25, bf16[3,3,96,96]{3,2,1,0:T(8,128)(2,1)S(1)} %copy-done.3), kind=kOutput, calls=%fused_computation.61 | convolution fusion | flops 75497472 | bytes 2383872 | tf_op jit(solution)/shard_map/oc,sclw->solw/dot_general | solution.py:28
  64.8 1.5 %fusion.50 = f32[2,8,256,96]{2,3,1,0:T(8,128)} fusion(bf16[2,96,10,258]{3,1,2,0:T(8,128)(2,1)S(1)} %fusion.25, bf16[3,3,96,96]{3,2,1,0:T(8,128)(2,1)S(1)} %copy-done.3), kind=kOutput, calls=%fused_computation.66 | convolution fusion | flops 75497472 | bytes 2383872 | tf_op jit(solution)/shard_map/oc,sclw->solw/dot_general | solution.py:28
  66.3 1.5 %fusion.48 = f32[2,8,256,96]{2,3,1,0:T(8,128)} fusion(bf16[2,96,8,256]{3,1,2,0:T(8,128)(2,1)S(1)} %fusion.23, bf16[2,96,1,256]{3,1,2,0:T(8,128)(2,1)S(1)} %collective-permute-done.4, bf16[3,3,96,96]{3,2,1,0:T(8,128)(2,1)S(1)} %copy-done.3), kind=kOutput, calls=%fused_computation.64 | convolution fusion | flops 77070336 | bytes 2482176 | tf_op jit(solution)/shard_map/oc,sclw->solw/dot_general | solution.py:28
  67.8 1.5 %fusion.38 = f32[2,8,256,96]{2,3,1,0:T(8,128)} fusion(bf16[2,96,1,256]{3,1,2,0:T(8,128)(2,1)S(1)} %collective-permute-done.5, bf16[2,96,8,256]{3,1,2,0:T(8,128)(2,1)S(1)} %fusion.23, bf16[3,3,96,96]{3,2,1,0:T(8,128)(2,1)S(1)} %copy-done.3), kind=kOutput, calls=%fused_computation.53 | convolution fusion | flops 77070336 | bytes 2482176 | tf_op jit(solution)/shard_map/oc,sclw->solw/dot_general | solution.py:28
  69.4 6.7 %fusion.31 = f32[2,64,8,256]{3,1,2,0:T(8,128)S(1)} fusion(f32[2,64,8,256]{3,2,1,0:T(8,128)} %param.12, f32[2,8,256,96]{2,3,1,0:T(8,128)} %fusion.38, f32[2,8,256,96]{2,3,1,0:T(8,128)} %fusion.40, f32[2,8,256,96]{2,3,1,0:T(8,128)} %fusion.42, f32[2,8,256,96]{2,3,1,0:T(8,128)} %fusion.77, f32[2,8,256,96]{2,3,1,0:T(8,128)} %fusion.44, ...), kind=kOutput, calls=%fused_computation.45 | convolution fusion | flops 134086656 | bytes 16572432 | tf_op jit(solution)/shard_map/co,solw->sclw/dot_general | solution.py:59
  76.1 1.6 %copy.16 = f32[2,64,8,256]{3,2,1,0:T(8,128)} copy(f32[2,64,8,256]{3,1,2,0:T(8,128)S(1)} %fusion.31) | data formatting | bytes 2097152 | tf_op jit(solution)/shard_map/add | solution.py:68
  (23 shorter events, 1.0 us)
Async XLA Ops:
  0.0 69.4 %copy-start = (bf16[64,96]{1,0:T(8,128)(2,1)S(1)}, bf16[64,96]{1,0:T(8,128)(2,1)}, u32[]{:S(2)}) copy-start(bf16[64,96]{1,0:T(8,128)(2,1)} %param.17) | copy-start | bytes 36868
  0.0 14.2 %copy-start.1 = (bf16[2,64,8,256]{3,2,1,0:T(8,128)(2,1)S(1)}, bf16[2,64,8,256]{3,2,1,0:T(8,128)(2,1)}, u32[]{:S(2)}) copy-start(bf16[2,64,8,256]{3,2,1,0:T(8,128)(2,1)} %param.9) | copy-start | bytes 1572868
  1.2 12.9 %collective-permute-start = (bf16[2,64,8,256]{3,1,2,0:T(8,128)(2,1)S(1)}, bf16[2,64,8,256]{3,1,2,0:T(8,128)(2,1)S(1)}, u32[]{:S(2)}, u32[]{:S(2)}) collective-permute-start(bf16[2,64,8,256]{3,1,2,0:T(8,128)(2,1)S(1)} %copy.10), channel_id=1, source_target_pairs={{0,16},{16,32},{32,48},{48,64},{64,80},{80,96},{96,112},{112,128},... | collective-permute-start | bytes 1572872 | tf_op jit(solution)/shard_map/ppermute | solution.py:12
  3.2 13.9 %collective-permute-start.1 = (bf16[2,64,8,256]{3,1,2,0:T(8,128)(2,1)S(1)}, bf16[2,64,8,256]{3,1,2,0:T(8,128)(2,1)S(1)}, u32[]{:S(2)}, u32[]{:S(2)}) collective-permute-start(bf16[2,64,8,256]{3,1,2,0:T(8,128)(2,1)S(1)} %copy.10), channel_id=1, source_target_pairs={{16,0},{32,16},{48,32},{64,48},{80,64},{96,80},{112,96},{128,112},... | collective-permute-start | bytes 1572872 | tf_op jit(solution)/shard_map/ppermute | solution.py:15
  14.2 11.7 %copy-start.4 = (s32[2,8,256]{2,1,0:T(8,128)S(1)}, s32[2,8,256]{2,1,0:T(8,128)}, u32[]{:S(2)}) copy-start(s32[2,8,256]{2,1,0:T(8,128)} %param.11) | copy-start | bytes 49156
  17.1 9.1 %collective-permute-start.2 = (bf16[6,64,1,256]{3,1,2,0:T(8,128)(2,1)S(1)}, bf16[6,64,1,256]{3,1,2,0:T(8,128)(2,1)S(1)}, u32[]{:S(2)}, u32[]{:S(2)}) collective-permute-start(bf16[6,64,1,256]{3,1,2,0:T(8,128)(2,1)S(1)} %get-tuple-element.5), channel_id=1, source_target_pairs={{0,1},{1,2},{2,3},{3,4},{4,5},{5,6},{6,7},{7,8},{8,9},{9,10},{10,1... | collective-permute-start | bytes 589832 | tf_op jit(solution)/shard_map/ppermute | solution.py:12
  21.4 11.7 %collective-permute-start.3 = (bf16[6,64,1,256]{3,1,2,0:T(8,128)(2,1)S(1)}, bf16[6,64,1,256]{3,1,2,0:T(8,128)(2,1)S(1)}, u32[]{:S(2)}, u32[]{:S(2)}) collective-permute-start(bf16[6,64,1,256]{3,1,2,0:T(8,128)(2,1)S(1)} %get-tuple-element.6), channel_id=1, source_target_pairs={{1,0},{2,1},{3,2},{4,3},{5,4},{6,5},{7,6},{8,7},{9,8},{10,9},{11,1... | collective-permute-start | bytes 589832 | tf_op jit(solution)/shard_map/ppermute | solution.py:15
  33.5 1.1 %copy-start.2 = (bf16[3,3,96,320]{3,2,1,0:T(8,128)(2,1)S(1)}, bf16[3,3,96,320]{3,2,1,0:T(8,128)(2,1)}, u32[]{:S(2)}) copy-start(bf16[3,3,96,320]{3,2,1,0:T(8,128)(2,1)} %param.15) | copy-start | bytes 1658884
  41.4 9.2 %copy-start.3 = (bf16[3,3,96,96]{3,2,1,0:T(8,128)(2,1)S(1)}, bf16[3,3,96,96]{3,2,1,0:T(8,128)(2,1)}, u32[]{:S(2)}) copy-start(bf16[3,3,96,96]{3,2,1,0:T(8,128)(2,1)} %param.16) | copy-start | bytes 497668
  43.1 9.1 %collective-permute-start.4 = (bf16[2,96,1,256]{3,1,2,0:T(8,128)(2,1)S(1)}, bf16[2,96,1,256]{3,1,2,0:T(8,128)(2,1)S(1)}, u32[]{:S(2)}, u32[]{:S(2)}) collective-permute-start(bf16[2,96,1,256]{3,1,2,0:T(8,128)(2,1)S(1)} %get-tuple-element.7), channel_id=1, source_target_pairs={{0,1},{1,2},{2,3},{3,4},{4,5},{5,6},{6,7},{7,8},{8,9},{9,10},{10,1... | collective-permute-start | bytes 294920 | tf_op jit(solution)/shard_map/ppermute | solution.py:12
  47.6 10.1 %collective-permute-start.5 = (bf16[2,96,1,256]{3,1,2,0:T(8,128)(2,1)S(1)}, bf16[2,96,1,256]{3,1,2,0:T(8,128)(2,1)S(1)}, u32[]{:S(2)}, u32[]{:S(2)}) collective-permute-start(bf16[2,96,1,256]{3,1,2,0:T(8,128)(2,1)S(1)} %get-tuple-element.8), channel_id=1, source_target_pairs={{1,0},{2,1},{3,2},{4,3},{5,4},{6,5},{7,6},{8,7},{9,8},{10,9},{11,1... | collective-permute-start | bytes 294920 | tf_op jit(solution)/shard_map/ppermute | solution.py:15
where the time goes:
time: 78 us; the launch traced here: 77.7 us
  matrix products  27.4 us (35%)
  starting transfers between devices  22.5 us (29%)
  waiting for transfers between devices  20.7 us (27%)
  local copies, waits for them, and re-layouts  4.25 us (5%)
  between operations  1.64 us (2%)
  other arithmetic  1.1 us (1%)
    dot_general x17, matrix products, conv_block(): jnp.einsum('oc,sclw->solw', kernel[offa, offb], piece, preferred_element_...  20.8 us
    ppermute x3, waiting for transfers between devices, padded_2(): lax.ppermute(lax.slice_in_dim(block, 0, width, axis=dim), axis, backward)  15.2 us
    ppermute x3, starting transfers between devices, padded_2(): lax.ppermute(lax.slice_in_dim(block, 0, width, axis=dim), axis, backward)  11.8 us
    ppermute x3, starting transfers between devices, padded_2(): lax.ppermute(lax.slice_in_dim(block, block.shape[dim] - width, None, axis...  10.7 us
    dot_general x1, matrix products, body(): jnp.einsum('co,solw->sclw', out_weight, hidden_two, preferred_element_typ...  6.69 us
    ppermute x3, waiting for transfers between devices, padded_2(): lax.ppermute(lax.slice_in_dim(block, block.shape[dim] - width, None, axis...  5.52 us
    unnamed x17, local copies, waits for them, and re-layouts  2.55 us
    add x1, local copies, waits for them, and re-layouts, body(): return current + drop * score + jnp.sqrt(drop) * noise  1.58 us
  transfers between devices with their start and end apart: 6, of which 5 were waited for; matrix products, arithmetic and copies ran while one was open for 2% of the time, Pallas kernels for 0%

commit v1 on v0

v1 whole, which is shorter than its diff:
```python
import functools

import jax
import jax.numpy as jnp
from jax import lax
from jax.experimental import pallas as pl
from jax.experimental.pallas import tpu as pltpu
from jax.sharding import PartitionSpec as P

F32 = jnp.float32
BF16 = jnp.bfloat16
AXES = ("tm", "space")
WID = 256
CH = 64
HID = 96


def core_swap(x, tm):
    return lax.ppermute(x, "tm", [(i, i ^ 1) for i in range(tm)])


def side_swap(x, tm):
    pairs = [(i, ((i + 1) ^ 1) - 1) for i in range(tm)]
    return lax.ppermute(x, "tm", [(i, j) for i, j in pairs if 0 <= j < tm])


def row_swap(x, tm, space):
    pairs = []
    for t in range(tm):
        step = -1 if t % 2 == 0 else 1
        for s in range(space):
            if 0 <= s + step < space:
                pairs.append((t * space + s, (t ^ 1) * space + s + step))
    return lax.ppermute(x, AXES, pairs)


def rows_first(states_ref, out_ref):
    n = states_ref.shape[0] * CH
    out_ref[...] = jnp.swapaxes(states_ref[...].reshape(n, states_ref.shape[2], WID), 0, 1)


def silu(v):
    u = 0.5 * v
    return u + u * jnp.tanh(u)


def side_shifts(v):
    lane = lax.broadcasted_iota(jnp.int32, v.shape, v.ndim - 1)
    right = jnp.where(lane == 0, 0.0, pltpu.roll(v, 1, v.ndim - 1))
    left = jnp.where(lane == WID - 1, 0.0, pltpu.roll(v, WID - 1, v.ndim - 1))
    return right, left


def put_shifted(dst, row, start, size, block):
    right, left = side_shifts(block.astype(F32))
    dst[row, 0, pl.ds(start, size)] = right.astype(BF16)
    dst[row, 1, pl.ds(start, size)] = block
    dst[row, 2, pl.ds(start, size)] = left.astype(BF16)


def step_kernel(
    place_ref,
    scalar_ref,
    own_ref,
    partner_ref,
    remote_ref,
    rows_a_ref,
    rows_b_ref,
    corner_ref,
    first_ref,
    second_ref,
    proj_ref,
    mask_ref,
    states_v,
    observed_v,
    noise_v,
    out_hbm,
    xs,
    w_one,
    w_two,
    hs,
    h2s,
    est,
    out_v,
    sems,
):
    core = place_ref[0]
    has_up = place_ref[1]
    has_down = place_ref[2]
    cur_k = scalar_ref[0]
    est_k = scalar_ref[1]
    obs_k = scalar_ref[2]
    noise_k = scalar_ref[3]
    scale_in = scalar_ref[4]

    for a in range(3):
        for b in range(3):
            n = a * 3 + b
            w_one[:, n * 5 * CH : (n + 1) * 5 * CH] = first_ref[a, b]
            w_two[:, n * HID : (n + 1) * HID] = second_ref[a, b]

    partner_at = pl.multiple_of((1 - core) * 4 * CH, 2 * CH)
    remote_at = pl.multiple_of(core * 4 * CH, 2 * CH)
    local_at = pl.multiple_of((1 - core) * 2 * CH, 2 * CH)
    for l in range(8):
        put_shifted(xs, l + 2, 2 * CH, 2 * CH, own_ref[l])
        put_shifted(xs, l + 2, partner_at, 2 * CH, partner_ref[l])
        put_shifted(xs, l + 2, remote_at, 2 * CH, remote_ref[l])
    for l in range(2):
        top = jnp.where(core == 0, rows_a_ref[l], rows_b_ref[l])
        low = jnp.where(core == 0, rows_b_ref[l], rows_a_ref[l])
        put_shifted(xs, l, local_at, 4 * CH, top)
        put_shifted(xs, l + 10, local_at, 4 * CH, low)
        put_shifted(xs, l, remote_at, 2 * CH, corner_ref[l])
        put_shifted(xs, l + 10, remote_at, 2 * CH, corner_ref[l + 2])

    for t in range(2):
        for r in range(10):
            window = jnp.concatenate(
                [xs[r + a, b, t * CH : (t + 5) * CH] for a in range(3) for b in range(3)], axis=0
            )
            pre = jnp.dot(w_one[...], window, preferred_element_type=F32)
            hid = silu(pre * scale_in)
            if r == 0:
                hid = jnp.where(has_up > 0, hid, 0.0)
            if r == 9:
                hid = jnp.where(has_down > 0, hid, 0.0)
            right, left = side_shifts(hid)
            hs[r, 0] = right.astype(BF16)
            hs[r, 1] = hid.astype(BF16)
            hs[r, 2] = left.astype(BF16)
        for r in range(8):
            pre = jnp.dot(
                w_two[...], hs[r : r + 3].reshape(9 * HID, WID), preferred_element_type=F32
            )
            h2s[r] = silu(pre).astype(BF16)
        for r in range(8):
            val = jnp.dot(proj_ref[...], h2s[r], preferred_element_type=F32)
            est[0, pl.ds(r, CH, stride=8), :] = val[:, :128]
            est[1, pl.ds(r, CH, stride=8), :] = val[:, 128:]
        weight = mask_ref[t].astype(F32) * obs_k
        estimate = jnp.concatenate([est[0], est[1]], axis=1).reshape(CH, 8, WID)
        current = states_v[t].astype(F32)
        seen = observed_v[t].astype(F32)
        out_v[t] = (
            current
            + est_k * estimate
            + weight[None] * (seen - current)
            + noise_k * noise_v[t]
        )
        pltpu.make_async_copy(out_v.at[t], out_hbm.at[t], sems.at[t]).start()
    for t in range(2):
        pltpu.make_async_copy(out_v.at[t], out_hbm.at[t], sems.at[t]).wait()


def body(
    states,
    observed,
    station_mask,
    noise,
    sigma_now,
    sigma_next,
    first_kernel,
    second_kernel,
    out_weight,
):
    tm, space = lax.axis_size("tm"), lax.axis_size("space")
    core = lax.axis_index("tm") % 2
    row_at = lax.axis_index("space")
    is_zero = core == 0
    vmem = pl.BlockSpec(memory_space=pltpu.VMEM)
    smem = pl.BlockSpec(memory_space=pltpu.SMEM)
    anywhere = pl.BlockSpec(memory_space=pl.ANY)

    own = pl.pallas_call(
        rows_first,
        out_shape=jax.ShapeDtypeStruct((8, 2 * CH, WID), BF16),
        in_specs=[vmem],
        out_specs=vmem,
        name="rows_first",
    )(states)

    top, foot = own[:2], own[6:]
    keep = jnp.where(is_zero, top, foot)
    give = jnp.where(is_zero, foot, top)
    got = core_swap(give, tm)
    edge = jnp.concatenate([jnp.where(is_zero, keep, got), jnp.where(is_zero, got, keep)], axis=1)
    rows_a = row_swap(edge, tm, space)
    own_late, rows_late = lax.optimization_barrier((own, edge))
    partner = core_swap(own_late, tm)
    remote = side_swap(own_late, tm)
    rows_b = core_swap(rows_a, tm)
    mine_a = jnp.where(is_zero, rows_a[:, : 2 * CH], rows_a[:, 2 * CH :])
    mine_b = jnp.where(is_zero, rows_b[:, : 2 * CH], rows_b[:, 2 * CH :])
    upper = jnp.where(is_zero, mine_a, mine_b)
    lower = jnp.where(is_zero, mine_b, mine_a)
    corner = side_swap(jnp.concatenate([upper, lower], axis=0), tm)

    level, later = sigma_now[0], sigma_next[0]
    drop = level * level - later * later
    scalars = jnp.stack(
        [
            level,
            -drop / level,
            drop / (0.1 + level * level),
            jnp.sqrt(drop),
            1.0 / jnp.sqrt(1.0 + level * level),
        ]
    )
    place = jnp.stack([core, row_at > 0, row_at < space - 1]).astype(jnp.int32)

    return pl.pallas_call(
        step_kernel,
        out_shape=jax.ShapeDtypeStruct(noise.shape, F32),
        in_specs=[smem] * 2 + [vmem] * 13,
        out_specs=anywhere,
        scratch_shapes=[
            pltpu.VMEM((12, 3, 6 * CH, WID), BF16),
            pltpu.VMEM((HID, 45 * CH), BF16),
            pltpu.VMEM((HID, 9 * HID), BF16),
            pltpu.VMEM((10, 3, HID, WID), BF16),
            pltpu.VMEM((8, HID, WID), BF16),
            pltpu.VMEM((2, CH * 8, 128), F32),
            pltpu.VMEM(noise.shape, F32),
            pltpu.SemaphoreType.DMA((2,)),
        ],
        compiler_params=pltpu.CompilerParams(vmem_limit_bytes=40 * 2**20),
        name="step",
    )(
        place,
        scalars,
        own,
        partner,
        remote,
        rows_a,
        rows_b,
        corner,
        first_kernel,
        second_kernel,
        out_weight,
        station_mask,
        states,
        observed,
        noise,
    )


def solution(mesh):
    in_specs = (
        P("tm", None, "space", None),
        P("tm", None, "space", None),
        P("tm", "space", None),
        P("tm", None, "space", None),
        P(),
        P(),
        P(),
        P(),
        P(),
    )
    out_specs = P("tm", None, "space", None)
    return jax.shard_map(body, mesh=mesh, in_specs=in_specs, out_specs=out_specs, check_vma=False)
```

time: 78 us -> 48.2 us (0.62)
  the two profiles are of different devices: /device:TPU:120 before, /device:TPU:135 now
where the time goes in v1:
time: 48.2 us; the launch traced here: 47.4 us
  starting transfers between devices  13.7 us (28%)
  waiting for transfers between devices  13.1 us (27%)
  Pallas kernels  12.6 us (26%)
  local copies, waits for them, and re-layouts  3.51 us (7%)
  other arithmetic  2.9 us (6%)
  between operations  1.58 us (3%)
    pallas_call x1, Pallas kernels, body(): pl.pallas_call(step_kernel, out_shape=jax.ShapeDtypeStruct(noise.shape, F...  10.6 us
    ppermute x2, starting transfers between devices, side_swap(): return lax.ppermute(x, 'tm', [(i, j) for i, j in pairs if 0 <= j < tm])  7.65 us
    ppermute x1, waiting for transfers between devices, row_swap(): return lax.ppermute(x, AXES, pairs)  6.93 us
    ppermute x2, waiting for transfers between devices, side_swap(): return lax.ppermute(x, 'tm', [(i, j) for i, j in pairs if 0 <= j < tm])  5.23 us
    ppermute x1, starting transfers between devices, row_swap(): return lax.ppermute(x, AXES, pairs)  5.2 us
    unnamed x16, local copies, waits for them, and re-layouts  3.43 us
    pallas_call x1, Pallas kernels, body(): pl.pallas_call(rows_first, out_shape=jax.ShapeDtypeStruct((8, 2 * CH, WID...  1.97 us
    select_n x1, other arithmetic, body(): give = jnp.where(is_zero, foot, top)  1.05 us
  transfers between devices with their start and end apart: 6, of which 4 were waited for; matrix products, arithmetic and copies ran while one was open for 2% of the time, Pallas kernels for 0%

profile of v1, /device:TPU:135, one launch (start us, length us, event | category | flops | bytes accessed | tf_op | source)
XLA Modules:
  0.0 47.4 jit_solution(12668722789352189605)
XLA Ops:
  0.0 2.0 %rows_first.1.own_ref = bf16[8,128,256]{2,1,0:T(8,128)(2,1)} custom-call(bf16[2,64,8,256]{3,2,1,0:T(8,128)(2,1)} %states_v.1), custom_call_target="tpu_custom_call" | custom-call | tf_op jit(solution)/shard_map/rows_first/pallas_call | solution.py:175
  2.0 0.0 copy-start.3
  2.0 1.0 %broadcast_select_fusion.4 = bf16[2,128,256]{2,1,0:T(8,128)(2,1)S(1)} fusion(pred[]{:T(512)S(6)} %eq.5, bf16[8,128,256]{2,1,0:T(8,128)(2,1)} %rows_first.1.own_ref), kind=kLoop, calls=%fused_computation.8 | loop fusion | flops 65536 | bytes 393217 | tf_op jit(solution)/shard_map/jit(_where)/select_n | solution.py:185
  3.0 0.0 copy-start
  3.0 0.8 %collective-permute-start = (bf16[2,128,256]{2,1,0:T(8,128)(2,1)S(1)}, bf16[2,128,256]{2,1,0:T(8,128)(2,1)S(1)}, u32[]{:S(2)}, u32[]{:S(2)}) collective-permute-start(bf16[2,128,256]{2,1,0:T(8,128)(2,1)S(1)} %broadcast_select_fusion.4), channel_id=1, source_target_pairs={{0,16},{16,0},{32,48},{48,32},{64,80},{80,64},{96,112},{112,96},{1... | collective-permute-start | bytes 393224 | tf_op jit(solution)/shard_map/ppermute | solution.py:19
  3.8 1.0 %collective-permute-done = bf16[2,128,256]{2,1,0:T(8,128)(2,1)S(1)} collective-permute-done((bf16[2,128,256]{2,1,0:T(8,128)(2,1)S(1)}, bf16[2,128,256]{2,1,0:T(8,128)(2,1)S(1)}, u32[]{:S(2)}, u32[]{:S(2)}) %collective-permute-start) | collective-permute-done | bytes 131104 | tf_op jit(solution)/shard_map/ppermute | solution.py:19
  4.8 1.0 %broadcast_select_fusion.3 = (bf16[2,128,256]{2,1,0:T(8,128)(2,1)S(1)}, bf16[2,128,256]{2,1,0:T(8,128)(2,1)S(1)}) fusion(bf16[2,128,256]{2,1,0:T(8,128)(2,1)S(1)} %collective-permute-done, pred[]{:T(512)S(6)} %eq.5, bf16[8,128,256]{2,1,0:T(8,128)(2,1)} %rows_first.1.own_ref), kind=kLoop, calls=%fused_computation.7 | loop fusion | flops 196608 | bytes 655361 | tf_op jit(solution)/shard_map/jit(_where)/select_n | solution.py:187
  5.8 0.0 copy-start.2
  5.8 0.0 copy-start.1
  5.8 5.2 %collective-permute-start.3 = (bf16[2,256,256]{2,1,0:T(8,128)(2,1)S(1)}, bf16[2,256,256]{2,1,0:T(8,128)(2,1)S(1)}, u32[]{:S(2)}, u32[]{:S(2)}) collective-permute-start(bf16[2,256,256]{2,1,0:T(8,128)(2,1)S(1)} %pad_maximum_fusion), channel_id=1, source_target_pairs={{1,16},{2,17},{3,18},{4,19},{5,20},{6,21},{7,22},{8,23},{9,24},{10... | collective-permute-start | bytes 786440 | tf_op jit(solution)/shard_map/ppermute | solution.py:34
  11.0 6.9 %collective-permute-done.3.rows_a_ref = bf16[2,256,256]{2,1,0:T(8,128)(2,1)S(1)} collective-permute-done((bf16[2,256,256]{2,1,0:T(8,128)(2,1)S(1)}, bf16[2,256,256]{2,1,0:T(8,128)(2,1)S(1)}, u32[]{:S(2)}, u32[]{:S(2)}) %collective-permute-start.3) | collective-permute-done | bytes 262176 | tf_op jit(solution)/shard_map/ppermute | solution.py:34
  18.0 0.0 collective-permute-start.4
  18.0 0.0 copy-done
  18.0 3.5 %collective-permute-start.2 = (bf16[8,128,256]{2,1,0:T(8,128)(2,1)S(1)}, bf16[8,128,256]{2,1,0:T(8,128)(2,1)}, u32[]{:S(2)}, u32[]{:S(2)}) collective-permute-start(bf16[8,128,256]{2,1,0:T(8,128)(2,1)S(1)} %copy-done), channel_id=1, source_target_pairs={{16,32},{32,16},{48,64},{64,48},{80,96},{96,80},{112,128},{128,112... | collective-permute-start | bytes 1572872 | tf_op jit(solution)/shard_map/ppermute | solution.py:24
  21.5 0.1 collective-permute-start.1
  21.6 0.0 collective-permute-done.4.rows_b_ref
  21.6 0.7 %pad_maximum_fusion.1 = bf16[4,128,256]{2,1,0:T(8,128)(2,1)} fusion(bf16[2,128,256]{2,1,0:T(8,128)(2,1)S(1)} %get-tuple-element.10, bf16[2,128,256]{2,1,0:T(8,128)(2,1)S(1)} %get-tuple-element.9), kind=kLoop, calls=%fused_computation.1 | loop fusion | flops 131072 | bytes 524288 | tf_op jit(solution)/shard_map/concatenate | solution.py:197
  22.4 4.1 %collective-permute-start.5 = (bf16[4,128,256]{2,1,0:T(8,128)(2,1)}, bf16[4,128,256]{2,1,0:T(8,128)(2,1)S(1)}, u32[]{:S(2)}, u32[]{:S(2)}) collective-permute-start(bf16[4,128,256]{2,1,0:T(8,128)(2,1)} %pad_maximum_fusion.1), channel_id=1, source_target_pairs={{16,32},{32,16},{48,64},{64,48},{80,96},{96,80},{112,128},{128,112... | collective-permute-start | bytes 786440 | tf_op jit(solution)/shard_map/ppermute | solution.py:24
  28.0 0.1 stack.43.scalar_ref
  28.1 0.1 pad_add_fusion.place_ref
  28.1 2.5 %collective-permute-done.2.remote_ref = bf16[8,128,256]{2,1,0:T(8,128)(2,1)} collective-permute-done((bf16[8,128,256]{2,1,0:T(8,128)(2,1)S(1)}, bf16[8,128,256]{2,1,0:T(8,128)(2,1)}, u32[]{:S(2)}, u32[]{:S(2)}) %collective-permute-start.2) | collective-permute-done | bytes 524320 | tf_op jit(solution)/shard_map/ppermute | solution.py:24
  30.7 0.0 collective-permute-done.1.partner_ref
  30.7 2.7 %collective-permute-done.5.corner_ref = bf16[4,128,256]{2,1,0:T(8,128)(2,1)S(1)} collective-permute-done((bf16[4,128,256]{2,1,0:T(8,128)(2,1)}, bf16[4,128,256]{2,1,0:T(8,128)(2,1)S(1)}, u32[]{:S(2)}, u32[]{:S(2)}) %collective-permute-start.5) | collective-permute-done | bytes 262176 | tf_op jit(solution)/shard_map/ppermute | solution.py:24
  33.4 0.0 copy-done.3
  33.4 0.0 copy-done.2
  33.4 0.0 copy-done.1
  33.4 0.0 copy-start.4
  33.4 1.0 %copy-done.4 = bf16[2,64,8,256]{3,2,1,0:T(8,128)(2,1)S(1)} copy-done((bf16[2,64,8,256]{3,2,1,0:T(8,128)(2,1)S(1)}, bf16[2,64,8,256]{3,2,1,0:T(8,128)(2,1)}, u32[]{:S(2)}) %copy-start.4) | copy-done | bytes 524312
  34.4 0.9 %copy-done.5 = bf16[3,3,96,96]{3,2,1,0:T(8,128)(2,1)S(1)} copy-done((bf16[3,3,96,96]{3,2,1,0:T(8,128)(2,1)S(1)}, bf16[3,3,96,96]{3,2,1,0:T(8,128)(2,1)}, u32[]{:S(2)}) %copy-start.5) | copy-done | bytes 165912
  35.4 0.7 %copy-done.6 = bf16[64,96]{1,0:T(8,128)(2,1)S(1)} copy-done((bf16[64,96]{1,0:T(8,128)(2,1)S(1)}, bf16[64,96]{1,0:T(8,128)(2,1)}, u32[]{:S(2)}) %copy-start.6) | copy-done | bytes 12312
  36.1 0.7 %copy-done.7 = s32[2,8,256]{2,1,0:T(8,128)S(1)} copy-done((s32[2,8,256]{2,1,0:T(8,128)S(1)}, s32[2,8,256]{2,1,0:T(8,128)}, u32[]{:S(2)}) %copy-start.7) | copy-done | bytes 16408
  36.8 10.6 %step.1 = f32[2,64,8,256]{3,2,1,0:T(8,128)} custom-call(s32[3]{0:T(128)S(1)} %pad_add_fusion.place_ref, f32[5]{0:T(128)S(1)} %stack.43.scalar_ref, bf16[8,128,256]{2,1,0:T(8,128)(2,1)S(1)} %copy-done, bf16[8,128,256]{2,1,0:T(8,128)(2,1)} %collective-permute-done.1.partner_ref, bf16[8,128,256]{2,1,0:T(8,128)(2,1)} %collective-permute-done.2.remote_ref, ...), custom_call_target="tpu_custom_call" | custom-call | tf_op jit(solution)/shard_map/step/pallas_call | solution.py:212
  (5 shorter events, 0.1 us)
Async XLA Ops:
  2.0 31.4 %copy-start.3 = (bf16[3,3,96,320]{3,2,1,0:T(8,128)(2,1)S(1)}, bf16[3,3,96,320]{3,2,1,0:T(8,128)(2,1)}, u32[]{:S(2)}) copy-start(bf16[3,3,96,320]{3,2,1,0:T(8,128)(2,1)} %first_ref.1) | copy-start | bytes 1658884
  3.0 15.0 %copy-start = (bf16[8,128,256]{2,1,0:T(8,128)(2,1)S(1)}, bf16[8,128,256]{2,1,0:T(8,128)(2,1)}, u32[]{:S(2)}) copy-start(bf16[8,128,256]{2,1,0:T(8,128)(2,1)} %rows_first.1.own_ref) | copy-start | bytes 1572868
  3.0 1.7 %collective-permute-start = (bf16[2,128,256]{2,1,0:T(8,128)(2,1)S(1)}, bf16[2,128,256]{2,1,0:T(8,128)(2,1)S(1)}, u32[]{:S(2)}, u32[]{:S(2)}) collective-permute-start(bf16[2,128,256]{2,1,0:T(8,128)(2,1)S(1)} %broadcast_select_fusion.4), channel_id=1, source_target_pairs={{0,16},{16,0},{32,48},{48,32},{64,80},{80,64},{96,112},{112,96},{1... | collective-permute-start | bytes 393224 | tf_op jit(solution)/shard_map/ppermute | solution.py:19
  5.8 27.6 %copy-start.2 = (f32[2,64,8,256]{3,2,1,0:T(8,128)S(1)}, f32[2,64,8,256]{3,2,1,0:T(8,128)}, u32[]{:S(2)}) copy-start(f32[2,64,8,256]{3,2,1,0:T(8,128)} %noise_v.1) | copy-start | bytes 3145732
  5.8 27.6 %copy-start.1 = (bf16[2,64,8,256]{3,2,1,0:T(8,128)(2,1)S(1)}, bf16[2,64,8,256]{3,2,1,0:T(8,128)(2,1)}, u32[]{:S(2)}) copy-start(bf16[2,64,8,256]{3,2,1,0:T(8,128)(2,1)} %states_v.1) | copy-start | bytes 1572868
  5.8 12.1 %collective-permute-start.3 = (bf16[2,256,256]{2,1,0:T(8,128)(2,1)S(1)}, bf16[2,256,256]{2,1,0:T(8,128)(2,1)S(1)}, u32[]{:S(2)}, u32[]{:S(2)}) collective-permute-start(bf16[2,256,256]{2,1,0:T(8,128)(2,1)S(1)} %pad_maximum_fusion), channel_id=1, source_target_pairs={{1,16},{2,17},{3,18},{4,19},{5,20},{6,21},{7,22},{8,23},{9,24},{10... | collective-permute-start | bytes 786440 | tf_op jit(solution)/shard_map/ppermute | solution.py:34
  18.0 3.6 %collective-permute-start.4 = (bf16[2,256,256]{2,1,0:T(8,128)(2,1)S(1)}, bf16[2,256,256]{2,1,0:T(8,128)(2,1)S(1)}, u32[]{:S(2)}, u32[]{:S(2)}) collective-permute-start(bf16[2,256,256]{2,1,0:T(8,128)(2,1)S(1)} %collective-permute-done.3.rows_a_ref), channel_id=1, source_target_pairs={{0,16},{16,0},{32,48},{48,32},{64,80},{80,64},{96,112},{112,96},{1... | collective-permute-start | bytes 786440 | tf_op jit(solution)/shard_map/ppermute | solution.py:19
  18.0 12.7 %collective-permute-start.2 = (bf16[8,128,256]{2,1,0:T(8,128)(2,1)S(1)}, bf16[8,128,256]{2,1,0:T(8,128)(2,1)}, u32[]{:S(2)}, u32[]{:S(2)}) collective-permute-start(bf16[8,128,256]{2,1,0:T(8,128)(2,1)S(1)} %copy-done), channel_id=1, source_target_pairs={{16,32},{32,16},{48,64},{64,48},{80,96},{96,80},{112,128},{128,112... | collective-permute-start | bytes 1572872 | tf_op jit(solution)/shard_map/ppermute | solution.py:24
  21.5 9.2 %collective-permute-start.1 = (bf16[8,128,256]{2,1,0:T(8,128)(2,1)S(1)}, bf16[8,128,256]{2,1,0:T(8,128)(2,1)}, u32[]{:S(2)}, u32[]{:S(2)}) collective-permute-start(bf16[8,128,256]{2,1,0:T(8,128)(2,1)S(1)} %copy-done), channel_id=1, source_target_pairs={{0,16},{16,0},{32,48},{48,32},{64,80},{80,64},{96,112},{112,96},{1... | collective-permute-start | bytes 1572872 | tf_op jit(solution)/shard_map/ppermute | solution.py:19
  22.4 11.0 %collective-permute-start.5 = (bf16[4,128,256]{2,1,0:T(8,128)(2,1)}, bf16[4,128,256]{2,1,0:T(8,128)(2,1)S(1)}, u32[]{:S(2)}, u32[]{:S(2)}) collective-permute-start(bf16[4,128,256]{2,1,0:T(8,128)(2,1)} %pad_maximum_fusion.1), channel_id=1, source_target_pairs={{16,32},{32,16},{48,64},{64,48},{80,96},{96,80},{112,128},{128,112... | collective-permute-start | bytes 786440 | tf_op jit(solution)/shard_map/ppermute | solution.py:24
  33.4 1.0 %copy-start.4 = (bf16[2,64,8,256]{3,2,1,0:T(8,128)(2,1)S(1)}, bf16[2,64,8,256]{3,2,1,0:T(8,128)(2,1)}, u32[]{:S(2)}) copy-start(bf16[2,64,8,256]{3,2,1,0:T(8,128)(2,1)} %observed_v.1) | copy-start | bytes 1572868
  34.4 0.9 %copy-start.5 = (bf16[3,3,96,96]{3,2,1,0:T(8,128)(2,1)S(1)}, bf16[3,3,96,96]{3,2,1,0:T(8,128)(2,1)}, u32[]{:S(2)}) copy-start(bf16[3,3,96,96]{3,2,1,0:T(8,128)(2,1)} %second_ref.1) | copy-start | bytes 497668
  35.4 0.7 %copy-start.6 = (bf16[64,96]{1,0:T(8,128)(2,1)S(1)}, bf16[64,96]{1,0:T(8,128)(2,1)}, u32[]{:S(2)}) copy-start(bf16[64,96]{1,0:T(8,128)(2,1)} %proj_ref.1) | copy-start | bytes 36868
  36.1 0.7 %copy-start.7 = (s32[2,8,256]{2,1,0:T(8,128)S(1)}, s32[2,8,256]{2,1,0:T(8,128)}, u32[]{:S(2)}) copy-start(s32[2,8,256]{2,1,0:T(8,128)} %mask_ref.1) | copy-start | bytes 49156

commit v2 on v0

v2 whole, which is shorter than its diff:
```python
import jax
import jax.numpy as jnp
from jax import lax
from jax.experimental import pallas as pl
from jax.experimental.pallas import tpu as pltpu
from jax.sharding import PartitionSpec as P

F32 = jnp.float32
BF16 = jnp.bfloat16
AXES = ("tm", "space")
WID = 256
ROWS = 8
CH = 64
HID = 96
TWO = 2 * CH
FOUR = 4 * CH


def core_swap(x, tm):
    return lax.ppermute(x, "tm", [(i, i ^ 1) for i in range(tm)])


def side_swap(x, tm):
    pairs = [(i, ((i + 1) ^ 1) - 1) for i in range(tm)]
    return lax.ppermute(x, "tm", [(i, j) for i, j in pairs if 0 <= j < tm])


def row_swap(x, tm, space):
    pairs = []
    for t in range(tm):
        step = -1 if t % 2 == 0 else 1
        for s in range(space):
            if 0 <= s + step < space:
                pairs.append((t * space + s, (t ^ 1) * space + s + step))
    return lax.ppermute(x, AXES, pairs)


def core_of():
    return lax.axis_index("tm") % 2


def silu(v):
    u = 0.5 * v
    return u + u * jnp.tanh(u)


def dot(a, b):
    return jnp.dot(a, b, preferred_element_type=F32)


def side_shifts(v):
    lane = lax.broadcasted_iota(jnp.int32, v.shape, v.ndim - 1)
    right = jnp.where(lane == 0, 0.0, pltpu.roll(v, 1, v.ndim - 1))
    left = jnp.where(lane == WID - 1, 0.0, pltpu.roll(v, WID - 1, v.ndim - 1))
    return right, left


def put_shifted(dst, start, block):
    size = block.shape[0]
    wide = block.astype(F32)
    right, left = side_shifts(wide)
    dst[0, pl.ds(start, size)] = right.astype(BF16)
    dst[1, pl.ds(start, size)] = block.astype(BF16)
    dst[2, pl.ds(start, size)] = left.astype(BF16)


def scale_in(now_ref):
    level = jnp.full((8, WID), now_ref[0], F32)
    return (1.0 / jnp.sqrt(1.0 + level * level))[:1]


def hidden_two(row_of, w_two_ref, t, r):
    window = [row_of(r + a)[b, t * HID : (t + 1) * HID] for a in (-1, 0, 1) for b in range(3)]
    return silu(dot(w_two_ref[...], jnp.concatenate(window, axis=0))).astype(BF16)


def put_estimate(est, r, val):
    est[0, pl.ds(r, CH, stride=ROWS), :] = val[:, :128]
    est[1, pl.ds(r, CH, stride=ROWS), :] = val[:, 128:]


def estimate_of(est):
    return jnp.concatenate([est[0], est[1]], axis=1).reshape(CH, ROWS, WID)


def rows_first(block):
    return jnp.swapaxes(block.reshape(TWO, ROWS, WID), 0, 1)


def own_kernel(states_ref, own_ref, block_v, sems):
    parts = sems.shape[0]
    size = TWO // parts
    copies = []
    for n in range(parts):
        t, c = divmod(n * size, CH)
        copies.append(pltpu.make_async_copy(states_ref.at[t, pl.ds(c, size)], block_v.at[n], sems.at[n]))
        copies[-1].start()
    for n in range(parts):
        copies[n].wait()
        own_ref[:, n * size : (n + 1) * size] = jnp.swapaxes(block_v[n], 0, 1)


def edge_kernel(own_ref, partner_ref, edge_ref):
    core = core_of()
    far = rows_first(partner_ref[...])
    edge_ref[:, pl.ds(pl.multiple_of(core * TWO, TWO), TWO)] = own_ref[pl.ds(core * (ROWS - 2), 2)]
    edge_ref[:, pl.ds(pl.multiple_of((1 - core) * TWO, TWO), TWO)] = jnp.where(core == 0, far[:2], far[-2:])


def corner_kernel(rows_a_ref, rows_b_ref, send_ref):
    core = core_of()
    mine = pl.ds(pl.multiple_of(core * TWO, TWO), TWO)
    send_ref[pl.ds(core * 2, 2)] = rows_a_ref[:, mine]
    send_ref[pl.ds((1 - core) * 2, 2)] = rows_b_ref[:, mine]


def rim_or(rim, mid, l):
    return rim.at[l if l < 2 else l - 4] if l in (0, 1, 6, 7) else mid.at[l - 2]


def three_rows(rows):
    return jnp.concatenate([r[...].reshape(-1, WID) for r in rows], axis=0)


def near_kernel(
    own_ref,
    partner_ref,
    first_ref,
    second_ref,
    w_near_ref,
    w_far_ref,
    w_two_ref,
    rim_ref,
    part_ref,
    rows_v,
    mid,
    first_v,
    second_v,
    sems,
):
    first_copy = pltpu.make_async_copy(first_ref, first_v, sems.at[0])
    second_copy = pltpu.make_async_copy(second_ref, second_v, sems.at[1])
    first_copy.start()
    second_copy.start()
    core = core_of()
    own_at = pl.multiple_of(core * TWO, TWO)
    partner_at = pl.multiple_of((1 - core) * TWO, TWO)
    rows_v[...] = rows_first(partner_ref[...])
    for l in range(ROWS):
        put_shifted(rim_or(rim_ref, mid, l), own_at, own_ref[l])
        put_shifted(rim_or(rim_ref, mid, l), partner_at, rows_v[l])

    first_copy.wait()
    second_copy.wait()
    blank = jnp.zeros((HID, CH), BF16)
    for n in range(9):
        a, b = divmod(n, 3)
        block = first_v[a, b]
        for t, six in enumerate(([block, blank], [blank, block])):
            six = jnp.concatenate(six, axis=1)
            near = jnp.where(core == 0, six[:, TWO:], six[:, :FOUR])
            far = jnp.where(core == 0, six[:, :TWO], six[:, FOUR:])
            w_near_ref[t * HID : (t + 1) * HID, n * FOUR : (n + 1) * FOUR] = near
            w_far_ref[t * HID : (t + 1) * HID, n * TWO : (n + 1) * TWO] = far
        w_two_ref[:, n * HID : (n + 1) * HID] = second_v[a, b]
    for r in range(1, ROWS - 1):
        window = three_rows([rim_or(rim_ref, mid, r + a) for a in (-1, 0, 1)])
        part_ref[r - 1] = dot(w_near_ref[...], window)


def far_kernel(now_ref, remote_ref, part_ref, w_far_ref, rim_ref, hid_ref, rows_v, mid):
    scale = scale_in(now_ref)
    rows_v[...] = rows_first(remote_ref[...])
    for l in range(ROWS):
        put_shifted(rim_or(rim_ref, mid, l), 0, rows_v[l])
    for r in range(1, ROWS - 1):
        window = three_rows([rim_or(rim_ref, mid, r + a) for a in (-1, 0, 1)])
        pre = part_ref[r - 1] + dot(w_far_ref[...], window)
        put_shifted(hid_ref.at[r - 1], 0, silu(pre * scale))


def middle_kernel(
    now_ref,
    next_ref,
    hid_ref,
    w_two_ref,
    proj_ref,
    mask_ref,
    states_ref,
    observed_ref,
    noise_ref,
    base_ref,
    h2s,
    est,
):
    for t in range(2):
        for r in range(2, 6):
            h2s[t, r - 2] = hidden_two(lambda i: hid_ref.at[i - 1], w_two_ref, t, r)

    level = jnp.full((ROWS, WID), now_ref[0], F32)
    later = jnp.full((ROWS, WID), next_ref[0], F32)
    drop = level * level - later * later
    obs_k = drop / (0.1 + level * level)
    noise_k = jnp.sqrt(drop)
    est_k = -drop / level
    est[...] = jnp.zeros(est.shape, F32)
    for t in range(2):
        for r in range(2, 6):
            put_estimate(est, r, dot(proj_ref[...], h2s[t, r - 2]))
        weight = mask_ref[t].astype(F32) * obs_k
        current = states_ref[t].astype(F32)
        seen = observed_ref[t].astype(F32)
        base_ref[t] = (
            current
            + est_k[None] * estimate_of(est)
            + weight[None] * (seen - current)
            + noise_k[None] * noise_ref[t]
        )


def rim_kernel(rows_a_ref, rows_b_ref, near_ref, far_ref, w_near_ref, w_far_ref, part_ref, halo):
    core = core_of()
    for l in range(2):
        put_shifted(halo.at[l], 0, jnp.where(core == 0, rows_a_ref[l], rows_b_ref[l]))
        put_shifted(halo.at[l + 2], 0, jnp.where(core == 0, rows_b_ref[l], rows_a_ref[l]))

    def near(*rows):
        return dot(w_near_ref[...], three_rows(rows))

    def far(a, l, n):
        columns = slice(3 * a * TWO, 3 * (a + n) * TWO)
        return dot(w_far_ref[:, columns], far_ref[l : l + n].reshape(3 * n * TWO, WID))

    part_ref[0] = near(halo.at[0], halo.at[1], near_ref.at[0]) + far(2, 0, 1)
    part_ref[1] = near(halo.at[1], near_ref.at[0], near_ref.at[1]) + far(1, 0, 2)
    part_ref[2] = near(near_ref.at[2], near_ref.at[3], halo.at[2]) + far(0, 2, 2)
    part_ref[3] = near(near_ref.at[3], halo.at[2], halo.at[3]) + far(0, 3, 1)


def outer_kernel(
    now_ref,
    next_ref,
    corner_ref,
    part_ref,
    w_far_ref,
    w_two_ref,
    proj_ref,
    hid_ref,
    base_ref,
    out_ref,
    far,
    hrim,
    h2s,
    est,
    out_v,
    sems,
):
    for l in range(4):
        put_shifted(far.at[l], 0, corner_ref[l])
    scale = scale_in(now_ref)
    up = lax.axis_index("space") > 0
    down = lax.axis_index("space") < lax.axis_size("space") - 1

    def far_one(a, l):
        return dot(w_far_ref[:, 3 * a * TWO : 3 * (a + 1) * TWO], far[l].reshape(3 * TWO, WID))

    def far_two(a, l):
        return dot(w_far_ref[:, 3 * a * TWO : 3 * (a + 2) * TWO], far[l : l + 2].reshape(6 * TWO, WID))

    pre = [
        part_ref[0] + far_two(0, 0),
        part_ref[1] + far_one(0, 1),
        part_ref[2] + far_one(2, 2),
        part_ref[3] + far_two(1, 2),
    ]
    hid = [silu(p * scale) for p in pre]
    hid[0] = jnp.where(up, hid[0], 0.0)
    hid[3] = jnp.where(down, hid[3], 0.0)
    for l in range(4):
        put_shifted(hrim.at[l], 0, hid[l])

    def row(r):
        return hid_ref.at[r - 1] if 0 < r < ROWS - 1 else hrim.at[r + 1 if r < 1 else r - 5]

    edge = (0, 1, 6, 7)
    level = jnp.full((ROWS, WID), now_ref[0], F32)
    later = jnp.full((ROWS, WID), next_ref[0], F32)
    est_k = -(level * level - later * later) / level
    est[...] = jnp.zeros(est.shape, F32)
    for t in range(2):
        for n, r in enumerate(edge):
            h2s[t, n] = hidden_two(row, w_two_ref, t, r)
        for n, r in enumerate(edge):
            put_estimate(est.at[t], r, dot(proj_ref[...], h2s[t, n]))
        out_v[t] = base_ref[t] + est_k[None] * estimate_of(est.at[t])
        pltpu.make_async_copy(out_v.at[t], out_ref.at[t], sems.at[t]).start()
    for t in range(2):
        pltpu.make_async_copy(out_v.at[t], out_ref.at[t], sems.at[t]).wait()


VMEM = pl.BlockSpec(memory_space=pltpu.VMEM)
SMEM = pl.BlockSpec(memory_space=pltpu.SMEM)
ANY = pl.BlockSpec(memory_space=pl.ANY)
HBM = pl.BlockSpec(memory_space=pltpu.HBM)


def in_hbm(x):
    return pltpu.with_memory_space_constraint(x, pltpu.HBM)


def call(kernel, outs, ins, scratch=(), mib=4, flops=0, scalars=0, hbm=0, out_specs=None):
    shapes = [jax.ShapeDtypeStruct(s, d) for s, d in outs]
    return pl.pallas_call(
        kernel,
        out_shape=shapes,
        in_specs=[SMEM] * scalars + [VMEM] * (len(ins) - scalars - hbm) + [HBM] * hbm,
        out_specs=out_specs or [VMEM] * len(shapes),
        scratch_shapes=scratch,
        compiler_params=pltpu.CompilerParams(vmem_limit_bytes=mib * 2**20),
        cost_estimate=pl.CostEstimate(flops=flops, bytes_accessed=2**20, transcendentals=0),
        name=kernel.__name__,
    )(*ins)


def body(
    states,
    observed,
    station_mask,
    noise,
    sigma_now,
    sigma_next,
    first_kernel,
    second_kernel,
    out_weight,
):
    tm, space = lax.axis_size("tm"), lax.axis_size("space")
    partner = core_swap(states, tm)
    (own,) = call(
        own_kernel,
        [((ROWS, TWO, WID), BF16)],
        [in_hbm(states)],
        [pltpu.VMEM((4, TWO // 4, ROWS, WID), BF16), pltpu.SemaphoreType.DMA((4,))],
        hbm=1,
    )
    (edge,) = call(edge_kernel, [((2, FOUR, WID), BF16)], [own, partner])
    rows_a = row_swap(edge, tm, space)
    remote = side_swap(states, tm)
    w_near, w_far, w_two, near_rim, part = call(
        near_kernel,
        [
            ((2 * HID, 9 * FOUR), BF16),
            ((2 * HID, 9 * TWO), BF16),
            ((HID, 9 * HID), BF16),
            ((4, 3, FOUR, WID), BF16),
            ((6, 2 * HID, WID), F32),
        ],
        [own, partner, in_hbm(first_kernel), in_hbm(second_kernel)],
        [
            pltpu.VMEM((ROWS, TWO, WID), BF16),
            pltpu.VMEM((4, 3, FOUR, WID), BF16),
            pltpu.VMEM(first_kernel.shape, BF16),
            pltpu.VMEM(second_kernel.shape, BF16),
            pltpu.SemaphoreType.DMA((2,)),
        ],
        mib=16,
        flops=2 * 10**9,
        hbm=2,
    )
    far_rim, hid = call(
        far_kernel,
        [((4, 3, TWO, WID), BF16), ((6, 3, 2 * HID, WID), BF16)],
        [sigma_now, remote, part, w_far],
        [pltpu.VMEM((ROWS, TWO, WID), BF16), pltpu.VMEM((4, 3, TWO, WID), BF16)],
        mib=8,
        flops=10**9,
        scalars=1,
    )
    rows_a, hid, far_rim = lax.optimization_barrier((rows_a, hid, far_rim))
    rows_b = core_swap(rows_a, tm)
    (send,) = call(corner_kernel, [((4, TWO, WID), BF16)], [rows_a, rows_b])
    corner = side_swap(send, tm)
    (part,) = call(
        rim_kernel,
        [((4, 2 * HID, WID), F32)],
        [rows_a, rows_b, near_rim, far_rim, w_near, w_far],
        [pltpu.VMEM((4, 3, FOUR, WID), BF16)],
        mib=12,
        flops=10**9,
    )
    (base,) = call(
        middle_kernel,
        [(noise.shape, F32)],
        [
            sigma_now,
            sigma_next,
            hid,
            w_two,
            out_weight,
            station_mask,
            states,
            observed,
            noise,
        ],
        [pltpu.VMEM((2, 4, HID, WID), BF16), pltpu.VMEM((2, CH * ROWS, 128), F32)],
        mib=8,
        flops=10**9,
        scalars=2,
    )
    (out,) = call(
        outer_kernel,
        [(noise.shape, F32)],
        [sigma_now, sigma_next, corner, part, w_far, w_two, out_weight, hid, base],
        [
            pltpu.VMEM((4, 3, TWO, WID), BF16),
            pltpu.VMEM((4, 3, 2 * HID, WID), BF16),
            pltpu.VMEM((2, 4, HID, WID), BF16),
            pltpu.VMEM((2, 2, CH * ROWS, 128), F32),
            pltpu.VMEM(noise.shape, F32),
            pltpu.SemaphoreType.DMA((2,)),
        ],
        mib=12,
        flops=10**9,
        scalars=2,
        out_specs=[ANY],
    )
    return out


def solution(mesh):
    in_specs = (
        P("tm", None, "space", None),
        P("tm", None, "space", None),
        P("tm", "space", None),
        P("tm", None, "space", None),
        P(),
        P(),
        P(),
        P(),
        P(),
    )
    out_specs = P("tm", None, "space", None)
    return jax.shard_map(body, mesh=mesh, in_specs=in_specs, out_specs=out_specs, check_vma=False)
```

time: 78 us -> 32.9 us (0.42)
  matrix products: 27.4 us -> 0 us
  starting transfers between devices: 22.5 us -> 9.35 us
  Pallas kernels: 0 us -> 11.1 us
  waiting for transfers between devices: 20.7 us -> 10.8 us
  local copies, waits for them, and re-layouts: 4.25 us -> 0.02 us
  other arithmetic: 1.1 us -> 0 us
    dot_general x18 -> x0, matrix products: 27.4 us -> none  [the longest x17 20.8 us: conv_block(): jnp.einsum('oc,sclw->solw', kernel[offa, offb], piece, preferred_element_...]
    ppermute x6 -> x5, starting transfers between devices: 22.5 us -> 9.35 us  [the longest x2 7.43 us: side_swap(): return lax.ppermute(x, 'tm', [(i, j) for i, j in pairs if 0 <= j < tm])]
    pallas_call x0 -> x8, Pallas kernels: none -> 11.1 us  [call(): pl.pallas_call(kernel, out_shape=shapes, in_specs=[SMEM] * scalars + [VME...]
    ppermute x6 -> x5, waiting for transfers between devices: 20.7 us -> 10.8 us  [the longest x2 7.53 us: side_swap(): return lax.ppermute(x, 'tm', [(i, j) for i, j in pairs if 0 <= j < tm])]
    unnamed x17 -> x10, local copies, waits for them, and re-layouts: 2.55 us -> 0.02 us
    add x1 -> x0, local copies, waits for them, and re-layouts: 1.58 us -> none  [body(): return current + drop * score + jnp.sqrt(drop) * noise]
    concatenate x2 -> x0, other arithmetic: 1.1 us -> none  [padded_2(): block = jnp.concatenate([low, block, high], axis=dim)]
  transfers between devices with their start and end apart: 6 -> 5, of which waited for: 5 -> 4; matrix products, arithmetic and copies ran while one was open for 2% -> 0% of each run, Pallas kernels for 0% -> 26%
where the time goes in v2:
time: 32.9 us; the launch traced here: 32.7 us
  Pallas kernels  11.1 us (34%)
  waiting for transfers between devices  10.8 us (33%)
  starting transfers between devices  9.35 us (28%)
  between operations  1.43 us (4%)
    pallas_call x8, Pallas kernels, call(): pl.pallas_call(kernel, out_shape=shapes, in_specs=[SMEM] * scalars + [VME...  11.1 us
    ppermute x2, waiting for transfers between devices, side_swap(): return lax.ppermute(x, 'tm', [(i, j) for i, j in pairs if 0 <= j < tm])  7.53 us
    ppermute x2, starting transfers between devices, side_swap(): return lax.ppermute(x, 'tm', [(i, j) for i, j in pairs if 0 <= j < tm])  7.43 us
    ppermute x1, starting transfers between devices, row_swap(): return lax.ppermute(x, AXES, pairs)  1.92 us
    ppermute x1, waiting for transfers between devices, row_swap(): return lax.ppermute(x, AXES, pairs)  1.76 us
    ppermute x2, waiting for transfers between devices, core_swap(): return lax.ppermute(x, 'tm', [(i, i ^ 1) for i in range(tm)])  1.54 us
  transfers between devices with their start and end apart: 5, of which 4 were waited for; matrix products, arithmetic and copies ran while one was open for 0% of the time, Pallas kernels for 26%

profile of v2, /device:TPU:120, one launch (start us, length us, event | category | flops | bytes accessed | tf_op | source)
XLA Modules:
  0.0 32.7 jit_solution(17608895637256024429)
XLA Ops:
  0.0 0.0 collective-permute-start
  0.0 4.9 %collective-permute-start.2 = (bf16[2,64,8,256]{3,2,1,0:T(8,128)(2,1)}, bf16[2,64,8,256]{3,2,1,0:T(8,128)(2,1)S(1)}, u32[]{:S(2)}, u32[]{:S(2)}) collective-permute-start(bf16[2,64,8,256]{3,2,1,0:T(8,128)(2,1)} %states_ref.3), channel_id=1, source_target_pairs={{16,32},{32,16},{48,64},{64,48},{80,96},{96,80},{112,128},{128,112... | collective-permute-start | bytes 1572872 | tf_op jit(solution)/shard_map/ppermute | solution.py:25
  5.0 1.2 %own_kernel.1.own_ref = bf16[8,128,256]{2,1,0:T(8,128)(2,1)S(1)} custom-call(bf16[2,64,8,256]{3,2,1,0:T(8,128)(2,1)} %states_ref.3), custom_call_target="tpu_custom_call" | custom-call | bytes 1048576 | tf_op jit(solution)/shard_map/own_kernel/pallas_call | solution.py:313
  6.8 0.0 collective-permute-done.partner_ref
  6.8 0.1 edge_kernel.1
  6.9 1.9 %collective-permute-start.1 = (bf16[2,256,256]{2,1,0:T(8,128)(2,1)S(1)}, bf16[2,256,256]{2,1,0:T(8,128)(2,1)S(1)}, u32[]{:S(2)}, u32[]{:S(2)}) collective-permute-start(bf16[2,256,256]{2,1,0:T(8,128)(2,1)S(1)} %edge_kernel.1), channel_id=1, source_target_pairs={{1,16},{2,17},{3,18},{4,19},{5,20},{6,21},{7,22},{8,23},{9,24},{10... | collective-permute-start | bytes 786440 | tf_op jit(solution)/shard_map/ppermute | solution.py:35
  8.8 3.4 %near_kernel.1 = (bf16[192,2304]{1,0:T(8,128)(2,1)S(1)}, bf16[192,1152]{1,0:T(8,128)(2,1)S(1)}, bf16[96,864]{1,0:T(8,128)(2,1)S(1)}, bf16[4,3,256,256]{3,2,1,0:T(8,128)(2,1)S(1)}, f32[6,192,256]{2,1,0:T(8,128)S(1)}) custom-call(bf16[8,128,256]{2,1,0:T(8,128)(2,1)S(1)} %own_kernel.1.own_ref, bf16[2,64,8,256]{3,2,1,0:T(8,128)(2,1)S(1)} %collective-permute-done.partner_ref, ...), custom_call_target="tpu_custom_call" | custom-call | flops 2000000000 | bytes 1048576 | tf_op jit(solution)/shard_map/near_kernel/pallas_call | solution.py:313
  12.3 3.5 %collective-permute-done.2.remote_ref = bf16[2,64,8,256]{3,2,1,0:T(8,128)(2,1)S(1)} collective-permute-done((bf16[2,64,8,256]{3,2,1,0:T(8,128)(2,1)}, bf16[2,64,8,256]{3,2,1,0:T(8,128)(2,1)S(1)}, u32[]{:S(2)}, u32[]{:S(2)}) %collective-permute-start.2) | collective-permute-done | bytes 524320 | tf_op jit(solution)/shard_map/ppermute | solution.py:25
  15.7 0.0 copy-start
  15.7 0.0 copy-start.1
  15.7 0.0 copy-start.2
  15.7 0.0 copy-start.3
  15.7 0.0 copy-start.4
  15.7 1.4 %far_kernel.1 = (bf16[4,3,128,256]{3,2,1,0:T(8,128)(2,1)S(1)}, bf16[6,3,192,256]{3,2,1,0:T(8,128)(2,1)S(1)}) custom-call(f32[1]{0:T(128)S(6)} %copy.10.now_ref, bf16[2,64,8,256]{3,2,1,0:T(8,128)(2,1)S(1)} %collective-permute-done.2.remote_ref, f32[6,192,256]{2,1,0:T(8,128)S(1)} %get-tuple-element.15.part_ref, bf16[192,1152]{1,0:T(8,128)(2,1)S(1)} %get-tuple-element.16.w_far_ref), custom_call_target="tpu_custom_call" | custom-call | flops 1000000000 | bytes 1048576 | tf_op jit(solution)/shard_map/far_kernel/pallas_call | solution.py:313
  17.1 1.8 %collective-permute-done.1.rows_a_ref = bf16[2,256,256]{2,1,0:T(8,128)(2,1)S(1)} collective-permute-done((bf16[2,256,256]{2,1,0:T(8,128)(2,1)S(1)}, bf16[2,256,256]{2,1,0:T(8,128)(2,1)S(1)}, u32[]{:S(2)}, u32[]{:S(2)}) %collective-permute-start.1) | collective-permute-done | bytes 262176 | tf_op jit(solution)/shard_map/ppermute | solution.py:35
  18.9 0.0 collective-permute-start.3
  18.9 1.5 %collective-permute-done.3.rows_b_ref = bf16[2,256,256]{2,1,0:T(8,128)(2,1)S(1)} collective-permute-done((bf16[2,256,256]{2,1,0:T(8,128)(2,1)S(1)}, bf16[2,256,256]{2,1,0:T(8,128)(2,1)S(1)}, u32[]{:S(2)}, u32[]{:S(2)}) %collective-permute-start.3) | collective-permute-done | bytes 262176 | tf_op jit(solution)/shard_map/ppermute | solution.py:20
  20.5 2.5 %collective-permute-start.4 = (bf16[4,128,256]{2,1,0:T(8,128)(2,1)S(1)}, bf16[4,128,256]{2,1,0:T(8,128)(2,1)S(1)}, u32[]{:S(2)}, u32[]{:S(2)}) collective-permute-start(bf16[4,128,256]{2,1,0:T(8,128)(2,1)S(1)} %corner_kernel.1), channel_id=1, source_target_pairs={{16,32},{32,16},{48,64},{64,48},{80,96},{96,80},{112,128},{128,112... | collective-permute-start | bytes 786440 | tf_op jit(solution)/shard_map/ppermute | solution.py:25
  23.6 0.0 copy-done
  23.6 0.0 copy-done.1
  23.6 0.0 copy-done.2
  23.6 0.0 copy-done.3
  23.6 0.0 copy-done.4
  23.6 1.2 %middle_kernel.1.base_ref = f32[2,64,8,256]{3,2,1,0:T(8,128)S(1)} custom-call(f32[1]{0:T(128)S(6)} %copy.10.now_ref, f32[1]{0:T(128)S(6)} %copy.11.next_ref, bf16[6,3,192,256]{3,2,1,0:T(8,128)(2,1)S(1)} %get-tuple-element.24.hid_ref, bf16[96,864]{1,0:T(8,128)(2,1)S(1)} %get-tuple-element.23.w_two_ref, bf16[64,96]{1,0:T(8,128)(2,1)S(1)} %copy-done.3, ...), custom_call_target="tpu_custom_call" | custom-call | flops 1000000000 | bytes 1048576 | tf_op jit(solution)/shard_map/middle_kernel/pallas_call | solution.py:313
  24.8 1.4 %rim_kernel.1.part_ref = f32[4,192,256]{2,1,0:T(8,128)S(1)} custom-call(bf16[2,256,256]{2,1,0:T(8,128)(2,1)S(1)} %collective-permute-done.1.rows_a_ref, bf16[2,256,256]{2,1,0:T(8,128)(2,1)S(1)} %collective-permute-done.3.rows_b_ref, bf16[4,3,256,256]{3,2,1,0:T(8,128)(2,1)S(1)} %get-tuple-element.20.near_ref, ...), custom_call_target="tpu_custom_call" | custom-call | flops 1000000000 | bytes 1048576 | tf_op jit(solution)/shard_map/rim_kernel/pallas_call | solution.py:313
  26.2 4.1 %collective-permute-done.4.corner_ref = bf16[4,128,256]{2,1,0:T(8,128)(2,1)S(1)} collective-permute-done((bf16[4,128,256]{2,1,0:T(8,128)(2,1)S(1)}, bf16[4,128,256]{2,1,0:T(8,128)(2,1)S(1)}, u32[]{:S(2)}, u32[]{:S(2)}) %collective-permute-start.4) | collective-permute-done | bytes 262176 | tf_op jit(solution)/shard_map/ppermute | solution.py:25
  30.3 2.5 %outer_kernel.1 = f32[2,64,8,256]{3,2,1,0:T(8,128)} custom-call(f32[1]{0:T(128)S(6)} %copy.10.now_ref, f32[1]{0:T(128)S(6)} %copy.11.next_ref, bf16[4,128,256]{2,1,0:T(8,128)(2,1)S(1)} %collective-permute-done.4.corner_ref, f32[4,192,256]{2,1,0:T(8,128)S(1)} %rim_kernel.1.part_ref, bf16[192,1152]{1,0:T(8,128)(2,1)S(1)} %get-tuple-element.16.w_far_ref, ...), custom_call_target="tpu_custom_call" | custom-call | flops 1000000000 | bytes 1048576 | tf_op jit(solution)/shard_map/outer_kernel/pallas_call | solution.py:313
  (1 shorter events, 0.0 us)
Async XLA Ops:
  0.0 6.8 %collective-permute-start = (bf16[2,64,8,256]{3,2,1,0:T(8,128)(2,1)}, bf16[2,64,8,256]{3,2,1,0:T(8,128)(2,1)S(1)}, u32[]{:S(2)}, u32[]{:S(2)}) collective-permute-start(bf16[2,64,8,256]{3,2,1,0:T(8,128)(2,1)} %states_ref.3), channel_id=1, source_target_pairs={{0,16},{16,0},{32,48},{48,32},{64,80},{80,64},{96,112},{112,96},{1... | collective-permute-start | bytes 1572872 | tf_op jit(solution)/shard_map/ppermute | solution.py:20
  0.0 15.7 %collective-permute-start.2 = (bf16[2,64,8,256]{3,2,1,0:T(8,128)(2,1)}, bf16[2,64,8,256]{3,2,1,0:T(8,128)(2,1)S(1)}, u32[]{:S(2)}, u32[]{:S(2)}) collective-permute-start(bf16[2,64,8,256]{3,2,1,0:T(8,128)(2,1)} %states_ref.3), channel_id=1, source_target_pairs={{16,32},{32,16},{48,64},{64,48},{80,96},{96,80},{112,128},{128,112... | collective-permute-start | bytes 1572872 | tf_op jit(solution)/shard_map/ppermute | solution.py:25
  6.9 12.0 %collective-permute-start.1 = (bf16[2,256,256]{2,1,0:T(8,128)(2,1)S(1)}, bf16[2,256,256]{2,1,0:T(8,128)(2,1)S(1)}, u32[]{:S(2)}, u32[]{:S(2)}) collective-permute-start(bf16[2,256,256]{2,1,0:T(8,128)(2,1)S(1)} %edge_kernel.1), channel_id=1, source_target_pairs={{1,16},{2,17},{3,18},{4,19},{5,20},{6,21},{7,22},{8,23},{9,24},{10... | collective-permute-start | bytes 786440 | tf_op jit(solution)/shard_map/ppermute | solution.py:35
  15.7 7.9 %copy-start = (bf16[2,64,8,256]{3,2,1,0:T(8,128)(2,1)S(1)}, bf16[2,64,8,256]{3,2,1,0:T(8,128)(2,1)}, u32[]{:S(2)}) copy-start(bf16[2,64,8,256]{3,2,1,0:T(8,128)(2,1)} %states_ref.3) | copy-start | bytes 1572868
  15.7 7.9 %copy-start.1 = (f32[2,64,8,256]{3,2,1,0:T(8,128)S(1)}, f32[2,64,8,256]{3,2,1,0:T(8,128)}, u32[]{:S(2)}) copy-start(f32[2,64,8,256]{3,2,1,0:T(8,128)} %noise_ref.1) | copy-start | bytes 3145732
  15.7 7.9 %copy-start.2 = (bf16[2,64,8,256]{3,2,1,0:T(8,128)(2,1)S(1)}, bf16[2,64,8,256]{3,2,1,0:T(8,128)(2,1)}, u32[]{:S(2)}) copy-start(bf16[2,64,8,256]{3,2,1,0:T(8,128)(2,1)} %observed_ref.1) | copy-start | bytes 1572868
  15.7 7.9 %copy-start.3 = (bf16[64,96]{1,0:T(8,128)(2,1)S(1)}, bf16[64,96]{1,0:T(8,128)(2,1)}, u32[]{:S(2)}) copy-start(bf16[64,96]{1,0:T(8,128)(2,1)} %proj_ref.3) | copy-start | bytes 36868
  15.7 7.9 %copy-start.4 = (s32[2,8,256]{2,1,0:T(8,128)S(1)}, s32[2,8,256]{2,1,0:T(8,128)}, u32[]{:S(2)}) copy-start(s32[2,8,256]{2,1,0:T(8,128)} %mask_ref.1) | copy-start | bytes 49156
  18.9 1.5 %collective-permute-start.3 = (bf16[2,256,256]{2,1,0:T(8,128)(2,1)S(1)}, bf16[2,256,256]{2,1,0:T(8,128)(2,1)S(1)}, u32[]{:S(2)}, u32[]{:S(2)}) collective-permute-start(bf16[2,256,256]{2,1,0:T(8,128)(2,1)S(1)} %collective-permute-done.1.rows_a_ref), channel_id=1, source_target_pairs={{0,16},{16,0},{32,48},{48,32},{64,80},{80,64},{96,112},{112,96},{1... | collective-permute-start | bytes 786440 | tf_op jit(solution)/shard_map/ppermute | solution.py:20
  20.5 9.8 %collective-permute-start.4 = (bf16[4,128,256]{2,1,0:T(8,128)(2,1)S(1)}, bf16[4,128,256]{2,1,0:T(8,128)(2,1)S(1)}, u32[]{:S(2)}, u32[]{:S(2)}) collective-permute-start(bf16[4,128,256]{2,1,0:T(8,128)(2,1)S(1)} %corner_kernel.1), channel_id=1, source_target_pairs={{16,32},{32,16},{48,64},{64,48},{80,96},{96,80},{112,128},{128,112... | collective-permute-start | bytes 786440 | tf_op jit(solution)/shard_map/ppermute | solution.py:25

commit v3 on v0

v3 whole, which is shorter than its diff:
```python
import jax
import jax.numpy as jnp
from jax import lax
from jax.experimental import pallas as pl
from jax.experimental.pallas import tpu as pltpu
from jax.sharding import PartitionSpec as P

F32 = jnp.float32
BF16 = jnp.bfloat16
AXES = ("tm", "space")
WID = 256
ROWS = 8
CH = 64
HID = 96
TWO = 2 * CH
FOUR = 4 * CH


def core_swap(x, tm):
    return lax.ppermute(x, "tm", [(i, i ^ 1) for i in range(tm)])


def side_swap(x, tm):
    return lax.ppermute(x, "tm", [(i, (((i + 1) ^ 1) - 1) % tm) for i in range(tm)])


def most_swap(x, tm):
    pairs = [(i, ((i + 1) ^ 1) - 1) for i in range(tm)]
    return lax.ppermute(x, "tm", [(i, j) for i, j in pairs if 0 <= j < tm and i + j != tm - 1])


def middle_swap(x, tm):
    low = tm // 2 - 1
    return lax.ppermute(x, "tm", [(low, low + 1), (low + 1, low)])


def row_swap(x, tm, space):
    pairs = []
    for t in range(tm):
        step = -1 if t % 2 == 0 else 1
        for s in range(space):
            inside = 0 <= s + step < space
            pairs.append((t * space + s, (t ^ 1) * space + s + step if inside else (t ^ 2) * space + s))
    return lax.ppermute(x, AXES, pairs)


def core_of():
    return lax.axis_index("tm") % 2


def silu(v):
    u = 0.5 * v
    return u + u * jnp.tanh(u)


def dot(a, b):
    return jnp.dot(a, b, preferred_element_type=F32)


def rows_first(block):
    return jnp.swapaxes(block.reshape(TWO, ROWS, WID), 0, 1)


def side_shifts(v):
    lane = lax.broadcasted_iota(jnp.int32, v.shape, v.ndim - 1)
    zero = jnp.zeros((), v.dtype)
    right = jnp.where(lane == 0, zero, pltpu.roll(v, 1, v.ndim - 1))
    left = jnp.where(lane == WID - 1, zero, pltpu.roll(v, WID - 1, v.ndim - 1))
    return right, left


def put_sides(dst, start, block):
    right, left = side_shifts(block)
    dst[0, pl.ds(start, block.shape[0])] = right
    dst[1, pl.ds(start, block.shape[0])] = left


def stacked(sides, *centre):
    return jnp.concatenate([sides[0], *centre, sides[1]], axis=0)


def put_hidden(dst, hid):
    right, left = side_shifts(hid)
    dst[0] = right.astype(BF16)
    dst[1] = hid.astype(BF16)
    dst[2] = left.astype(BF16)


def two_rows(row_of, w_two_ref, t, r):
    window = [row_of(i)[b, t * HID : (t + 1) * HID] for i in range(r - 1, r + 3) for b in range(3)]
    return silu(dot(w_two_ref[...], jnp.concatenate(window, axis=0))).astype(BF16)


def put_estimates(est, r, val):
    for n in range(2):
        est[0, pl.ds(r + n, CH, stride=ROWS), :] = val[n * CH : (n + 1) * CH, :128]
        est[1, pl.ds(r + n, CH, stride=ROWS), :] = val[n * CH : (n + 1) * CH, 128:]


def prepare_kernel(
    states_ref,
    first_ref,
    second_ref,
    proj_ref,
    own_ref,
    w_near_ref,
    w_far_ref,
    w_two_ref,
    w_proj_ref,
    block_v,
    first_v,
    second_v,
    proj_v,
    sems,
):
    parts = block_v.shape[0]
    size = TWO // parts
    copies = []
    for n in range(parts):
        t, c = divmod(n * size, CH)
        copies.append(pltpu.make_async_copy(states_ref.at[t, pl.ds(c, size)], block_v.at[n], sems.at[n]))
    copies += [
        pltpu.make_async_copy(first_ref, first_v, sems.at[parts]),
        pltpu.make_async_copy(second_ref, second_v, sems.at[parts + 1]),
        pltpu.make_async_copy(proj_ref, proj_v, sems.at[parts + 2]),
    ]
    for copy in copies:
        copy.start()
    core = core_of()
    for n in range(parts):
        copies[n].wait()
        own_ref[:, n * size : (n + 1) * size] = jnp.swapaxes(block_v[n], 0, 1)
    for copy in copies[parts:]:
        copy.wait()
    blank = jnp.zeros((HID, CH), BF16)
    for n in range(9):
        block = first_v[n // 3, n % 3]
        for t, six in enumerate(([block, blank], [blank, block])):
            six = jnp.concatenate(six, axis=1)
            first, last = six[:, :TWO], six[:, FOUR:]
            rows = slice(t * HID, (t + 1) * HID)
            w_near_ref[rows, n * FOUR : n * FOUR + TWO] = six[:, TWO:FOUR]
            w_near_ref[rows, n * FOUR + TWO : (n + 1) * FOUR] = jnp.where(core == 0, last, first)
            w_far_ref[rows, n * TWO : (n + 1) * TWO] = jnp.where(core == 0, first, last)
    blank = jnp.zeros((HID, 3 * HID), BF16)
    w_two_ref[:HID, 9 * HID :] = blank
    w_two_ref[HID:, : 3 * HID] = blank
    for n in range(9):
        block = second_v[n // 3, n % 3]
        w_two_ref[:HID, n * HID : (n + 1) * HID] = block
        w_two_ref[HID:, (n + 3) * HID : (n + 4) * HID] = block
    blank = jnp.zeros((CH, HID), BF16)
    w_proj_ref[:CH] = jnp.concatenate([proj_v[...], blank], axis=1)
    w_proj_ref[CH:] = jnp.concatenate([blank, proj_v[...]], axis=1)


def edge_kernel(own_ref, partner_ref, edge_ref):
    core = core_of()
    other = rows_first(partner_ref[...])
    last = jnp.where(core == 0, 0, lax.axis_size("space") - 1)
    inside = lax.axis_index("space") != last
    zero = jnp.zeros((), BF16)
    mine = jnp.where(inside, own_ref[pl.ds(core * (ROWS - 2), 2)], zero)
    other = jnp.where(inside, jnp.where(core == 0, other[:2], other[-2:]), zero)
    edge_ref[:, pl.ds(pl.multiple_of(core * TWO, TWO), TWO)] = mine
    edge_ref[:, pl.ds(pl.multiple_of((1 - core) * TWO, TWO), TWO)] = other


def at_end():
    at = lax.axis_index("tm")
    return (at == 0) | (at == lax.axis_size("tm") - 1)


def corner_kernel(rows_a_ref, rows_b_ref, send_ref):
    core = core_of()
    mine = pl.ds(pl.multiple_of(core * TWO, TWO), TWO)
    zero = jnp.zeros((), BF16)
    send_ref[pl.ds(core * 2, 2)] = jnp.where(at_end(), zero, rows_a_ref[:, mine])
    send_ref[pl.ds((1 - core) * 2, 2)] = jnp.where(at_end(), zero, rows_b_ref[:, mine])


def rim_or(rim, mid, l):
    return rim.at[l if l < 2 else l - 4] if l in (0, 1, 6, 7) else mid.at[l - 2]


def near_kernel(own_ref, partner_ref, w_near_ref, partner_rows_ref, rim_ref, part_ref, mid):
    partner_rows_ref[...] = rows_first(partner_ref[...])

    def shift_row(l):
        put_sides(rim_or(rim_ref, mid, l), 0, own_ref[l])
        put_sides(rim_or(rim_ref, mid, l), TWO, partner_rows_ref[l])

    def row(l):
        return stacked(rim_or(rim_ref, mid, l), own_ref[l], partner_rows_ref[l])

    for l in range(3):
        shift_row(l)
    for r in range(1, ROWS - 1):
        if r + 2 < ROWS:
            shift_row(r + 2)
        window = jnp.concatenate([row(r + a) for a in (-1, 0, 1)], axis=0)
        part_ref[r - 1] = dot(w_near_ref[...], window)


def base_kernel(
    now_ref, next_ref, mask_ref, states_ref, observed_ref, noise_ref, base_ref, coef_ref
):
    level = jnp.full((ROWS, WID), now_ref[0], F32)
    later = jnp.full((ROWS, WID), next_ref[0], F32)
    drop = level * level - later * later
    coef_ref[0] = 1.0 / jnp.sqrt(1.0 + level * level)
    coef_ref[1] = -drop / level
    obs_k = drop / (0.1 + level * level)
    noise_k = jnp.sqrt(drop)
    for t in range(2):
        weight = mask_ref[t].astype(F32) * obs_k
        current = states_ref[t].astype(F32)
        seen = observed_ref[t].astype(F32)
        base_ref[t] = current + weight[None] * (seen - current) + noise_k[None] * noise_ref[t]


def rim_kernel(
    rows_a_ref, rows_b_ref, own_ref, partner_rows_ref, near_ref, w_near_ref, part_ref, halo, sides
):
    core = core_of()
    own_at = pl.multiple_of(core * TWO, TWO)
    partner_at = pl.multiple_of((1 - core) * TWO, TWO)
    for l in range(2):
        for n, at in ((0, own_at), (1, partner_at)):
            a, b = rows_a_ref[l, pl.ds(at, TWO)], rows_b_ref[l, pl.ds(at, TWO)]
            halo[l, n * TWO : (n + 1) * TWO] = jnp.where(core == 0, a, b)
            halo[l + 2, n * TWO : (n + 1) * TWO] = jnp.where(core == 0, b, a)

    def tile(l):
        return stacked(near_ref.at[l if l < 2 else l - 4], own_ref[l], partner_rows_ref[l])

    def outside(l):
        put_sides(sides.at[l], 0, halo[l])
        return stacked(sides.at[l], halo[l])

    def near(*rows):
        return dot(w_near_ref[...], jnp.concatenate(rows, axis=0))

    above, below = [outside(0), outside(1)], [outside(2), outside(3)]
    part_ref[0] = near(above[0], above[1], tile(0))
    part_ref[1] = near(above[1], tile(0), tile(1))
    part_ref[2] = near(tile(6), tile(7), below[0])
    part_ref[3] = near(tile(7), below[0], below[1])


def far_kernel(
    most_ref, middle_ref, part_ref, rim_part_ref, w_far_ref, coef_ref, hid_ref, rim_out_ref, rows_v, sides
):
    scale = coef_ref[0][:1]
    at, size = lax.axis_index("tm"), lax.axis_size("tm")
    in_middle = (at == size // 2 - 1) | (at == size // 2)
    block = jnp.where(in_middle, middle_ref[...], most_ref[...])
    rows_v[...] = rows_first(jnp.where(at_end(), jnp.zeros((), BF16), block))

    def far(a, l, n):
        columns = slice(3 * a * TWO, 3 * (a + n) * TWO)
        rows = [stacked(sides.at[i], rows_v[i]) for i in range(l, l + n)]
        return dot(w_far_ref[:, columns], jnp.concatenate(rows, axis=0))

    for l in range(3):
        put_sides(sides.at[l], 0, rows_v[l])
    for r in range(1, ROWS - 1):
        if r + 2 < ROWS:
            put_sides(sides.at[r + 2], 0, rows_v[r + 2])
        pre = part_ref[r - 1] + far(0, r - 1, 3)
        put_hidden(hid_ref.at[r - 1], silu(pre * scale))
    rim_out_ref[0] = rim_part_ref[0] + far(2, 0, 1)
    rim_out_ref[1] = rim_part_ref[1] + far(1, 0, 2)
    rim_out_ref[2] = rim_part_ref[2] + far(0, ROWS - 2, 2)
    rim_out_ref[3] = rim_part_ref[3] + far(0, ROWS - 1, 1)


def middle_kernel(hid_ref, w_two_ref, proj_ref, est_ref, h2s):
    spots = [(t, r) for t in range(2) for r in (2, 4)]
    for n, (t, r) in enumerate(spots):
        h2s[n] = two_rows(lambda i: hid_ref.at[i - 1], w_two_ref, t, r)
    for n, (t, r) in enumerate(spots):
        put_estimates(est_ref.at[t], r, dot(proj_ref[...], h2s[n]))


def outer_kernel(
    corner_ref,
    part_ref,
    w_far_ref,
    w_two_ref,
    proj_ref,
    coef_ref,
    hid_ref,
    base_ref,
    est_in_ref,
    out_ref,
    sides,
    hrim,
    h2s,
    est,
    out_v,
    sems,
):
    for l in range(4):
        put_sides(sides.at[l], 0, corner_ref[l])
    scale = coef_ref[0][:1]
    up = lax.axis_index("space") > 0
    down = lax.axis_index("space") < lax.axis_size("space") - 1

    def far(a, l, n):
        columns = slice(3 * a * TWO, 3 * (a + n) * TWO)
        rows = [stacked(sides.at[i], corner_ref[i]) for i in range(l, l + n)]
        return dot(w_far_ref[:, columns], jnp.concatenate(rows, axis=0))

    pre = [
        part_ref[0] + far(0, 0, 2),
        part_ref[1] + far(0, 1, 1),
        part_ref[2] + far(2, 2, 1),
        part_ref[3] + far(1, 2, 2),
    ]
    hid = [silu(p * scale) for p in pre]
    hid[0] = jnp.where(up, hid[0], 0.0)
    hid[3] = jnp.where(down, hid[3], 0.0)
    for l in range(4):
        put_hidden(hrim.at[l], hid[l])

    def row(r):
        return hid_ref.at[r - 1] if 0 < r < ROWS - 1 else hrim.at[r + 1 if r < 1 else r - 5]

    est[...] = est_in_ref[...]
    half = CH // 2
    copies = []
    for t in range(2):
        for n, r in enumerate((0, 6)):
            h2s[t, n] = two_rows(row, w_two_ref, t, r)
        for n, r in enumerate((0, 6)):
            put_estimates(est.at[t], r, dot(proj_ref[...], h2s[t, n]))
        for n in range(2):
            channels = slice(n * half, (n + 1) * half)
            rows = slice(n * half * ROWS, (n + 1) * half * ROWS)
            val = jnp.concatenate([est[t, 0, rows], est[t, 1, rows]], axis=1).reshape(half, ROWS, WID)
            out_v[t, channels] = base_ref[t, channels] + coef_ref[1][None] * val
            at = (t, pl.ds(n * half, half))
            copies.append(pltpu.make_async_copy(out_v.at[at], out_ref.at[at], sems.at[2 * t + n]))
            copies[-1].start()
    for copy in copies:
        copy.wait()


VMEM = pl.BlockSpec(memory_space=pltpu.VMEM)
SMEM = pl.BlockSpec(memory_space=pltpu.SMEM)
ANY = pl.BlockSpec(memory_space=pl.ANY)
HBM = pl.BlockSpec(memory_space=pltpu.HBM)


def in_hbm(x):
    return pltpu.with_memory_space_constraint(x, pltpu.HBM)


def call(kernel, outs, ins, scratch=(), mib=4, flops=0, scalars=0, hbm=0, out_specs=None):
    shapes = [jax.ShapeDtypeStruct(s, d) for s, d in outs]
    ins = list(ins[: len(ins) - hbm]) + [in_hbm(x) for x in ins[len(ins) - hbm :]]
    return pl.pallas_call(
        kernel,
        out_shape=shapes,
        in_specs=[SMEM] * scalars + [VMEM] * (len(ins) - scalars - hbm) + [HBM] * hbm,
        out_specs=out_specs or [VMEM] * len(shapes),
        scratch_shapes=scratch,
        compiler_params=pltpu.CompilerParams(vmem_limit_bytes=mib * 2**20),
        cost_estimate=pl.CostEstimate(flops=flops, bytes_accessed=2**20, transcendentals=0),
        name=kernel.__name__,
    )(*ins)


def body(
    states,
    observed,
    station_mask,
    noise,
    sigma_now,
    sigma_next,
    first_kernel,
    second_kernel,
    out_weight,
):
    tm, space = lax.axis_size("tm"), lax.axis_size("space")
    rows_shape = ((ROWS, TWO, WID), BF16)
    partner = core_swap(states, tm)
    own, w_near, w_far, w_two, w_proj = call(
        prepare_kernel,
        [
            rows_shape,
            ((2 * HID, 9 * FOUR), BF16),
            ((2 * HID, 9 * TWO), BF16),
            ((2 * HID, 12 * HID), BF16),
            ((2 * CH, 2 * HID), BF16),
        ],
        [states, first_kernel, second_kernel, out_weight],
        [
            pltpu.VMEM((4, TWO // 4, ROWS, WID), BF16),
            pltpu.VMEM(first_kernel.shape, BF16),
            pltpu.VMEM(second_kernel.shape, BF16),
            pltpu.VMEM(out_weight.shape, BF16),
            pltpu.SemaphoreType.DMA((7,)),
        ],
        mib=8,
        hbm=4,
    )
    (edge,) = call(edge_kernel, [((2, FOUR, WID), BF16)], [own, partner])
    edge, states_x = lax.optimization_barrier((edge, states))
    rows_a = row_swap(edge, tm, space)
    most = most_swap(states_x, tm)
    partner_rows, near_rim, part = call(
        near_kernel,
        [rows_shape, ((4, 2, FOUR, WID), BF16), ((6, 2 * HID, WID), F32)],
        [own, partner, w_near],
        [pltpu.VMEM((4, 2, FOUR, WID), BF16)],
        mib=16,
        flops=2 * 10**9,
    )
    states_late, part = lax.optimization_barrier((states, part))
    middle = middle_swap(states_late, tm)
    rows_a, part = lax.optimization_barrier((rows_a, part))
    rows_b = core_swap(rows_a, tm)
    (send,) = call(corner_kernel, [((4, TWO, WID), BF16)], [rows_a, rows_b])
    send, noise_late = lax.optimization_barrier((send, noise))
    base, coef = call(
        base_kernel,
        [(noise.shape, F32), ((2, ROWS, WID), F32)],
        [sigma_now, sigma_next, station_mask, states, observed, noise_late],
        flops=10**8,
        scalars=2,
    )
    corner = side_swap(send, tm)
    (rim_part,) = call(
        rim_kernel,
        [((4, 2 * HID, WID), F32)],
        [rows_a, rows_b, own, partner_rows, near_rim, w_near],
        [pltpu.VMEM((4, FOUR, WID), BF16), pltpu.VMEM((4, 2, FOUR, WID), BF16)],
        mib=12,
        flops=10**9,
    )
    hid, rim_part = call(
        far_kernel,
        [((6, 3, 2 * HID, WID), BF16), ((4, 2 * HID, WID), F32)],
        [most, middle, part, rim_part, w_far, coef],
        [pltpu.VMEM((ROWS, TWO, WID), BF16), pltpu.VMEM((ROWS, 2, TWO, WID), BF16)],
        mib=8,
        flops=10**9,
    )
    (est,) = call(
        middle_kernel,
        [((2, 2, CH * ROWS, 128), F32)],
        [hid, w_two, w_proj],
        [pltpu.VMEM((4, 2 * HID, WID), BF16)],
        mib=8,
        flops=10**9,
    )
    (out,) = call(
        outer_kernel,
        [(noise.shape, F32)],
        [corner, rim_part, w_far, w_two, w_proj, coef, hid, base, est],
        [
            pltpu.VMEM((4, 2, TWO, WID), BF16),
            pltpu.VMEM((4, 3, 2 * HID, WID), BF16),
            pltpu.VMEM((2, 2, 2 * HID, WID), BF16),
            pltpu.VMEM((2, 2, CH * ROWS, 128), F32),
            pltpu.VMEM(noise.shape, F32),
            pltpu.SemaphoreType.DMA((4,)),
        ],
        mib=12,
        flops=10**9,
        out_specs=[ANY],
    )
    return out


def solution(mesh):
    in_specs = (
        P("tm", None, "space", None),
        P("tm", None, "space", None),
        P("tm", "space", None),
        P("tm", None, "space", None),
        P(),
        P(),
        P(),
        P(),
        P(),
    )
    out_specs = P("tm", None, "space", None)
    return jax.shard_map(body, mesh=mesh, in_specs=in_specs, out_specs=out_specs, check_vma=False)
```

time: 78 us -> 26.2 us (0.34)
  the two profiles are of different devices: /device:TPU:120 before, /device:TPU:135 now
where the time goes in v3:
time: 26.2 us; the launch traced here: 26 us
  Pallas kernels  9.95 us (38%)
  starting transfers between devices  7.89 us (30%)
  waiting for transfers between devices  6.76 us (26%)
  between operations  1.42 us (5%)
    pallas_call x9, Pallas kernels, call(): pl.pallas_call(kernel, out_shape=shapes, in_specs=[SMEM] * scalars + [VME...  9.95 us
    ppermute x1, waiting for transfers between devices, middle_swap(): return lax.ppermute(x, 'tm', [(low, low + 1), (low + 1, low)])  3.39 us
    ppermute x1, starting transfers between devices, row_swap(): return lax.ppermute(x, AXES, pairs)  3.1 us
    ppermute x1, waiting for transfers between devices, row_swap(): return lax.ppermute(x, AXES, pairs)  2.73 us
    ppermute x1, starting transfers between devices, middle_swap(): return lax.ppermute(x, 'tm', [(low, low + 1), (low + 1, low)])  1.94 us
    ppermute x1, starting transfers between devices, side_swap(): lax.ppermute(x, 'tm', [(i, ((i + 1 ^ 1) - 1) % tm) for i in range(tm)])  1.49 us
    ppermute x1, starting transfers between devices, most_swap(): lax.ppermute(x, 'tm', [(i, j) for i, j in pairs if 0 <= j < tm and i + j...  0.68 us
    ppermute x2, starting transfers between devices, core_swap(): return lax.ppermute(x, 'tm', [(i, i ^ 1) for i in range(tm)])  0.68 us
  transfers between devices with their start and end apart: 6, of which 4 were waited for; matrix products, arithmetic and copies ran while one was open for 0% of the time, Pallas kernels for 29%

profile of v3, /device:TPU:135, one launch (start us, length us, event | category | flops | bytes accessed | tf_op | source)
XLA Modules:
  0.0 26.0 jit_solution(17259149212577617353)
XLA Ops:
  0.0 0.0 copy-start
  0.0 0.7 %collective-permute-start = (bf16[2,64,8,256]{3,2,1,0:T(8,128)(2,1)}, bf16[2,64,8,256]{3,2,1,0:T(8,128)(2,1)S(1)}, u32[]{:S(2)}, u32[]{:S(2)}) collective-permute-start(bf16[2,64,8,256]{3,2,1,0:T(8,128)(2,1)} %states_ref.3), channel_id=1, source_target_pairs={{0,16},{16,0},{32,48},{48,32},{64,80},{80,64},{96,112},{112,96},{1... | collective-permute-start | bytes 1572872 | tf_op jit(solution)/shard_map/ppermute | solution.py:20
  0.7 1.9 %prepare_kernel.1 = (bf16[8,128,256]{2,1,0:T(8,128)(2,1)S(1)}, bf16[192,2304]{1,0:T(8,128)(2,1)S(1)}, bf16[192,1152]{1,0:T(8,128)(2,1)S(1)}, bf16[192,1152]{1,0:T(8,128)(2,1)S(1)}, bf16[128,192]{1,0:T(8,128)(2,1)S(1)}) custom-call(bf16[2,64,8,256]{3,2,1,0:T(8,128)(2,1)} %states_ref.3, bf16[3,3,96,320]{3,2,1,0:T(8,128)(2,1)} %first_ref.1, ...), custom_call_target="tpu_custom_call" | custom-call | bytes 1048576 | tf_op jit(solution)/shard_map/prepare_kernel/pallas_call | solution.py:363
  2.6 0.0 collective-permute-done.partner_ref
  2.6 0.1 edge_kernel.1
  2.7 3.1 %collective-permute-start.1 = (bf16[2,256,256]{2,1,0:T(8,128)(2,1)S(1)}, bf16[2,256,256]{2,1,0:T(8,128)(2,1)S(1)}, u32[]{:S(2)}, u32[]{:S(2)}) collective-permute-start(bf16[2,256,256]{2,1,0:T(8,128)(2,1)S(1)} %edge_kernel.1), channel_id=1, source_target_pairs={{0,32},{1,16},{2,17},{3,18},{4,19},{5,20},{6,21},{7,22},{8,23},{9,... | collective-permute-start | bytes 786440 | tf_op jit(solution)/shard_map/ppermute | solution.py:44
  5.8 0.0 copy-done
  5.8 0.7 %collective-permute-start.4 = (bf16[2,64,8,256]{3,2,1,0:T(8,128)(2,1)S(1)}, bf16[2,64,8,256]{3,2,1,0:T(8,128)(2,1)S(1)}, u32[]{:S(2)}, u32[]{:S(2)}) collective-permute-start(bf16[2,64,8,256]{3,2,1,0:T(8,128)(2,1)S(1)} %copy-done), channel_id=1, source_target_pairs={{16,32},{32,16},{48,64},{64,48},{80,96},{96,80},{144,160},{160,144... | collective-permute-start | bytes 1572872 | tf_op jit(solution)/shard_map/ppermute | solution.py:29
  6.5 0.0 copy-start.1
  6.5 0.0 copy-start.2
  6.5 0.0 copy-start.3
  6.5 1.7 %near_kernel.1 = (bf16[8,128,256]{2,1,0:T(8,128)(2,1)S(1)}, bf16[4,2,256,256]{3,2,1,0:T(8,128)(2,1)S(1)}, f32[6,192,256]{2,1,0:T(8,128)S(1)}) custom-call(bf16[8,128,256]{2,1,0:T(8,128)(2,1)S(1)} %get-tuple-element.25.own_ref, bf16[2,64,8,256]{3,2,1,0:T(8,128)(2,1)S(1)} %collective-permute-done.partner_ref, bf16[192,2304]{1,0:T(8,128)(2,1)S(1)} %get-tuple-element.27.w_near_ref), custom_call_target="tpu_custom_call" | custom-call | flops 2000000000 | bytes 1048576 | tf_op jit(solution)/shard_map/near_kernel/pallas_call | solution.py:363
  8.2 1.9 %collective-permute-start.5 = (bf16[2,64,8,256]{3,2,1,0:T(8,128)(2,1)S(1)}, bf16[2,64,8,256]{3,2,1,0:T(8,128)(2,1)S(1)}, u32[]{:S(2)}, u32[]{:S(2)}) collective-permute-start(bf16[2,64,8,256]{3,2,1,0:T(8,128)(2,1)S(1)} %copy-done), channel_id=1, source_target_pairs={{112,128},{128,112},{113,129},{129,113},{114,130},{130,114},{115,1... | collective-permute-start | bytes 1572872 | tf_op jit(solution)/shard_map/ppermute | solution.py:34
  10.2 2.7 %collective-permute-done.1.rows_a_ref = bf16[2,256,256]{2,1,0:T(8,128)(2,1)S(1)} collective-permute-done((bf16[2,256,256]{2,1,0:T(8,128)(2,1)S(1)}, bf16[2,256,256]{2,1,0:T(8,128)(2,1)S(1)}, u32[]{:S(2)}, u32[]{:S(2)}) %collective-permute-start.1) | collective-permute-done | bytes 262176 | tf_op jit(solution)/shard_map/ppermute | solution.py:44
  12.9 0.0 collective-permute-start.2
  14.2 0.2 collective-permute-done.2.rows_b_ref
  14.5 1.5 %collective-permute-start.3 = (bf16[4,128,256]{2,1,0:T(8,128)(2,1)S(1)}, bf16[4,128,256]{2,1,0:T(8,128)(2,1)S(1)}, u32[]{:S(2)}, u32[]{:S(2)}) collective-permute-start(bf16[4,128,256]{2,1,0:T(8,128)(2,1)S(1)} %corner_kernel.1), channel_id=1, source_target_pairs={{0,240},{16,32},{32,16},{48,64},{64,48},{80,96},{96,80},{112,128},... | collective-permute-start | bytes 786440 | tf_op jit(solution)/shard_map/ppermute | solution.py:24
  16.0 0.0 copy-done.1
  16.0 0.0 copy-done.2
  16.0 0.0 copy-done.3
  16.0 0.2 base_kernel.1
  16.2 1.2 %rim_kernel.1.rim_part_ref = f32[4,192,256]{2,1,0:T(8,128)S(1)} custom-call(bf16[2,256,256]{2,1,0:T(8,128)(2,1)S(1)} %collective-permute-done.1.rows_a_ref, bf16[2,256,256]{2,1,0:T(8,128)(2,1)S(1)} %collective-permute-done.2.rows_b_ref, bf16[8,128,256]{2,1,0:T(8,128)(2,1)S(1)} %get-tuple-element.25.own_ref, ...), custom_call_target="tpu_custom_call" | custom-call | flops 1000000000 | bytes 1048576 | tf_op jit(solution)/shard_map/rim_kernel/pallas_call | solution.py:363
  17.4 0.0 collective-permute-done.4.most_ref
  17.4 3.4 %collective-permute-done.5.middle_ref = bf16[2,64,8,256]{3,2,1,0:T(8,128)(2,1)S(1)} collective-permute-done((bf16[2,64,8,256]{3,2,1,0:T(8,128)(2,1)S(1)}, bf16[2,64,8,256]{3,2,1,0:T(8,128)(2,1)S(1)}, u32[]{:S(2)}, u32[]{:S(2)}) %collective-permute-start.5) | collective-permute-done | bytes 524320 | tf_op jit(solution)/shard_map/ppermute | solution.py:34
  20.8 1.5 %far_kernel.1 = (bf16[6,3,192,256]{3,2,1,0:T(8,128)(2,1)S(1)}, f32[4,192,256]{2,1,0:T(8,128)S(1)}) custom-call(bf16[2,64,8,256]{3,2,1,0:T(8,128)(2,1)S(1)} %collective-permute-done.4.most_ref, bf16[2,64,8,256]{3,2,1,0:T(8,128)(2,1)S(1)} %collective-permute-done.5.middle_ref, f32[6,192,256]{2,1,0:T(8,128)S(1)} %get-tuple-element.34.part_ref, ...), custom_call_target="tpu_custom_call" | custom-call | flops 1000000000 | bytes 1048576 | tf_op jit(solution)/shard_map/far_kernel/pallas_call | solution.py:363
  22.3 0.9 %middle_kernel.1.est_in_ref = f32[2,2,512,128]{3,2,1,0:T(8,128)S(1)} custom-call(bf16[6,3,192,256]{3,2,1,0:T(8,128)(2,1)S(1)} %get-tuple-element.43.hid_ref, bf16[192,1152]{1,0:T(8,128)(2,1)S(1)} %get-tuple-element.41.w_two_ref, bf16[128,192]{1,0:T(8,128)(2,1)S(1)} %get-tuple-element.42.proj_ref), custom_call_target="tpu_custom_call" | custom-call | flops 1000000000 | bytes 1048576 | tf_op jit(solution)/shard_map/middle_kernel/pallas_call | solution.py:363
  23.2 0.4 %collective-permute-done.3.corner_ref = bf16[4,128,256]{2,1,0:T(8,128)(2,1)S(1)} collective-permute-done((bf16[4,128,256]{2,1,0:T(8,128)(2,1)S(1)}, bf16[4,128,256]{2,1,0:T(8,128)(2,1)S(1)}, u32[]{:S(2)}, u32[]{:S(2)}) %collective-permute-start.3) | collective-permute-done | bytes 262176 | tf_op jit(solution)/shard_map/ppermute | solution.py:24
  23.6 2.4 %outer_kernel.1 = f32[2,64,8,256]{3,2,1,0:T(8,128)} custom-call(bf16[4,128,256]{2,1,0:T(8,128)(2,1)S(1)} %collective-permute-done.3.corner_ref, f32[4,192,256]{2,1,0:T(8,128)S(1)} %get-tuple-element.40.part_ref, bf16[192,1152]{1,0:T(8,128)(2,1)S(1)} %get-tuple-element.37.w_far_ref, bf16[192,1152]{1,0:T(8,128)(2,1)S(1)} %get-tuple-element.41.w_two_ref, ...), custom_call_target="tpu_custom_call" | custom-call | flops 1000000000 | bytes 1048576 | tf_op jit(solution)/shard_map/outer_kernel/pallas_call | solution.py:363
  (1 shorter events, 0.0 us)
Async XLA Ops:
  0.0 5.8 %copy-start = (bf16[2,64,8,256]{3,2,1,0:T(8,128)(2,1)S(1)}, bf16[2,64,8,256]{3,2,1,0:T(8,128)(2,1)}, u32[]{:S(2)}) copy-start(bf16[2,64,8,256]{3,2,1,0:T(8,128)(2,1)} %states_ref.3) | copy-start | bytes 1572868
  0.0 2.6 %collective-permute-start = (bf16[2,64,8,256]{3,2,1,0:T(8,128)(2,1)}, bf16[2,64,8,256]{3,2,1,0:T(8,128)(2,1)S(1)}, u32[]{:S(2)}, u32[]{:S(2)}) collective-permute-start(bf16[2,64,8,256]{3,2,1,0:T(8,128)(2,1)} %states_ref.3), channel_id=1, source_target_pairs={{0,16},{16,0},{32,48},{48,32},{64,80},{80,64},{96,112},{112,96},{1... | collective-permute-start | bytes 1572872 | tf_op jit(solution)/shard_map/ppermute | solution.py:20
  2.7 10.2 %collective-permute-start.1 = (bf16[2,256,256]{2,1,0:T(8,128)(2,1)S(1)}, bf16[2,256,256]{2,1,0:T(8,128)(2,1)S(1)}, u32[]{:S(2)}, u32[]{:S(2)}) collective-permute-start(bf16[2,256,256]{2,1,0:T(8,128)(2,1)S(1)} %edge_kernel.1), channel_id=1, source_target_pairs={{0,32},{1,16},{2,17},{3,18},{4,19},{5,20},{6,21},{7,22},{8,23},{9,... | collective-permute-start | bytes 786440 | tf_op jit(solution)/shard_map/ppermute | solution.py:44
  5.8 11.6 %collective-permute-start.4 = (bf16[2,64,8,256]{3,2,1,0:T(8,128)(2,1)S(1)}, bf16[2,64,8,256]{3,2,1,0:T(8,128)(2,1)S(1)}, u32[]{:S(2)}, u32[]{:S(2)}) collective-permute-start(bf16[2,64,8,256]{3,2,1,0:T(8,128)(2,1)S(1)} %copy-done), channel_id=1, source_target_pairs={{16,32},{32,16},{48,64},{64,48},{80,96},{96,80},{144,160},{160,144... | collective-permute-start | bytes 1572872 | tf_op jit(solution)/shard_map/ppermute | solution.py:29
  6.5 9.5 %copy-start.1 = (f32[2,64,8,256]{3,2,1,0:T(8,128)S(1)}, f32[2,64,8,256]{3,2,1,0:T(8,128)}, u32[]{:S(2)}) copy-start(f32[2,64,8,256]{3,2,1,0:T(8,128)} %noise_ref) | copy-start | bytes 3145732
  6.5 9.5 %copy-start.2 = (bf16[2,64,8,256]{3,2,1,0:T(8,128)(2,1)S(1)}, bf16[2,64,8,256]{3,2,1,0:T(8,128)(2,1)}, u32[]{:S(2)}) copy-start(bf16[2,64,8,256]{3,2,1,0:T(8,128)(2,1)} %observed_ref.1) | copy-start | bytes 1572868
  6.5 9.4 %copy-start.3 = (s32[2,8,256]{2,1,0:T(8,128)S(1)}, s32[2,8,256]{2,1,0:T(8,128)}, u32[]{:S(2)}) copy-start(s32[2,8,256]{2,1,0:T(8,128)} %mask_ref.1) | copy-start | bytes 49156
  8.2 12.6 %collective-permute-start.5 = (bf16[2,64,8,256]{3,2,1,0:T(8,128)(2,1)S(1)}, bf16[2,64,8,256]{3,2,1,0:T(8,128)(2,1)S(1)}, u32[]{:S(2)}, u32[]{:S(2)}) collective-permute-start(bf16[2,64,8,256]{3,2,1,0:T(8,128)(2,1)S(1)} %copy-done), channel_id=1, source_target_pairs={{112,128},{128,112},{113,129},{129,113},{114,130},{130,114},{115,1... | collective-permute-start | bytes 1572872 | tf_op jit(solution)/shard_map/ppermute | solution.py:34
  12.9 1.5 %collective-permute-start.2 = (bf16[2,256,256]{2,1,0:T(8,128)(2,1)S(1)}, bf16[2,256,256]{2,1,0:T(8,128)(2,1)S(1)}, u32[]{:S(2)}, u32[]{:S(2)}) collective-permute-start(bf16[2,256,256]{2,1,0:T(8,128)(2,1)S(1)} %collective-permute-done.1.rows_a_ref), channel_id=1, source_target_pairs={{0,16},{16,0},{32,48},{48,32},{64,80},{80,64},{96,112},{112,96},{1... | collective-permute-start | bytes 786440 | tf_op jit(solution)/shard_map/ppermute | solution.py:20
  14.5 9.2 %collective-permute-start.3 = (bf16[4,128,256]{2,1,0:T(8,128)(2,1)S(1)}, bf16[4,128,256]{2,1,0:T(8,128)(2,1)S(1)}, u32[]{:S(2)}, u32[]{:S(2)}) collective-permute-start(bf16[4,128,256]{2,1,0:T(8,128)(2,1)S(1)} %corner_kernel.1), channel_id=1, source_target_pairs={{0,240},{16,32},{32,16},{48,64},{64,48},{80,96},{96,80},{112,128},... | collective-permute-start | bytes 786440 | tf_op jit(solution)/shard_map/ppermute | solution.py:24

commit v4 on v3

--- a/solution.py
+++ b/solution.py
@@ -80,21 +80,22 @@
 
 
 def put_hidden(dst, hid):
-    right, left = side_shifts(hid)
-    dst[0] = right.astype(BF16)
-    dst[1] = hid.astype(BF16)
-    dst[2] = left.astype(BF16)
-
-
-def two_rows(row_of, w_two_ref, t, r):
-    window = [row_of(i)[b, t * HID : (t + 1) * HID] for i in range(r - 1, r + 3) for b in range(3)]
-    return silu(dot(w_two_ref[...], jnp.concatenate(window, axis=0))).astype(BF16)
-
-
-def put_estimates(est, r, val):
-    for n in range(2):
-        est[0, pl.ds(r + n, CH, stride=ROWS), :] = val[n * CH : (n + 1) * CH, :128]
-        est[1, pl.ds(r + n, CH, stride=ROWS), :] = val[n * CH : (n + 1) * CH, 128:]
+    hid = hid.astype(BF16)
+    dst[0], dst[2] = side_shifts(hid)
+    dst[1] = hid
+
+
+def hidden_window(row_of, t, rows):
+    return jnp.concatenate([row_of(i)[b, t * HID : (t + 1) * HID] for i in rows for b in range(3)], axis=0)
+
+
+def add_estimates(acc, est_k, r, val):
+    val = est_k * val
+    for half in range(2):
+        flat = acc.at[half].reshape(CH * ROWS, 128)
+        for n in range(2):
+            rows = pl.ds(r + n, CH, stride=ROWS)
+            flat[rows, :] = flat[rows, :] + val[n * CH : (n + 1) * CH, half * 128 : (half + 1) * 128]
 
 
 def prepare_kernel(
@@ -179,27 +180,29 @@
     send_ref[pl.ds((1 - core) * 2, 2)] = jnp.where(at_end(), zero, rows_b_ref[:, mine])
 
 
-def rim_or(rim, mid, l):
-    return rim.at[l if l < 2 else l - 4] if l in (0, 1, 6, 7) else mid.at[l - 2]
-
-
-def near_kernel(own_ref, partner_ref, w_near_ref, partner_rows_ref, rim_ref, part_ref, mid):
+def near_rows(sides_ref, own_ref, partner_rows_ref, *rows):
+    return jnp.concatenate([stacked(sides_ref.at[l], own_ref[l], partner_rows_ref[l]) for l in rows], axis=0)
+
+
+def near_kernel(own_ref, partner_ref, w_near_ref, partner_rows_ref, sides_ref, part_ref, edge_part_ref):
     partner_rows_ref[...] = rows_first(partner_ref[...])
-
-    def shift_row(l):
-        put_sides(rim_or(rim_ref, mid, l), 0, own_ref[l])
-        put_sides(rim_or(rim_ref, mid, l), TWO, partner_rows_ref[l])
-
-    def row(l):
-        return stacked(rim_or(rim_ref, mid, l), own_ref[l], partner_rows_ref[l])
-
-    for l in range(3):
-        shift_row(l)
-    for r in range(1, ROWS - 1):
-        if r + 2 < ROWS:
-            shift_row(r + 2)
-        window = jnp.concatenate([row(r + a) for a in (-1, 0, 1)], axis=0)
-        part_ref[r - 1] = dot(w_near_ref[...], window)
+    for l in range(ROWS):
+        put_sides(sides_ref.at[l], 0, own_ref[l])
+        put_sides(sides_ref.at[l], TWO, partner_rows_ref[l])
+        if 2 <= l < part_ref.shape[0] + 2:
+            part_ref[l - 2] = dot(w_near_ref[...], near_rows(sides_ref, own_ref, partner_rows_ref, l - 2, l - 1, l))
+        if l == 1:
+            edge_part_ref[0] = dot(w_near_ref[:, 3 * FOUR :], near_rows(sides_ref, own_ref, partner_rows_ref, 0, 1))
+    edge_part_ref[1] = dot(w_near_ref[:, : 6 * FOUR], near_rows(sides_ref, own_ref, partner_rows_ref, 6, 7))
+    edge_part_ref[2] = dot(w_near_ref[:, : 3 * FOUR], near_rows(sides_ref, own_ref, partner_rows_ref, 7))
+
+
+def rest_kernel(own_ref, partner_rows_ref, sides_ref, w_near_ref, part_ref):
+    count = part_ref.shape[0]
+    for n in range(count):
+        r = ROWS - 1 - count + n
+        window = near_rows(sides_ref, own_ref, partner_rows_ref, r - 1, r, r + 1)
+        part_ref[n] = dot(w_near_ref[...], window)
 
 
 def base_kernel(
@@ -216,11 +219,13 @@
         weight = mask_ref[t].astype(F32) * obs_k
         current = states_ref[t].astype(F32)
         seen = observed_ref[t].astype(F32)
-        base_ref[t] = current + weight[None] * (seen - current) + noise_k[None] * noise_ref[t]
+        val = current + weight[None] * (seen - current) + noise_k[None] * noise_ref[t]
+        base_ref[t, 0] = val[:, :, :128]
+        base_ref[t, 1] = val[:, :, 128:]
 
 
 def rim_kernel(
-    rows_a_ref, rows_b_ref, own_ref, partner_rows_ref, near_ref, w_near_ref, part_ref, halo, sides
+    rows_a_ref, rows_b_ref, own_ref, partner_rows_ref, near_ref, w_near_ref, edge_part_ref, part_ref, halo, sides
 ):
     core = core_of()
     own_at = pl.multiple_of(core * TWO, TWO)
@@ -232,7 +237,7 @@
             halo[l + 2, n * TWO : (n + 1) * TWO] = jnp.where(core == 0, b, a)
 
     def tile(l):
-        return stacked(near_ref.at[l if l < 2 else l - 4], own_ref[l], partner_rows_ref[l])
+        return stacked(near_ref.at[l], own_ref[l], partner_rows_ref[l])
 
     def outside(l):
         put_sides(sides.at[l], 0, halo[l])
@@ -243,13 +248,13 @@
 
     above, below = [outside(0), outside(1)], [outside(2), outside(3)]
     part_ref[0] = near(above[0], above[1], tile(0))
-    part_ref[1] = near(above[1], tile(0), tile(1))
-    part_ref[2] = near(tile(6), tile(7), below[0])
-    part_ref[3] = near(tile(7), below[0], below[1])
+    part_ref[1] = edge_part_ref[0] + dot(w_near_ref[:, : 3 * FOUR], above[1])
+    part_ref[2] = edge_part_ref[1] + dot(w_near_ref[:, 6 * FOUR :], below[0])
+    part_ref[3] = edge_part_ref[2] + dot(w_near_ref[:, 3 * FOUR :], jnp.concatenate(below, axis=0))
 
 
 def far_kernel(
-    most_ref, middle_ref, part_ref, rim_part_ref, w_far_ref, coef_ref, hid_ref, rim_out_ref, rows_v, sides
+    most_ref, middle_ref, part_ref, part_late_ref, rim_part_ref, w_far_ref, coef_ref, hid_ref, rim_out_ref, rows_v, sides
 ):
     scale = coef_ref[0][:1]
     at, size = lax.axis_index("tm"), lax.axis_size("tm")
@@ -267,7 +272,9 @@
     for r in range(1, ROWS - 1):
         if r + 2 < ROWS:
             put_sides(sides.at[r + 2], 0, rows_v[r + 2])
-        pre = part_ref[r - 1] + far(0, r - 1, 3)
+        early = part_ref.shape[0]
+        part = part_ref[r - 1] if r <= early else part_late_ref[r - 1 - early]
+        pre = part + far(0, r - 1, 3)
         put_hidden(hid_ref.at[r - 1], silu(pre * scale))
     rim_out_ref[0] = rim_part_ref[0] + far(2, 0, 1)
     rim_out_ref[1] = rim_part_ref[1] + far(1, 0, 2)
@@ -275,12 +282,21 @@
     rim_out_ref[3] = rim_part_ref[3] + far(0, ROWS - 1, 1)
 
 
-def middle_kernel(hid_ref, w_two_ref, proj_ref, est_ref, h2s):
+def middle_kernel(hid_ref, w_two_ref, proj_ref, coef_ref, base_ref, known_ref, acc_ref, h2s):
+    est_k = coef_ref[1][:1]
+
+    def row(r):
+        return hid_ref.at[r - 1]
+
     spots = [(t, r) for t in range(2) for r in (2, 4)]
     for n, (t, r) in enumerate(spots):
-        h2s[n] = two_rows(lambda i: hid_ref.at[i - 1], w_two_ref, t, r)
+        window = hidden_window(row, t, range(r - 1, r + 3))
+        h2s[n] = silu(dot(w_two_ref[...], window)).astype(BF16)
+    for t in range(2):
+        known_ref[t, 0] = dot(w_two_ref[:, 6 * HID :], hidden_window(row, t, (1, 2)))
+        known_ref[t, 1] = dot(w_two_ref[:, : 6 * HID], hidden_window(row, t, (ROWS - 3, ROWS - 2)))
     for n, (t, r) in enumerate(spots):
-        put_estimates(est_ref.at[t], r, dot(proj_ref[...], h2s[n]))
+        add_estimates(acc_ref.at[t], est_k, r, dot(proj_ref[...], h2s[n]))
 
 
 def outer_kernel(
@@ -290,15 +306,13 @@
     w_two_ref,
     proj_ref,
     coef_ref,
-    hid_ref,
+    known_ref,
     base_ref,
-    est_in_ref,
     out_ref,
+    acc_ref,
     sides,
     hrim,
     h2s,
-    est,
-    out_v,
     sems,
 ):
     for l in range(4):
@@ -324,25 +338,19 @@
     for l in range(4):
         put_hidden(hrim.at[l], hid[l])
 
-    def row(r):
-        return hid_ref.at[r - 1] if 0 < r < ROWS - 1 else hrim.at[r + 1 if r < 1 else r - 5]
-
-    est[...] = est_in_ref[...]
-    half = CH // 2
+    est_k = coef_ref[1][:1]
+    spots = [(t, n) for n in range(2) for t in range(2)]
+    weights = (w_two_ref[:, : 6 * HID], w_two_ref[:, 6 * HID :])
+    for t, n in spots:
+        window = hidden_window(lambda i: hrim.at[i], t, (2 * n, 2 * n + 1))
+        h2s[t, n] = silu(known_ref[t, n] + dot(weights[n], window)).astype(BF16)
+    for t, n in spots:
+        add_estimates(acc_ref.at[t], est_k, n * (ROWS - 2), dot(proj_ref[...], h2s[t, n]))
     copies = []
-    for t in range(2):
-        for n, r in enumerate((0, 6)):
-            h2s[t, n] = two_rows(row, w_two_ref, t, r)
-        for n, r in enumerate((0, 6)):
-            put_estimates(est.at[t], r, dot(proj_ref[...], h2s[t, n]))
-        for n in range(2):
-            channels = slice(n * half, (n + 1) * half)
-            rows = slice(n * half * ROWS, (n + 1) * half * ROWS)
-            val = jnp.concatenate([est[t, 0, rows], est[t, 1, rows]], axis=1).reshape(half, ROWS, WID)
-            out_v[t, channels] = base_ref[t, channels] + coef_ref[1][None] * val
-            at = (t, pl.ds(n * half, half))
-            copies.append(pltpu.make_async_copy(out_v.at[at], out_ref.at[at], sems.at[2 * t + n]))
-            copies[-1].start()
+    for t, half in spots:
+        target = out_ref.at[t, :, :, pl.ds(half * 128, 128)]
+        copies.append(pltpu.make_async_copy(acc_ref.at[t, half], target, sems.at[2 * t + half]))
+        copies[-1].start()
     for copy in copies:
         copy.wait()
 
@@ -357,7 +365,7 @@
     return pltpu.with_memory_space_constraint(x, pltpu.HBM)
 
 
-def call(kernel, outs, ins, scratch=(), mib=4, flops=0, scalars=0, hbm=0, out_specs=None):
+def call(kernel, outs, ins, scratch=(), mib=4, flops=0, scalars=0, hbm=0, out_specs=None, alias=()):
     shapes = [jax.ShapeDtypeStruct(s, d) for s, d in outs]
     ins = list(ins[: len(ins) - hbm]) + [in_hbm(x) for x in ins[len(ins) - hbm :]]
     return pl.pallas_call(
@@ -366,6 +374,7 @@
         in_specs=[SMEM] * scalars + [VMEM] * (len(ins) - scalars - hbm) + [HBM] * hbm,
         out_specs=out_specs or [VMEM] * len(shapes),
         scratch_shapes=scratch,
+        input_output_aliases=dict(alias),
         compiler_params=pltpu.CompilerParams(vmem_limit_bytes=mib * 2**20),
         cost_estimate=pl.CostEstimate(flops=flops, bytes_accessed=2**20, transcendentals=0),
         name=kernel.__name__,
@@ -385,6 +394,7 @@
 ):
     tm, space = lax.axis_size("tm"), lax.axis_size("space")
     rows_shape = ((ROWS, TWO, WID), BF16)
+    acc_shape = ((2, 2, CH, ROWS, 128), F32)
     partner = core_swap(states, tm)
     own, w_near, w_far, w_two, w_proj = call(
         prepare_kernel,
@@ -410,23 +420,29 @@
     edge, states_x = lax.optimization_barrier((edge, states))
     rows_a = row_swap(edge, tm, space)
     most = most_swap(states_x, tm)
-    partner_rows, near_rim, part = call(
+    early = 5
+    partner_rows, near_sides, part, edge_part = call(
         near_kernel,
-        [rows_shape, ((4, 2, FOUR, WID), BF16), ((6, 2 * HID, WID), F32)],
+        [rows_shape, ((ROWS, 2, FOUR, WID), BF16), ((early, 2 * HID, WID), F32), ((3, 2 * HID, WID), F32)],
         [own, partner, w_near],
-        [pltpu.VMEM((4, 2, FOUR, WID), BF16)],
-        mib=16,
+        mib=8,
         flops=2 * 10**9,
     )
     states_late, part = lax.optimization_barrier((states, part))
     middle = middle_swap(states_late, tm)
-    rows_a, part = lax.optimization_barrier((rows_a, part))
+    (part_late,) = call(
+        rest_kernel,
+        [((ROWS - 2 - early, 2 * HID, WID), F32)],
+        [own, partner_rows, near_sides, w_near],
+        mib=8,
+    )
+    rows_a, part, part_late = lax.optimization_barrier((rows_a, part, part_late))
     rows_b = core_swap(rows_a, tm)
     (send,) = call(corner_kernel, [((4, TWO, WID), BF16)], [rows_a, rows_b])
     send, noise_late = lax.optimization_barrier((send, noise))
     base, coef = call(
         base_kernel,
-        [(noise.shape, F32), ((2, ROWS, WID), F32)],
+        [acc_shape, ((2, ROWS, WID), F32)],
         [sigma_now, sigma_next, station_mask, states, observed, noise_late],
         flops=10**8,
         scalars=2,
@@ -435,7 +451,7 @@
     (rim_part,) = call(
         rim_kernel,
         [((4, 2 * HID, WID), F32)],
-        [rows_a, rows_b, own, partner_rows, near_rim, w_near],
+        [rows_a, rows_b, own, partner_rows, near_sides, w_near, edge_part],
         [pltpu.VMEM((4, FOUR, WID), BF16), pltpu.VMEM((4, 2, FOUR, WID), BF16)],
         mib=12,
         flops=10**9,
@@ -443,34 +459,34 @@
     hid, rim_part = call(
         far_kernel,
         [((6, 3, 2 * HID, WID), BF16), ((4, 2 * HID, WID), F32)],
-        [most, middle, part, rim_part, w_far, coef],
+        [most, middle, part, part_late, rim_part, w_far, coef],
         [pltpu.VMEM((ROWS, TWO, WID), BF16), pltpu.VMEM((ROWS, 2, TWO, WID), BF16)],
         mib=8,
         flops=10**9,
     )
-    (est,) = call(
+    known, acc = call(
         middle_kernel,
-        [((2, 2, CH * ROWS, 128), F32)],
-        [hid, w_two, w_proj],
+        [((2, 2, 2 * HID, WID), F32), acc_shape],
+        [hid, w_two, w_proj, coef, base],
         [pltpu.VMEM((4, 2 * HID, WID), BF16)],
         mib=8,
         flops=10**9,
-    )
-    (out,) = call(
+        alias=[(4, 1)],
+    )
+    out, _ = call(
         outer_kernel,
-        [(noise.shape, F32)],
-        [corner, rim_part, w_far, w_two, w_proj, coef, hid, base, est],
+        [(noise.shape, F32), acc_shape],
+        [corner, rim_part, w_far, w_two, w_proj, coef, known, acc],
         [
             pltpu.VMEM((4, 2, TWO, WID), BF16),
             pltpu.VMEM((4, 3, 2 * HID, WID), BF16),
             pltpu.VMEM((2, 2, 2 * HID, WID), BF16),
-            pltpu.VMEM((2, 2, CH * ROWS, 128), F32),
-            pltpu.VMEM(noise.shape, F32),
             pltpu.SemaphoreType.DMA((4,)),
         ],
         mib=12,
         flops=10**9,
-        out_specs=[ANY],
+        out_specs=[ANY, VMEM],
+        alias=[(7, 1)],
     )
     return out
 

time: 26.2 us -> 25.4 us (0.969)
  waiting for transfers between devices: 6.76 us -> 5.35 us
  starting transfers between devices: 7.89 us -> 8.27 us
    ppermute x1, waiting for transfers between devices: 2.73 us -> 2.16 us  [row_swap(): return lax.ppermute(x, AXES, pairs)]
    ppermute x1, waiting for transfers between devices: 3.39 us -> 2.84 us  [middle_swap(): return lax.ppermute(x, 'tm', [(low, low + 1), (low + 1, low)])]
    ppermute x1, starting transfers between devices: 1.49 us -> 1.85 us  [side_swap(): lax.ppermute(x, 'tm', [(i, ((i + 1 ^ 1) - 1) % tm) for i in range(tm)])]
    ppermute x1, waiting for transfers between devices: 0.41 us -> 0.11 us  [side_swap(): lax.ppermute(x, 'tm', [(i, ((i + 1 ^ 1) - 1) % tm) for i in range(tm)])]
    pallas_call x9 -> x10, Pallas kernels: 9.95 us -> 10.2 us  [call(): pl.pallas_call(kernel, out_shape=shapes, in_specs=[SMEM] * scalars + [VME...]
  transfers between devices with their start and end apart: 6 -> 6, of which waited for: 4 -> 4; matrix products, arithmetic and copies ran while one was open for 0% -> 0% of each run, Pallas kernels for 29% -> 31%
where the time goes in v4:
time: 25.4 us; the launch traced here: 25.2 us
  Pallas kernels  10.2 us (40%)
  starting transfers between devices  8.27 us (33%)
  waiting for transfers between devices  5.35 us (21%)
  between operations  1.42 us (6%)
    pallas_call x10, Pallas kernels, call(): pl.pallas_call(kernel, out_shape=shapes, in_specs=[SMEM] * scalars + [VME...  10.2 us
    ppermute x1, starting transfers between devices, row_swap(): return lax.ppermute(x, AXES, pairs)  3.1 us
    ppermute x1, waiting for transfers between devices, middle_swap(): return lax.ppermute(x, 'tm', [(low, low + 1), (low + 1, low)])  2.84 us
    ppermute x1, waiting for transfers between devices, row_swap(): return lax.ppermute(x, AXES, pairs)  2.16 us
    ppermute x1, starting transfers between devices, middle_swap(): return lax.ppermute(x, 'tm', [(low, low + 1), (low + 1, low)])  1.94 us
    ppermute x1, starting transfers between devices, side_swap(): lax.ppermute(x, 'tm', [(i, ((i + 1 ^ 1) - 1) % tm) for i in range(tm)])  1.85 us
    ppermute x1, starting transfers between devices, most_swap(): lax.ppermute(x, 'tm', [(i, j) for i, j in pairs if 0 <= j < tm and i + j...  0.69 us
    ppermute x2, starting transfers between devices, core_swap(): return lax.ppermute(x, 'tm', [(i, i ^ 1) for i in range(tm)])  0.68 us
  transfers between devices with their start and end apart: 6, of which 4 were waited for; matrix products, arithmetic and copies ran while one was open for 0% of the time, Pallas kernels for 31%

profile of v4, /device:TPU:135, one launch (start us, length us, event | category | flops | bytes accessed | tf_op | source)
XLA Modules:
  0.0 25.2 jit_solution(1836448087425551811)
XLA Ops:
  0.0 0.7 %collective-permute-start = (bf16[2,64,8,256]{3,2,1,0:T(8,128)(2,1)}, bf16[2,64,8,256]{3,2,1,0:T(8,128)(2,1)S(1)}, u32[]{:S(2)}, u32[]{:S(2)}) collective-permute-start(bf16[2,64,8,256]{3,2,1,0:T(8,128)(2,1)} %states_ref.3), channel_id=1, source_target_pairs={{0,16},{16,0},{32,48},{48,32},{64,80},{80,64},{96,112},{112,96},{1... | collective-permute-start | bytes 1572872 | tf_op jit(solution)/shard_map/ppermute | solution.py:20
  0.7 1.9 %prepare_kernel.1 = (bf16[8,128,256]{2,1,0:T(8,128)(2,1)S(1)}, bf16[192,2304]{1,0:T(8,128)(2,1)S(1)}, bf16[192,1152]{1,0:T(8,128)(2,1)S(1)}, bf16[192,1152]{1,0:T(8,128)(2,1)S(1)}, bf16[128,192]{1,0:T(8,128)(2,1)S(1)}) custom-call(bf16[2,64,8,256]{3,2,1,0:T(8,128)(2,1)} %states_ref.3, bf16[3,3,96,320]{3,2,1,0:T(8,128)(2,1)} %first_ref.1, ...), custom_call_target="tpu_custom_call" | custom-call | bytes 1048576 | tf_op jit(solution)/shard_map/prepare_kernel/pallas_call | solution.py:371
  2.6 0.0 collective-permute-done.partner_ref
  2.6 0.1 edge_kernel.1
  2.7 3.1 %collective-permute-start.1 = (bf16[2,256,256]{2,1,0:T(8,128)(2,1)S(1)}, bf16[2,256,256]{2,1,0:T(8,128)(2,1)S(1)}, u32[]{:S(2)}, u32[]{:S(2)}) collective-permute-start(bf16[2,256,256]{2,1,0:T(8,128)(2,1)S(1)} %edge_kernel.1), channel_id=1, source_target_pairs={{0,32},{1,16},{2,17},{3,18},{4,19},{5,20},{6,21},{7,22},{8,23},{9,... | collective-permute-start | bytes 786440 | tf_op jit(solution)/shard_map/ppermute | solution.py:44
  5.8 0.0 copy-start
  5.8 1.8 %near_kernel.1 = (bf16[8,128,256]{2,1,0:T(8,128)(2,1)S(1)}, bf16[8,2,256,256]{3,2,1,0:T(8,128)(2,1)S(1)}, f32[5,192,256]{2,1,0:T(8,128)S(1)}, f32[3,192,256]{2,1,0:T(8,128)S(1)}) custom-call(bf16[8,128,256]{2,1,0:T(8,128)(2,1)S(1)} %get-tuple-element.30.own_ref, bf16[2,64,8,256]{3,2,1,0:T(8,128)(2,1)S(1)} %collective-permute-done.partner_ref, ...), custom_call_target="tpu_custom_call" | custom-call | flops 2000000000 | bytes 1048576 | tf_op jit(solution)/shard_map/near_kernel/pallas_call | solution.py:371
  7.6 0.0 copy-done
  7.6 1.9 %collective-permute-start.5 = (bf16[2,64,8,256]{3,2,1,0:T(8,128)(2,1)S(1)}, bf16[2,64,8,256]{3,2,1,0:T(8,128)(2,1)S(1)}, u32[]{:S(2)}, u32[]{:S(2)}) collective-permute-start(bf16[2,64,8,256]{3,2,1,0:T(8,128)(2,1)S(1)} %copy-done), channel_id=1, source_target_pairs={{112,128},{128,112},{113,129},{129,113},{114,130},{130,114},{115,1... | collective-permute-start | bytes 1572872 | tf_op jit(solution)/shard_map/ppermute | solution.py:34
  9.6 0.7 %collective-permute-start.4 = (bf16[2,64,8,256]{3,2,1,0:T(8,128)(2,1)S(1)}, bf16[2,64,8,256]{3,2,1,0:T(8,128)(2,1)S(1)}, u32[]{:S(2)}, u32[]{:S(2)}) collective-permute-start(bf16[2,64,8,256]{3,2,1,0:T(8,128)(2,1)S(1)} %copy-done), channel_id=1, source_target_pairs={{16,32},{32,16},{48,64},{64,48},{80,96},{96,80},{144,160},{160,144... | collective-permute-start | bytes 1572872 | tf_op jit(solution)/shard_map/ppermute | solution.py:29
  10.3 0.0 copy-start.1
  10.3 0.0 copy-start.2
  10.3 0.0 copy-start.3
  10.3 0.4 %rest_kernel.1.part_late_ref = f32[1,192,256]{2,1,0:T(8,128)S(1)} custom-call(bf16[8,128,256]{2,1,0:T(8,128)(2,1)S(1)} %get-tuple-element.30.own_ref, bf16[8,128,256]{2,1,0:T(8,128)(2,1)S(1)} %get-tuple-element.35.partner_rows_ref, bf16[8,2,256,256]{3,2,1,0:T(8,128)(2,1)S(1)} %get-tuple-element.36.sides_ref.near_ref, ...), custom_call_target="tpu_custom_call" | custom-call | bytes 1048576 | tf_op jit(solution)/shard_map/rest_kernel/pallas_call | solution.py:371
  10.7 2.2 %collective-permute-done.1.rows_a_ref = bf16[2,256,256]{2,1,0:T(8,128)(2,1)S(1)} collective-permute-done((bf16[2,256,256]{2,1,0:T(8,128)(2,1)S(1)}, bf16[2,256,256]{2,1,0:T(8,128)(2,1)S(1)}, u32[]{:S(2)}, u32[]{:S(2)}) %collective-permute-start.1) | collective-permute-done | bytes 262176 | tf_op jit(solution)/shard_map/ppermute | solution.py:44
  12.9 0.0 collective-permute-start.2
  14.2 0.2 collective-permute-done.2.rows_b_ref
  14.5 1.9 %collective-permute-start.3 = (bf16[4,128,256]{2,1,0:T(8,128)(2,1)S(1)}, bf16[4,128,256]{2,1,0:T(8,128)(2,1)S(1)}, u32[]{:S(2)}, u32[]{:S(2)}) collective-permute-start(bf16[4,128,256]{2,1,0:T(8,128)(2,1)S(1)} %corner_kernel.1), channel_id=1, source_target_pairs={{0,240},{16,32},{32,16},{48,64},{64,48},{80,96},{96,80},{112,128},... | collective-permute-start | bytes 786440 | tf_op jit(solution)/shard_map/ppermute | solution.py:24
  16.3 0.0 copy-done.1
  16.3 0.0 copy-done.2
  16.3 0.0 copy-done.3
  16.3 0.3 %base_kernel.1 = (f32[2,2,64,8,128]{4,3,2,1,0:T(8,128)S(1)}, f32[2,8,256]{2,1,0:T(8,128)S(1)}) custom-call(f32[1]{0:T(128)S(6)} %copy.14.now_ref, f32[1]{0:T(128)S(6)} %copy.15.next_ref, s32[2,8,256]{2,1,0:T(8,128)S(1)} %copy-done.3, bf16[2,64,8,256]{3,2,1,0:T(8,128)(2,1)S(1)} %copy-done, bf16[2,64,8,256]{3,2,1,0:T(8,128)(2,1)S(1)} %copy-done.2, ...), custom_call_target="tpu_custom_call" | custom-call | flops 100000000 | bytes 1048576 | tf_op jit(solution)/shard_map/base_kernel/pallas_call | solution.py:371
  16.6 0.8 %rim_kernel.1.rim_part_ref = f32[4,192,256]{2,1,0:T(8,128)S(1)} custom-call(bf16[2,256,256]{2,1,0:T(8,128)(2,1)S(1)} %collective-permute-done.1.rows_a_ref, bf16[2,256,256]{2,1,0:T(8,128)(2,1)S(1)} %collective-permute-done.2.rows_b_ref, bf16[8,128,256]{2,1,0:T(8,128)(2,1)S(1)} %get-tuple-element.30.own_ref, ...), custom_call_target="tpu_custom_call" | custom-call | flops 1000000000 | bytes 1048576 | tf_op jit(solution)/shard_map/rim_kernel/pallas_call | solution.py:371
  17.4 2.8 %collective-permute-done.5.middle_ref = bf16[2,64,8,256]{3,2,1,0:T(8,128)(2,1)S(1)} collective-permute-done((bf16[2,64,8,256]{3,2,1,0:T(8,128)(2,1)S(1)}, bf16[2,64,8,256]{3,2,1,0:T(8,128)(2,1)S(1)}, u32[]{:S(2)}, u32[]{:S(2)}) %collective-permute-start.5) | collective-permute-done | bytes 524320 | tf_op jit(solution)/shard_map/ppermute | solution.py:34
  20.2 0.0 collective-permute-done.4.most_ref
  20.3 1.5 %far_kernel.1 = (bf16[6,3,192,256]{3,2,1,0:T(8,128)(2,1)S(1)}, f32[4,192,256]{2,1,0:T(8,128)S(1)}) custom-call(bf16[2,64,8,256]{3,2,1,0:T(8,128)(2,1)S(1)} %collective-permute-done.4.most_ref, bf16[2,64,8,256]{3,2,1,0:T(8,128)(2,1)S(1)} %collective-permute-done.5.middle_ref, f32[5,192,256]{2,1,0:T(8,128)S(1)} %get-tuple-element.41.part_ref, ...), custom_call_target="tpu_custom_call" | custom-call | flops 1000000000 | bytes 1048576 | tf_op jit(solution)/shard_map/far_kernel/pallas_call | solution.py:371
  21.8 1.2 %middle_kernel.1 = (f32[2,2,192,256]{3,2,1,0:T(8,128)S(1)}, f32[2,2,64,8,128]{4,3,2,1,0:T(8,128)S(1)}) custom-call(bf16[6,3,192,256]{3,2,1,0:T(8,128)(2,1)S(1)} %get-tuple-element.50.hid_ref, bf16[192,1152]{1,0:T(8,128)(2,1)S(1)} %get-tuple-element.48.w_two_ref, bf16[128,192]{1,0:T(8,128)(2,1)S(1)} %get-tuple-element.49.proj_ref, ...), custom_call_target="tpu_custom_call", output_to_operand_aliasing={{1}: (4, {})} | custom-call | flops 1000000000 | bytes 1048576 | tf_op jit(solution)/shard_map/middle_kernel/pallas_call | solution.py:371
  22.9 0.1 collective-permute-done.3.corner_ref
  23.1 2.2 %outer_kernel.1 = (f32[2,64,8,256]{3,2,1,0:T(8,128)}, f32[2,2,64,8,128]{4,3,2,1,0:T(8,128)S(1)}) custom-call(bf16[4,128,256]{2,1,0:T(8,128)(2,1)S(1)} %collective-permute-done.3.corner_ref, f32[4,192,256]{2,1,0:T(8,128)S(1)} %get-tuple-element.47.part_ref, bf16[192,1152]{1,0:T(8,128)(2,1)S(1)} %get-tuple-element.44.w_far_ref, ...), custom_call_target="tpu_custom_call", output_to_operand_aliasing={{1}: (7, {})} | custom-call | flops 1000000000 | bytes 1048576 | tf_op jit(solution)/shard_map/outer_kernel/pallas_call | solution.py:371
  (1 shorter events, 0.0 us)
Async XLA Ops:
  0.0 2.6 %collective-permute-start = (bf16[2,64,8,256]{3,2,1,0:T(8,128)(2,1)}, bf16[2,64,8,256]{3,2,1,0:T(8,128)(2,1)S(1)}, u32[]{:S(2)}, u32[]{:S(2)}) collective-permute-start(bf16[2,64,8,256]{3,2,1,0:T(8,128)(2,1)} %states_ref.3), channel_id=1, source_target_pairs={{0,16},{16,0},{32,48},{48,32},{64,80},{80,64},{96,112},{112,96},{1... | collective-permute-start | bytes 1572872 | tf_op jit(solution)/shard_map/ppermute | solution.py:20
  2.7 10.2 %collective-permute-start.1 = (bf16[2,256,256]{2,1,0:T(8,128)(2,1)S(1)}, bf16[2,256,256]{2,1,0:T(8,128)(2,1)S(1)}, u32[]{:S(2)}, u32[]{:S(2)}) collective-permute-start(bf16[2,256,256]{2,1,0:T(8,128)(2,1)S(1)} %edge_kernel.1), channel_id=1, source_target_pairs={{0,32},{1,16},{2,17},{3,18},{4,19},{5,20},{6,21},{7,22},{8,23},{9,... | collective-permute-start | bytes 786440 | tf_op jit(solution)/shard_map/ppermute | solution.py:44
  5.8 1.8 %copy-start = (bf16[2,64,8,256]{3,2,1,0:T(8,128)(2,1)S(1)}, bf16[2,64,8,256]{3,2,1,0:T(8,128)(2,1)}, u32[]{:S(2)}) copy-start(bf16[2,64,8,256]{3,2,1,0:T(8,128)(2,1)} %states_ref.3) | copy-start | bytes 1572868
  7.6 12.6 %collective-permute-start.5 = (bf16[2,64,8,256]{3,2,1,0:T(8,128)(2,1)S(1)}, bf16[2,64,8,256]{3,2,1,0:T(8,128)(2,1)S(1)}, u32[]{:S(2)}, u32[]{:S(2)}) collective-permute-start(bf16[2,64,8,256]{3,2,1,0:T(8,128)(2,1)S(1)} %copy-done), channel_id=1, source_target_pairs={{112,128},{128,112},{113,129},{129,113},{114,130},{130,114},{115,1... | collective-permute-start | bytes 1572872 | tf_op jit(solution)/shard_map/ppermute | solution.py:34
  9.6 10.7 %collective-permute-start.4 = (bf16[2,64,8,256]{3,2,1,0:T(8,128)(2,1)S(1)}, bf16[2,64,8,256]{3,2,1,0:T(8,128)(2,1)S(1)}, u32[]{:S(2)}, u32[]{:S(2)}) collective-permute-start(bf16[2,64,8,256]{3,2,1,0:T(8,128)(2,1)S(1)} %copy-done), channel_id=1, source_target_pairs={{16,32},{32,16},{48,64},{64,48},{80,96},{96,80},{144,160},{160,144... | collective-permute-start | bytes 1572872 | tf_op jit(solution)/shard_map/ppermute | solution.py:29
  10.3 6.0 %copy-start.1 = (f32[2,64,8,256]{3,2,1,0:T(8,128)S(1)}, f32[2,64,8,256]{3,2,1,0:T(8,128)}, u32[]{:S(2)}) copy-start(f32[2,64,8,256]{3,2,1,0:T(8,128)} %noise_ref) | copy-start | bytes 3145732
  10.3 6.0 %copy-start.2 = (bf16[2,64,8,256]{3,2,1,0:T(8,128)(2,1)S(1)}, bf16[2,64,8,256]{3,2,1,0:T(8,128)(2,1)}, u32[]{:S(2)}) copy-start(bf16[2,64,8,256]{3,2,1,0:T(8,128)(2,1)} %observed_ref.1) | copy-start | bytes 1572868
  10.3 6.0 %copy-start.3 = (s32[2,8,256]{2,1,0:T(8,128)S(1)}, s32[2,8,256]{2,1,0:T(8,128)}, u32[]{:S(2)}) copy-start(s32[2,8,256]{2,1,0:T(8,128)} %mask_ref.1) | copy-start | bytes 49156
  12.9 1.5 %collective-permute-start.2 = (bf16[2,256,256]{2,1,0:T(8,128)(2,1)S(1)}, bf16[2,256,256]{2,1,0:T(8,128)(2,1)S(1)}, u32[]{:S(2)}, u32[]{:S(2)}) collective-permute-start(bf16[2,256,256]{2,1,0:T(8,128)(2,1)S(1)} %collective-permute-done.1.rows_a_ref), channel_id=1, source_target_pairs={{0,16},{16,0},{32,48},{48,32},{64,80},{80,64},{96,112},{112,96},{1... | collective-permute-start | bytes 786440 | tf_op jit(solution)/shard_map/ppermute | solution.py:20
  14.5 8.6 %collective-permute-start.3 = (bf16[4,128,256]{2,1,0:T(8,128)(2,1)S(1)}, bf16[4,128,256]{2,1,0:T(8,128)(2,1)S(1)}, u32[]{:S(2)}, u32[]{:S(2)}) collective-permute-start(bf16[4,128,256]{2,1,0:T(8,128)(2,1)S(1)} %corner_kernel.1), channel_id=1, source_target_pairs={{0,240},{16,32},{32,16},{48,64},{64,48},{80,96},{96,80},{112,128},... | collective-permute-start | bytes 786440 | tf_op jit(solution)/shard_map/ppermute | solution.py:24

commit v5 on v4

--- a/solution.py
+++ b/solution.py
@@ -194,7 +194,6 @@
         if l == 1:
             edge_part_ref[0] = dot(w_near_ref[:, 3 * FOUR :], near_rows(sides_ref, own_ref, partner_rows_ref, 0, 1))
     edge_part_ref[1] = dot(w_near_ref[:, : 6 * FOUR], near_rows(sides_ref, own_ref, partner_rows_ref, 6, 7))
-    edge_part_ref[2] = dot(w_near_ref[:, : 3 * FOUR], near_rows(sides_ref, own_ref, partner_rows_ref, 7))
 
 
 def rest_kernel(own_ref, partner_rows_ref, sides_ref, w_near_ref, part_ref):
@@ -250,7 +249,7 @@
     part_ref[0] = near(above[0], above[1], tile(0))
     part_ref[1] = edge_part_ref[0] + dot(w_near_ref[:, : 3 * FOUR], above[1])
     part_ref[2] = edge_part_ref[1] + dot(w_near_ref[:, 6 * FOUR :], below[0])
-    part_ref[3] = edge_part_ref[2] + dot(w_near_ref[:, 3 * FOUR :], jnp.concatenate(below, axis=0))
+    part_ref[3] = near(tile(7), below[0], below[1])
 
 
 def far_kernel(
@@ -344,13 +343,15 @@
     for t, n in spots:
         window = hidden_window(lambda i: hrim.at[i], t, (2 * n, 2 * n + 1))
         h2s[t, n] = silu(known_ref[t, n] + dot(weights[n], window)).astype(BF16)
-    for t, n in spots:
-        add_estimates(acc_ref.at[t], est_k, n * (ROWS - 2), dot(proj_ref[...], h2s[t, n]))
+    vals = {(t, n): dot(proj_ref[...], h2s[t, n]) for t, n in spots}
     copies = []
-    for t, half in spots:
-        target = out_ref.at[t, :, :, pl.ds(half * 128, 128)]
-        copies.append(pltpu.make_async_copy(acc_ref.at[t, half], target, sems.at[2 * t + half]))
-        copies[-1].start()
+    for t in range(2):
+        for n in range(2):
+            add_estimates(acc_ref.at[t], est_k, n * (ROWS - 2), vals[t, n])
+        for half in range(2):
+            target = out_ref.at[t, :, :, pl.ds(half * 128, 128)]
+            copies.append(pltpu.make_async_copy(acc_ref.at[t, half], target, sems.at[2 * t + half]))
+            copies[-1].start()
     for copy in copies:
         copy.wait()
 
@@ -423,7 +424,7 @@
     early = 5
     partner_rows, near_sides, part, edge_part = call(
         near_kernel,
-        [rows_shape, ((ROWS, 2, FOUR, WID), BF16), ((early, 2 * HID, WID), F32), ((3, 2 * HID, WID), F32)],
+        [rows_shape, ((ROWS, 2, FOUR, WID), BF16), ((early, 2 * HID, WID), F32), ((2, 2 * HID, WID), F32)],
         [own, partner, w_near],
         mib=8,
         flops=2 * 10**9,

time: 25.4 us -> 25.3 us (level)
  transfers between devices with their start and end apart: 6 -> 6, of which waited for: 4 -> 4; matrix products, arithmetic and copies ran while one was open for 0% -> 0% of each run, Pallas kernels for 31% -> 32%
where the time goes in v5:
time: 25.3 us; the launch traced here: 25.1 us
  Pallas kernels  10.2 us (40%)
  starting transfers between devices  8.2 us (32%)
  waiting for transfers between devices  5.29 us (21%)
  between operations  1.42 us (6%)
    pallas_call x10, Pallas kernels, call(): pl.pallas_call(kernel, out_shape=shapes, in_specs=[SMEM] * scalars + [VME...  10.2 us
    ppermute x1, starting transfers between devices, row_swap(): return lax.ppermute(x, AXES, pairs)  3.1 us
    ppermute x1, waiting for transfers between devices, middle_swap(): return lax.ppermute(x, 'tm', [(low, low + 1), (low + 1, low)])  2.69 us
    ppermute x1, waiting for transfers between devices, row_swap(): return lax.ppermute(x, AXES, pairs)  2.25 us
    ppermute x1, starting transfers between devices, middle_swap(): return lax.ppermute(x, 'tm', [(low, low + 1), (low + 1, low)])  1.94 us
    ppermute x1, starting transfers between devices, side_swap(): lax.ppermute(x, 'tm', [(i, ((i + 1 ^ 1) - 1) % tm) for i in range(tm)])  1.78 us
    ppermute x1, starting transfers between devices, most_swap(): lax.ppermute(x, 'tm', [(i, j) for i, j in pairs if 0 <= j < tm and i + j...  0.69 us
    ppermute x2, starting transfers between devices, core_swap(): return lax.ppermute(x, 'tm', [(i, i ^ 1) for i in range(tm)])  0.68 us
  transfers between devices with their start and end apart: 6, of which 4 were waited for; matrix products, arithmetic and copies ran while one was open for 0% of the time, Pallas kernels for 32%

profile of v5, /device:TPU:135, one launch (start us, length us, event | category | flops | bytes accessed | tf_op | source)
XLA Modules:
  0.0 25.1 jit_solution(8204971330169795653)
XLA Ops:
  0.0 0.7 %collective-permute-start = (bf16[2,64,8,256]{3,2,1,0:T(8,128)(2,1)}, bf16[2,64,8,256]{3,2,1,0:T(8,128)(2,1)S(1)}, u32[]{:S(2)}, u32[]{:S(2)}) collective-permute-start(bf16[2,64,8,256]{3,2,1,0:T(8,128)(2,1)} %states_ref.3), channel_id=1, source_target_pairs={{0,16},{16,0},{32,48},{48,32},{64,80},{80,64},{96,112},{112,96},{1... | collective-permute-start | bytes 1572872 | tf_op jit(solution)/shard_map/ppermute | solution.py:20
  0.7 1.9 %prepare_kernel.1 = (bf16[8,128,256]{2,1,0:T(8,128)(2,1)S(1)}, bf16[192,2304]{1,0:T(8,128)(2,1)S(1)}, bf16[192,1152]{1,0:T(8,128)(2,1)S(1)}, bf16[192,1152]{1,0:T(8,128)(2,1)S(1)}, bf16[128,192]{1,0:T(8,128)(2,1)S(1)}) custom-call(bf16[2,64,8,256]{3,2,1,0:T(8,128)(2,1)} %states_ref.3, bf16[3,3,96,320]{3,2,1,0:T(8,128)(2,1)} %first_ref.1, ...), custom_call_target="tpu_custom_call" | custom-call | bytes 1048576 | tf_op jit(solution)/shard_map/prepare_kernel/pallas_call | solution.py:372
  2.6 0.0 collective-permute-done.partner_ref
  2.6 0.1 edge_kernel.1
  2.7 3.1 %collective-permute-start.1 = (bf16[2,256,256]{2,1,0:T(8,128)(2,1)S(1)}, bf16[2,256,256]{2,1,0:T(8,128)(2,1)S(1)}, u32[]{:S(2)}, u32[]{:S(2)}) collective-permute-start(bf16[2,256,256]{2,1,0:T(8,128)(2,1)S(1)} %edge_kernel.1), channel_id=1, source_target_pairs={{0,32},{1,16},{2,17},{3,18},{4,19},{5,20},{6,21},{7,22},{8,23},{9,... | collective-permute-start | bytes 786440 | tf_op jit(solution)/shard_map/ppermute | solution.py:44
  5.8 0.0 copy-start
  5.8 1.7 %near_kernel.1 = (bf16[8,128,256]{2,1,0:T(8,128)(2,1)S(1)}, bf16[8,2,256,256]{3,2,1,0:T(8,128)(2,1)S(1)}, f32[5,192,256]{2,1,0:T(8,128)S(1)}, f32[2,192,256]{2,1,0:T(8,128)S(1)}) custom-call(bf16[8,128,256]{2,1,0:T(8,128)(2,1)S(1)} %get-tuple-element.30.own_ref, bf16[2,64,8,256]{3,2,1,0:T(8,128)(2,1)S(1)} %collective-permute-done.partner_ref, ...), custom_call_target="tpu_custom_call" | custom-call | flops 2000000000 | bytes 1048576 | tf_op jit(solution)/shard_map/near_kernel/pallas_call | solution.py:372
  7.5 0.0 copy-done
  7.5 1.9 %collective-permute-start.5 = (bf16[2,64,8,256]{3,2,1,0:T(8,128)(2,1)S(1)}, bf16[2,64,8,256]{3,2,1,0:T(8,128)(2,1)S(1)}, u32[]{:S(2)}, u32[]{:S(2)}) collective-permute-start(bf16[2,64,8,256]{3,2,1,0:T(8,128)(2,1)S(1)} %copy-done), channel_id=1, source_target_pairs={{112,128},{128,112},{113,129},{129,113},{114,130},{130,114},{115,1... | collective-permute-start | bytes 1572872 | tf_op jit(solution)/shard_map/ppermute | solution.py:34
  9.5 0.7 %collective-permute-start.4 = (bf16[2,64,8,256]{3,2,1,0:T(8,128)(2,1)S(1)}, bf16[2,64,8,256]{3,2,1,0:T(8,128)(2,1)S(1)}, u32[]{:S(2)}, u32[]{:S(2)}) collective-permute-start(bf16[2,64,8,256]{3,2,1,0:T(8,128)(2,1)S(1)} %copy-done), channel_id=1, source_target_pairs={{16,32},{32,16},{48,64},{64,48},{80,96},{96,80},{144,160},{160,144... | collective-permute-start | bytes 1572872 | tf_op jit(solution)/shard_map/ppermute | solution.py:29
  10.2 0.0 copy-start.1
  10.2 0.0 copy-start.2
  10.2 0.0 copy-start.3
  10.2 0.4 %rest_kernel.1.part_late_ref = f32[1,192,256]{2,1,0:T(8,128)S(1)} custom-call(bf16[8,128,256]{2,1,0:T(8,128)(2,1)S(1)} %get-tuple-element.30.own_ref, bf16[8,128,256]{2,1,0:T(8,128)(2,1)S(1)} %get-tuple-element.35.partner_rows_ref, bf16[8,2,256,256]{3,2,1,0:T(8,128)(2,1)S(1)} %get-tuple-element.36.sides_ref.near_ref, ...), custom_call_target="tpu_custom_call" | custom-call | bytes 1048576 | tf_op jit(solution)/shard_map/rest_kernel/pallas_call | solution.py:372
  10.6 2.2 %collective-permute-done.1.rows_a_ref = bf16[2,256,256]{2,1,0:T(8,128)(2,1)S(1)} collective-permute-done((bf16[2,256,256]{2,1,0:T(8,128)(2,1)S(1)}, bf16[2,256,256]{2,1,0:T(8,128)(2,1)S(1)}, u32[]{:S(2)}, u32[]{:S(2)}) %collective-permute-start.1) | collective-permute-done | bytes 262176 | tf_op jit(solution)/shard_map/ppermute | solution.py:44
  12.9 0.0 collective-permute-start.2
  14.2 0.2 collective-permute-done.2.rows_b_ref
  14.5 1.8 %collective-permute-start.3 = (bf16[4,128,256]{2,1,0:T(8,128)(2,1)S(1)}, bf16[4,128,256]{2,1,0:T(8,128)(2,1)S(1)}, u32[]{:S(2)}, u32[]{:S(2)}) collective-permute-start(bf16[4,128,256]{2,1,0:T(8,128)(2,1)S(1)} %corner_kernel.1), channel_id=1, source_target_pairs={{0,240},{16,32},{32,16},{48,64},{64,48},{80,96},{96,80},{112,128},... | collective-permute-start | bytes 786440 | tf_op jit(solution)/shard_map/ppermute | solution.py:24
  16.2 0.0 copy-done.1
  16.3 0.0 copy-done.2
  16.3 0.0 copy-done.3
  16.3 0.3 %base_kernel.1 = (f32[2,2,64,8,128]{4,3,2,1,0:T(8,128)S(1)}, f32[2,8,256]{2,1,0:T(8,128)S(1)}) custom-call(f32[1]{0:T(128)S(6)} %copy.14.now_ref, f32[1]{0:T(128)S(6)} %copy.15.next_ref, s32[2,8,256]{2,1,0:T(8,128)S(1)} %copy-done.3, bf16[2,64,8,256]{3,2,1,0:T(8,128)(2,1)S(1)} %copy-done, bf16[2,64,8,256]{3,2,1,0:T(8,128)(2,1)S(1)} %copy-done.2, ...), custom_call_target="tpu_custom_call" | custom-call | flops 100000000 | bytes 1048576 | tf_op jit(solution)/shard_map/base_kernel/pallas_call | solution.py:372
  16.6 0.9 %rim_kernel.1.rim_part_ref = f32[4,192,256]{2,1,0:T(8,128)S(1)} custom-call(bf16[2,256,256]{2,1,0:T(8,128)(2,1)S(1)} %collective-permute-done.1.rows_a_ref, bf16[2,256,256]{2,1,0:T(8,128)(2,1)S(1)} %collective-permute-done.2.rows_b_ref, bf16[8,128,256]{2,1,0:T(8,128)(2,1)S(1)} %get-tuple-element.30.own_ref, ...), custom_call_target="tpu_custom_call" | custom-call | flops 1000000000 | bytes 1048576 | tf_op jit(solution)/shard_map/rim_kernel/pallas_call | solution.py:372
  17.5 2.7 %collective-permute-done.5.middle_ref = bf16[2,64,8,256]{3,2,1,0:T(8,128)(2,1)S(1)} collective-permute-done((bf16[2,64,8,256]{3,2,1,0:T(8,128)(2,1)S(1)}, bf16[2,64,8,256]{3,2,1,0:T(8,128)(2,1)S(1)}, u32[]{:S(2)}, u32[]{:S(2)}) %collective-permute-start.5) | collective-permute-done | bytes 524320 | tf_op jit(solution)/shard_map/ppermute | solution.py:34
  20.2 0.0 collective-permute-done.4.most_ref
  20.2 1.5 %far_kernel.1 = (bf16[6,3,192,256]{3,2,1,0:T(8,128)(2,1)S(1)}, f32[4,192,256]{2,1,0:T(8,128)S(1)}) custom-call(bf16[2,64,8,256]{3,2,1,0:T(8,128)(2,1)S(1)} %collective-permute-done.4.most_ref, bf16[2,64,8,256]{3,2,1,0:T(8,128)(2,1)S(1)} %collective-permute-done.5.middle_ref, f32[5,192,256]{2,1,0:T(8,128)S(1)} %get-tuple-element.41.part_ref, ...), custom_call_target="tpu_custom_call" | custom-call | flops 1000000000 | bytes 1048576 | tf_op jit(solution)/shard_map/far_kernel/pallas_call | solution.py:372
  21.7 1.2 %middle_kernel.1 = (f32[2,2,192,256]{3,2,1,0:T(8,128)S(1)}, f32[2,2,64,8,128]{4,3,2,1,0:T(8,128)S(1)}) custom-call(bf16[6,3,192,256]{3,2,1,0:T(8,128)(2,1)S(1)} %get-tuple-element.50.hid_ref, bf16[192,1152]{1,0:T(8,128)(2,1)S(1)} %get-tuple-element.48.w_two_ref, bf16[128,192]{1,0:T(8,128)(2,1)S(1)} %get-tuple-element.49.proj_ref, ...), custom_call_target="tpu_custom_call", output_to_operand_aliasing={{1}: (4, {})} | custom-call | flops 1000000000 | bytes 1048576 | tf_op jit(solution)/shard_map/middle_kernel/pallas_call | solution.py:372
  22.9 0.1 collective-permute-done.3.corner_ref
  23.0 2.1 %outer_kernel.1 = (f32[2,64,8,256]{3,2,1,0:T(8,128)}, f32[2,2,64,8,128]{4,3,2,1,0:T(8,128)S(1)}) custom-call(bf16[4,128,256]{2,1,0:T(8,128)(2,1)S(1)} %collective-permute-done.3.corner_ref, f32[4,192,256]{2,1,0:T(8,128)S(1)} %get-tuple-element.47.part_ref, bf16[192,1152]{1,0:T(8,128)(2,1)S(1)} %get-tuple-element.44.w_far_ref, ...), custom_call_target="tpu_custom_call", output_to_operand_aliasing={{1}: (7, {})} | custom-call | flops 1000000000 | bytes 1048576 | tf_op jit(solution)/shard_map/outer_kernel/pallas_call | solution.py:372
  (1 shorter events, 0.0 us)
Async XLA Ops:
  0.0 2.6 %collective-permute-start = (bf16[2,64,8,256]{3,2,1,0:T(8,128)(2,1)}, bf16[2,64,8,256]{3,2,1,0:T(8,128)(2,1)S(1)}, u32[]{:S(2)}, u32[]{:S(2)}) collective-permute-start(bf16[2,64,8,256]{3,2,1,0:T(8,128)(2,1)} %states_ref.3), channel_id=1, source_target_pairs={{0,16},{16,0},{32,48},{48,32},{64,80},{80,64},{96,112},{112,96},{1... | collective-permute-start | bytes 1572872 | tf_op jit(solution)/shard_map/ppermute | solution.py:20
  2.7 10.2 %collective-permute-start.1 = (bf16[2,256,256]{2,1,0:T(8,128)(2,1)S(1)}, bf16[2,256,256]{2,1,0:T(8,128)(2,1)S(1)}, u32[]{:S(2)}, u32[]{:S(2)}) collective-permute-start(bf16[2,256,256]{2,1,0:T(8,128)(2,1)S(1)} %edge_kernel.1), channel_id=1, source_target_pairs={{0,32},{1,16},{2,17},{3,18},{4,19},{5,20},{6,21},{7,22},{8,23},{9,... | collective-permute-start | bytes 786440 | tf_op jit(solution)/shard_map/ppermute | solution.py:44
  5.8 1.7 %copy-start = (bf16[2,64,8,256]{3,2,1,0:T(8,128)(2,1)S(1)}, bf16[2,64,8,256]{3,2,1,0:T(8,128)(2,1)}, u32[]{:S(2)}) copy-start(bf16[2,64,8,256]{3,2,1,0:T(8,128)(2,1)} %states_ref.3) | copy-start | bytes 1572868
  7.5 12.6 %collective-permute-start.5 = (bf16[2,64,8,256]{3,2,1,0:T(8,128)(2,1)S(1)}, bf16[2,64,8,256]{3,2,1,0:T(8,128)(2,1)S(1)}, u32[]{:S(2)}, u32[]{:S(2)}) collective-permute-start(bf16[2,64,8,256]{3,2,1,0:T(8,128)(2,1)S(1)} %copy-done), channel_id=1, source_target_pairs={{112,128},{128,112},{113,129},{129,113},{114,130},{130,114},{115,1... | collective-permute-start | bytes 1572872 | tf_op jit(solution)/shard_map/ppermute | solution.py:34
  9.5 10.7 %collective-permute-start.4 = (bf16[2,64,8,256]{3,2,1,0:T(8,128)(2,1)S(1)}, bf16[2,64,8,256]{3,2,1,0:T(8,128)(2,1)S(1)}, u32[]{:S(2)}, u32[]{:S(2)}) collective-permute-start(bf16[2,64,8,256]{3,2,1,0:T(8,128)(2,1)S(1)} %copy-done), channel_id=1, source_target_pairs={{16,32},{32,16},{48,64},{64,48},{80,96},{96,80},{144,160},{160,144... | collective-permute-start | bytes 1572872 | tf_op jit(solution)/shard_map/ppermute | solution.py:29
  10.2 6.1 %copy-start.1 = (f32[2,64,8,256]{3,2,1,0:T(8,128)S(1)}, f32[2,64,8,256]{3,2,1,0:T(8,128)}, u32[]{:S(2)}) copy-start(f32[2,64,8,256]{3,2,1,0:T(8,128)} %noise_ref) | copy-start | bytes 3145732
  10.2 6.0 %copy-start.2 = (bf16[2,64,8,256]{3,2,1,0:T(8,128)(2,1)S(1)}, bf16[2,64,8,256]{3,2,1,0:T(8,128)(2,1)}, u32[]{:S(2)}) copy-start(bf16[2,64,8,256]{3,2,1,0:T(8,128)(2,1)} %observed_ref.1) | copy-start | bytes 1572868
  10.2 6.0 %copy-start.3 = (s32[2,8,256]{2,1,0:T(8,128)S(1)}, s32[2,8,256]{2,1,0:T(8,128)}, u32[]{:S(2)}) copy-start(s32[2,8,256]{2,1,0:T(8,128)} %mask_ref.1) | copy-start | bytes 49156
  12.9 1.5 %collective-permute-start.2 = (bf16[2,256,256]{2,1,0:T(8,128)(2,1)S(1)}, bf16[2,256,256]{2,1,0:T(8,128)(2,1)S(1)}, u32[]{:S(2)}, u32[]{:S(2)}) collective-permute-start(bf16[2,256,256]{2,1,0:T(8,128)(2,1)S(1)} %collective-permute-done.1.rows_a_ref), channel_id=1, source_target_pairs={{0,16},{16,0},{32,48},{48,32},{64,80},{80,64},{96,112},{112,96},{1... | collective-permute-start | bytes 786440 | tf_op jit(solution)/shard_map/ppermute | solution.py:20
  14.5 8.5 %collective-permute-start.3 = (bf16[4,128,256]{2,1,0:T(8,128)(2,1)S(1)}, bf16[4,128,256]{2,1,0:T(8,128)(2,1)S(1)}, u32[]{:S(2)}, u32[]{:S(2)}) collective-permute-start(bf16[4,128,256]{2,1,0:T(8,128)(2,1)S(1)} %corner_kernel.1), channel_id=1, source_target_pairs={{0,240},{16,32},{32,16},{48,64},{64,48},{80,96},{96,80},{112,128},... | collective-permute-start | bytes 786440 | tf_op jit(solution)/shard_map/ppermute | solution.py:24

commit v6 on v5

--- a/solution.py
+++ b/solution.py
@@ -157,12 +157,13 @@
 
 def edge_kernel(own_ref, partner_ref, edge_ref):
     core = core_of()
-    other = rows_first(partner_ref[...])
+    other = partner_ref[...].reshape(TWO, ROWS, WID)
+    other = jnp.swapaxes(jnp.where(core == 0, other[:, :2], other[:, ROWS - 2 :]), 0, 1)
     last = jnp.where(core == 0, 0, lax.axis_size("space") - 1)
     inside = lax.axis_index("space") != last
     zero = jnp.zeros((), BF16)
     mine = jnp.where(inside, own_ref[pl.ds(core * (ROWS - 2), 2)], zero)
-    other = jnp.where(inside, jnp.where(core == 0, other[:2], other[-2:]), zero)
+    other = jnp.where(inside, other, zero)
     edge_ref[:, pl.ds(pl.multiple_of(core * TWO, TWO), TWO)] = mine
     edge_ref[:, pl.ds(pl.multiple_of((1 - core) * TWO, TWO), TWO)] = other
 

time: 25.3 us -> 25.3 us (level)
  no operation moved by 1% of the time
where the time goes in v6:
time: 25.3 us; the launch traced here: 25.1 us
  Pallas kernels  10.2 us (40%)
  starting transfers between devices  8.2 us (32%)
  waiting for transfers between devices  5.29 us (21%)
  between operations  1.42 us (6%)
    pallas_call x10, Pallas kernels, call(): pl.pallas_call(kernel, out_shape=shapes, in_specs=[SMEM] * scalars + [VME...  10.2 us
    ppermute x1, starting transfers between devices, row_swap(): return lax.ppermute(x, AXES, pairs)  3.1 us
    ppermute x1, waiting for transfers between devices, middle_swap(): return lax.ppermute(x, 'tm', [(low, low + 1), (low + 1, low)])  2.69 us
    ppermute x1, waiting for transfers between devices, row_swap(): return lax.ppermute(x, AXES, pairs)  2.25 us
    ppermute x1, starting transfers between devices, middle_swap(): return lax.ppermute(x, 'tm', [(low, low + 1), (low + 1, low)])  1.94 us
    ppermute x1, starting transfers between devices, side_swap(): lax.ppermute(x, 'tm', [(i, ((i + 1 ^ 1) - 1) % tm) for i in range(tm)])  1.78 us
    ppermute x1, starting transfers between devices, most_swap(): lax.ppermute(x, 'tm', [(i, j) for i, j in pairs if 0 <= j < tm and i + j...  0.69 us
    ppermute x2, starting transfers between devices, core_swap(): return lax.ppermute(x, 'tm', [(i, i ^ 1) for i in range(tm)])  0.68 us
  transfers between devices with their start and end apart: 6, of which 4 were waited for; matrix products, arithmetic and copies ran while one was open for 0% of the time, Pallas kernels for 32%

profile of v6, /device:TPU:135, one launch (start us, length us, event | category | flops | bytes accessed | tf_op | source)
XLA Modules:
  0.0 25.1 jit_solution(12640802109261477495)
XLA Ops:
  0.0 0.7 %collective-permute-start = (bf16[2,64,8,256]{3,2,1,0:T(8,128)(2,1)}, bf16[2,64,8,256]{3,2,1,0:T(8,128)(2,1)S(1)}, u32[]{:S(2)}, u32[]{:S(2)}) collective-permute-start(bf16[2,64,8,256]{3,2,1,0:T(8,128)(2,1)} %states_ref.3), channel_id=1, source_target_pairs={{0,16},{16,0},{32,48},{48,32},{64,80},{80,64},{96,112},{112,96},{1... | collective-permute-start | bytes 1572872 | tf_op jit(solution)/shard_map/ppermute | solution.py:20
  0.7 1.9 %prepare_kernel.1 = (bf16[8,128,256]{2,1,0:T(8,128)(2,1)S(1)}, bf16[192,2304]{1,0:T(8,128)(2,1)S(1)}, bf16[192,1152]{1,0:T(8,128)(2,1)S(1)}, bf16[192,1152]{1,0:T(8,128)(2,1)S(1)}, bf16[128,192]{1,0:T(8,128)(2,1)S(1)}) custom-call(bf16[2,64,8,256]{3,2,1,0:T(8,128)(2,1)} %states_ref.3, bf16[3,3,96,320]{3,2,1,0:T(8,128)(2,1)} %first_ref.1, ...), custom_call_target="tpu_custom_call" | custom-call | bytes 1048576 | tf_op jit(solution)/shard_map/prepare_kernel/pallas_call | solution.py:373
  2.6 0.0 collective-permute-done.partner_ref
  2.6 0.1 edge_kernel.1
  2.7 3.1 %collective-permute-start.1 = (bf16[2,256,256]{2,1,0:T(8,128)(2,1)S(1)}, bf16[2,256,256]{2,1,0:T(8,128)(2,1)S(1)}, u32[]{:S(2)}, u32[]{:S(2)}) collective-permute-start(bf16[2,256,256]{2,1,0:T(8,128)(2,1)S(1)} %edge_kernel.1), channel_id=1, source_target_pairs={{0,32},{1,16},{2,17},{3,18},{4,19},{5,20},{6,21},{7,22},{8,23},{9,... | collective-permute-start | bytes 786440 | tf_op jit(solution)/shard_map/ppermute | solution.py:44
  5.8 0.0 copy-start
  5.8 1.7 %near_kernel.1 = (bf16[8,128,256]{2,1,0:T(8,128)(2,1)S(1)}, bf16[8,2,256,256]{3,2,1,0:T(8,128)(2,1)S(1)}, f32[5,192,256]{2,1,0:T(8,128)S(1)}, f32[2,192,256]{2,1,0:T(8,128)S(1)}) custom-call(bf16[8,128,256]{2,1,0:T(8,128)(2,1)S(1)} %get-tuple-element.30.own_ref, bf16[2,64,8,256]{3,2,1,0:T(8,128)(2,1)S(1)} %collective-permute-done.partner_ref, ...), custom_call_target="tpu_custom_call" | custom-call | flops 2000000000 | bytes 1048576 | tf_op jit(solution)/shard_map/near_kernel/pallas_call | solution.py:373
  7.6 0.0 copy-done
  7.6 1.9 %collective-permute-start.5 = (bf16[2,64,8,256]{3,2,1,0:T(8,128)(2,1)S(1)}, bf16[2,64,8,256]{3,2,1,0:T(8,128)(2,1)S(1)}, u32[]{:S(2)}, u32[]{:S(2)}) collective-permute-start(bf16[2,64,8,256]{3,2,1,0:T(8,128)(2,1)S(1)} %copy-done), channel_id=1, source_target_pairs={{112,128},{128,112},{113,129},{129,113},{114,130},{130,114},{115,1... | collective-permute-start | bytes 1572872 | tf_op jit(solution)/shard_map/ppermute | solution.py:34
  9.5 0.7 %collective-permute-start.4 = (bf16[2,64,8,256]{3,2,1,0:T(8,128)(2,1)S(1)}, bf16[2,64,8,256]{3,2,1,0:T(8,128)(2,1)S(1)}, u32[]{:S(2)}, u32[]{:S(2)}) collective-permute-start(bf16[2,64,8,256]{3,2,1,0:T(8,128)(2,1)S(1)} %copy-done), channel_id=1, source_target_pairs={{16,32},{32,16},{48,64},{64,48},{80,96},{96,80},{144,160},{160,144... | collective-permute-start | bytes 1572872 | tf_op jit(solution)/shard_map/ppermute | solution.py:29
  10.2 0.0 copy-start.1
  10.2 0.0 copy-start.2
  10.2 0.0 copy-start.3
  10.2 0.4 %rest_kernel.1.part_late_ref = f32[1,192,256]{2,1,0:T(8,128)S(1)} custom-call(bf16[8,128,256]{2,1,0:T(8,128)(2,1)S(1)} %get-tuple-element.30.own_ref, bf16[8,128,256]{2,1,0:T(8,128)(2,1)S(1)} %get-tuple-element.35.partner_rows_ref, bf16[8,2,256,256]{3,2,1,0:T(8,128)(2,1)S(1)} %get-tuple-element.36.sides_ref.near_ref, ...), custom_call_target="tpu_custom_call" | custom-call | bytes 1048576 | tf_op jit(solution)/shard_map/rest_kernel/pallas_call | solution.py:373
  10.7 2.2 %collective-permute-done.1.rows_a_ref = bf16[2,256,256]{2,1,0:T(8,128)(2,1)S(1)} collective-permute-done((bf16[2,256,256]{2,1,0:T(8,128)(2,1)S(1)}, bf16[2,256,256]{2,1,0:T(8,128)(2,1)S(1)}, u32[]{:S(2)}, u32[]{:S(2)}) %collective-permute-start.1) | collective-permute-done | bytes 262176 | tf_op jit(solution)/shard_map/ppermute | solution.py:44
  12.9 0.0 collective-permute-start.2
  14.2 0.2 collective-permute-done.2.rows_b_ref
  14.5 1.8 %collective-permute-start.3 = (bf16[4,128,256]{2,1,0:T(8,128)(2,1)S(1)}, bf16[4,128,256]{2,1,0:T(8,128)(2,1)S(1)}, u32[]{:S(2)}, u32[]{:S(2)}) collective-permute-start(bf16[4,128,256]{2,1,0:T(8,128)(2,1)S(1)} %corner_kernel.1), channel_id=1, source_target_pairs={{0,240},{16,32},{32,16},{48,64},{64,48},{80,96},{96,80},{112,128},... | collective-permute-start | bytes 786440 | tf_op jit(solution)/shard_map/ppermute | solution.py:24
  16.3 0.0 copy-done.1
  16.3 0.0 copy-done.2
  16.3 0.0 copy-done.3
  16.3 0.3 %base_kernel.1 = (f32[2,2,64,8,128]{4,3,2,1,0:T(8,128)S(1)}, f32[2,8,256]{2,1,0:T(8,128)S(1)}) custom-call(f32[1]{0:T(128)S(6)} %copy.14.now_ref, f32[1]{0:T(128)S(6)} %copy.15.next_ref, s32[2,8,256]{2,1,0:T(8,128)S(1)} %copy-done.3, bf16[2,64,8,256]{3,2,1,0:T(8,128)(2,1)S(1)} %copy-done, bf16[2,64,8,256]{3,2,1,0:T(8,128)(2,1)S(1)} %copy-done.2, ...), custom_call_target="tpu_custom_call" | custom-call | flops 100000000 | bytes 1048576 | tf_op jit(solution)/shard_map/base_kernel/pallas_call | solution.py:373
  16.6 0.9 %rim_kernel.1.rim_part_ref = f32[4,192,256]{2,1,0:T(8,128)S(1)} custom-call(bf16[2,256,256]{2,1,0:T(8,128)(2,1)S(1)} %collective-permute-done.1.rows_a_ref, bf16[2,256,256]{2,1,0:T(8,128)(2,1)S(1)} %collective-permute-done.2.rows_b_ref, bf16[8,128,256]{2,1,0:T(8,128)(2,1)S(1)} %get-tuple-element.30.own_ref, ...), custom_call_target="tpu_custom_call" | custom-call | flops 1000000000 | bytes 1048576 | tf_op jit(solution)/shard_map/rim_kernel/pallas_call | solution.py:373
  17.5 2.7 %collective-permute-done.5.middle_ref = bf16[2,64,8,256]{3,2,1,0:T(8,128)(2,1)S(1)} collective-permute-done((bf16[2,64,8,256]{3,2,1,0:T(8,128)(2,1)S(1)}, bf16[2,64,8,256]{3,2,1,0:T(8,128)(2,1)S(1)}, u32[]{:S(2)}, u32[]{:S(2)}) %collective-permute-start.5) | collective-permute-done | bytes 524320 | tf_op jit(solution)/shard_map/ppermute | solution.py:34
  20.2 0.0 collective-permute-done.4.most_ref
  20.2 1.5 %far_kernel.1 = (bf16[6,3,192,256]{3,2,1,0:T(8,128)(2,1)S(1)}, f32[4,192,256]{2,1,0:T(8,128)S(1)}) custom-call(bf16[2,64,8,256]{3,2,1,0:T(8,128)(2,1)S(1)} %collective-permute-done.4.most_ref, bf16[2,64,8,256]{3,2,1,0:T(8,128)(2,1)S(1)} %collective-permute-done.5.middle_ref, f32[5,192,256]{2,1,0:T(8,128)S(1)} %get-tuple-element.41.part_ref, ...), custom_call_target="tpu_custom_call" | custom-call | flops 1000000000 | bytes 1048576 | tf_op jit(solution)/shard_map/far_kernel/pallas_call | solution.py:373
  21.7 1.2 %middle_kernel.1 = (f32[2,2,192,256]{3,2,1,0:T(8,128)S(1)}, f32[2,2,64,8,128]{4,3,2,1,0:T(8,128)S(1)}) custom-call(bf16[6,3,192,256]{3,2,1,0:T(8,128)(2,1)S(1)} %get-tuple-element.50.hid_ref, bf16[192,1152]{1,0:T(8,128)(2,1)S(1)} %get-tuple-element.48.w_two_ref, bf16[128,192]{1,0:T(8,128)(2,1)S(1)} %get-tuple-element.49.proj_ref, ...), custom_call_target="tpu_custom_call", output_to_operand_aliasing={{1}: (4, {})} | custom-call | flops 1000000000 | bytes 1048576 | tf_op jit(solution)/shard_map/middle_kernel/pallas_call | solution.py:373
  22.9 0.1 collective-permute-done.3.corner_ref
  23.0 2.2 %outer_kernel.1 = (f32[2,64,8,256]{3,2,1,0:T(8,128)}, f32[2,2,64,8,128]{4,3,2,1,0:T(8,128)S(1)}) custom-call(bf16[4,128,256]{2,1,0:T(8,128)(2,1)S(1)} %collective-permute-done.3.corner_ref, f32[4,192,256]{2,1,0:T(8,128)S(1)} %get-tuple-element.47.part_ref, bf16[192,1152]{1,0:T(8,128)(2,1)S(1)} %get-tuple-element.44.w_far_ref, ...), custom_call_target="tpu_custom_call", output_to_operand_aliasing={{1}: (7, {})} | custom-call | flops 1000000000 | bytes 1048576 | tf_op jit(solution)/shard_map/outer_kernel/pallas_call | solution.py:373
  (1 shorter events, 0.0 us)
Async XLA Ops:
  0.0 2.6 %collective-permute-start = (bf16[2,64,8,256]{3,2,1,0:T(8,128)(2,1)}, bf16[2,64,8,256]{3,2,1,0:T(8,128)(2,1)S(1)}, u32[]{:S(2)}, u32[]{:S(2)}) collective-permute-start(bf16[2,64,8,256]{3,2,1,0:T(8,128)(2,1)} %states_ref.3), channel_id=1, source_target_pairs={{0,16},{16,0},{32,48},{48,32},{64,80},{80,64},{96,112},{112,96},{1... | collective-permute-start | bytes 1572872 | tf_op jit(solution)/shard_map/ppermute | solution.py:20
  2.7 10.2 %collective-permute-start.1 = (bf16[2,256,256]{2,1,0:T(8,128)(2,1)S(1)}, bf16[2,256,256]{2,1,0:T(8,128)(2,1)S(1)}, u32[]{:S(2)}, u32[]{:S(2)}) collective-permute-start(bf16[2,256,256]{2,1,0:T(8,128)(2,1)S(1)} %edge_kernel.1), channel_id=1, source_target_pairs={{0,32},{1,16},{2,17},{3,18},{4,19},{5,20},{6,21},{7,22},{8,23},{9,... | collective-permute-start | bytes 786440 | tf_op jit(solution)/shard_map/ppermute | solution.py:44
  5.8 1.7 %copy-start = (bf16[2,64,8,256]{3,2,1,0:T(8,128)(2,1)S(1)}, bf16[2,64,8,256]{3,2,1,0:T(8,128)(2,1)}, u32[]{:S(2)}) copy-start(bf16[2,64,8,256]{3,2,1,0:T(8,128)(2,1)} %states_ref.3) | copy-start | bytes 1572868
  7.6 12.6 %collective-permute-start.5 = (bf16[2,64,8,256]{3,2,1,0:T(8,128)(2,1)S(1)}, bf16[2,64,8,256]{3,2,1,0:T(8,128)(2,1)S(1)}, u32[]{:S(2)}, u32[]{:S(2)}) collective-permute-start(bf16[2,64,8,256]{3,2,1,0:T(8,128)(2,1)S(1)} %copy-done), channel_id=1, source_target_pairs={{112,128},{128,112},{113,129},{129,113},{114,130},{130,114},{115,1... | collective-permute-start | bytes 1572872 | tf_op jit(solution)/shard_map/ppermute | solution.py:34
  9.5 10.7 %collective-permute-start.4 = (bf16[2,64,8,256]{3,2,1,0:T(8,128)(2,1)S(1)}, bf16[2,64,8,256]{3,2,1,0:T(8,128)(2,1)S(1)}, u32[]{:S(2)}, u32[]{:S(2)}) collective-permute-start(bf16[2,64,8,256]{3,2,1,0:T(8,128)(2,1)S(1)} %copy-done), channel_id=1, source_target_pairs={{16,32},{32,16},{48,64},{64,48},{80,96},{96,80},{144,160},{160,144... | collective-permute-start | bytes 1572872 | tf_op jit(solution)/shard_map/ppermute | solution.py:29
  10.2 6.1 %copy-start.1 = (f32[2,64,8,256]{3,2,1,0:T(8,128)S(1)}, f32[2,64,8,256]{3,2,1,0:T(8,128)}, u32[]{:S(2)}) copy-start(f32[2,64,8,256]{3,2,1,0:T(8,128)} %noise_ref) | copy-start | bytes 3145732
  10.2 6.0 %copy-start.2 = (bf16[2,64,8,256]{3,2,1,0:T(8,128)(2,1)S(1)}, bf16[2,64,8,256]{3,2,1,0:T(8,128)(2,1)}, u32[]{:S(2)}) copy-start(bf16[2,64,8,256]{3,2,1,0:T(8,128)(2,1)} %observed_ref.1) | copy-start | bytes 1572868
  10.2 6.0 %copy-start.3 = (s32[2,8,256]{2,1,0:T(8,128)S(1)}, s32[2,8,256]{2,1,0:T(8,128)}, u32[]{:S(2)}) copy-start(s32[2,8,256]{2,1,0:T(8,128)} %mask_ref.1) | copy-start | bytes 49156
  12.9 1.5 %collective-permute-start.2 = (bf16[2,256,256]{2,1,0:T(8,128)(2,1)S(1)}, bf16[2,256,256]{2,1,0:T(8,128)(2,1)S(1)}, u32[]{:S(2)}, u32[]{:S(2)}) collective-permute-start(bf16[2,256,256]{2,1,0:T(8,128)(2,1)S(1)} %collective-permute-done.1.rows_a_ref), channel_id=1, source_target_pairs={{0,16},{16,0},{32,48},{48,32},{64,80},{80,64},{96,112},{112,96},{1... | collective-permute-start | bytes 786440 | tf_op jit(solution)/shard_map/ppermute | solution.py:20
  14.5 8.5 %collective-permute-start.3 = (bf16[4,128,256]{2,1,0:T(8,128)(2,1)S(1)}, bf16[4,128,256]{2,1,0:T(8,128)(2,1)S(1)}, u32[]{:S(2)}, u32[]{:S(2)}) collective-permute-start(bf16[4,128,256]{2,1,0:T(8,128)(2,1)S(1)} %corner_kernel.1), channel_id=1, source_target_pairs={{0,240},{16,32},{32,16},{48,64},{64,48},{80,96},{96,80},{112,128},... | collective-permute-start | bytes 786440 | tf_op jit(solution)/shard_map/ppermute | solution.py:24

commit v7 on v4

--- a/solution.py
+++ b/solution.py
@@ -194,7 +194,6 @@
         if l == 1:
             edge_part_ref[0] = dot(w_near_ref[:, 3 * FOUR :], near_rows(sides_ref, own_ref, partner_rows_ref, 0, 1))
     edge_part_ref[1] = dot(w_near_ref[:, : 6 * FOUR], near_rows(sides_ref, own_ref, partner_rows_ref, 6, 7))
-    edge_part_ref[2] = dot(w_near_ref[:, : 3 * FOUR], near_rows(sides_ref, own_ref, partner_rows_ref, 7))
 
 
 def rest_kernel(own_ref, partner_rows_ref, sides_ref, w_near_ref, part_ref):
@@ -250,7 +249,7 @@
     part_ref[0] = near(above[0], above[1], tile(0))
     part_ref[1] = edge_part_ref[0] + dot(w_near_ref[:, : 3 * FOUR], above[1])
     part_ref[2] = edge_part_ref[1] + dot(w_near_ref[:, 6 * FOUR :], below[0])
-    part_ref[3] = edge_part_ref[2] + dot(w_near_ref[:, 3 * FOUR :], jnp.concatenate(below, axis=0))
+    part_ref[3] = near(tile(7), below[0], below[1])
 
 
 def far_kernel(
@@ -423,7 +422,7 @@
     early = 5
     partner_rows, near_sides, part, edge_part = call(
         near_kernel,
-        [rows_shape, ((ROWS, 2, FOUR, WID), BF16), ((early, 2 * HID, WID), F32), ((3, 2 * HID, WID), F32)],
+        [rows_shape, ((ROWS, 2, FOUR, WID), BF16), ((early, 2 * HID, WID), F32), ((2, 2 * HID, WID), F32)],
         [own, partner, w_near],
         mib=8,
         flops=2 * 10**9,

time: 25.4 us -> 25.3 us (level)
  transfers between devices with their start and end apart: 6 -> 6, of which waited for: 4 -> 4; matrix products, arithmetic and copies ran while one was open for 0% -> 0% of each run, Pallas kernels for 31% -> 32%
where the time goes in v7:
time: 25.3 us; the launch traced here: 25.1 us
  Pallas kernels  10.2 us (40%)
  starting transfers between devices  8.2 us (32%)
  waiting for transfers between devices  5.29 us (21%)
  between operations  1.42 us (6%)
    pallas_call x10, Pallas kernels, call(): pl.pallas_call(kernel, out_shape=shapes, in_specs=[SMEM] * scalars + [VME...  10.2 us
    ppermute x1, starting transfers between devices, row_swap(): return lax.ppermute(x, AXES, pairs)  3.1 us
    ppermute x1, waiting for transfers between devices, middle_swap(): return lax.ppermute(x, 'tm', [(low, low + 1), (low + 1, low)])  2.69 us
    ppermute x1, waiting for transfers between devices, row_swap(): return lax.ppermute(x, AXES, pairs)  2.25 us
    ppermute x1, starting transfers between devices, middle_swap(): return lax.ppermute(x, 'tm', [(low, low + 1), (low + 1, low)])  1.94 us
    ppermute x1, starting transfers between devices, side_swap(): lax.ppermute(x, 'tm', [(i, ((i + 1 ^ 1) - 1) % tm) for i in range(tm)])  1.78 us
    ppermute x1, starting transfers between devices, most_swap(): lax.ppermute(x, 'tm', [(i, j) for i, j in pairs if 0 <= j < tm and i + j...  0.69 us
    ppermute x2, starting transfers between devices, core_swap(): return lax.ppermute(x, 'tm', [(i, i ^ 1) for i in range(tm)])  0.68 us
  transfers between devices with their start and end apart: 6, of which 4 were waited for; matrix products, arithmetic and copies ran while one was open for 0% of the time, Pallas kernels for 32%

profile of v7, /device:TPU:135, one launch (start us, length us, event | category | flops | bytes accessed | tf_op | source)
XLA Modules:
  0.0 25.1 jit_solution(18252760240444500605)
XLA Ops:
  0.0 0.7 %collective-permute-start = (bf16[2,64,8,256]{3,2,1,0:T(8,128)(2,1)}, bf16[2,64,8,256]{3,2,1,0:T(8,128)(2,1)S(1)}, u32[]{:S(2)}, u32[]{:S(2)}) collective-permute-start(bf16[2,64,8,256]{3,2,1,0:T(8,128)(2,1)} %states_ref.3), channel_id=1, source_target_pairs={{0,16},{16,0},{32,48},{48,32},{64,80},{80,64},{96,112},{112,96},{1... | collective-permute-start | bytes 1572872 | tf_op jit(solution)/shard_map/ppermute | solution.py:20
  0.7 1.9 %prepare_kernel.1 = (bf16[8,128,256]{2,1,0:T(8,128)(2,1)S(1)}, bf16[192,2304]{1,0:T(8,128)(2,1)S(1)}, bf16[192,1152]{1,0:T(8,128)(2,1)S(1)}, bf16[192,1152]{1,0:T(8,128)(2,1)S(1)}, bf16[128,192]{1,0:T(8,128)(2,1)S(1)}) custom-call(bf16[2,64,8,256]{3,2,1,0:T(8,128)(2,1)} %states_ref.3, bf16[3,3,96,320]{3,2,1,0:T(8,128)(2,1)} %first_ref.1, ...), custom_call_target="tpu_custom_call" | custom-call | bytes 1048576 | tf_op jit(solution)/shard_map/prepare_kernel/pallas_call | solution.py:370
  2.6 0.0 collective-permute-done.partner_ref
  2.6 0.1 edge_kernel.1
  2.7 3.1 %collective-permute-start.1 = (bf16[2,256,256]{2,1,0:T(8,128)(2,1)S(1)}, bf16[2,256,256]{2,1,0:T(8,128)(2,1)S(1)}, u32[]{:S(2)}, u32[]{:S(2)}) collective-permute-start(bf16[2,256,256]{2,1,0:T(8,128)(2,1)S(1)} %edge_kernel.1), channel_id=1, source_target_pairs={{0,32},{1,16},{2,17},{3,18},{4,19},{5,20},{6,21},{7,22},{8,23},{9,... | collective-permute-start | bytes 786440 | tf_op jit(solution)/shard_map/ppermute | solution.py:44
  5.8 0.0 copy-start
  5.8 1.7 %near_kernel.1 = (bf16[8,128,256]{2,1,0:T(8,128)(2,1)S(1)}, bf16[8,2,256,256]{3,2,1,0:T(8,128)(2,1)S(1)}, f32[5,192,256]{2,1,0:T(8,128)S(1)}, f32[2,192,256]{2,1,0:T(8,128)S(1)}) custom-call(bf16[8,128,256]{2,1,0:T(8,128)(2,1)S(1)} %get-tuple-element.30.own_ref, bf16[2,64,8,256]{3,2,1,0:T(8,128)(2,1)S(1)} %collective-permute-done.partner_ref, ...), custom_call_target="tpu_custom_call" | custom-call | flops 2000000000 | bytes 1048576 | tf_op jit(solution)/shard_map/near_kernel/pallas_call | solution.py:370
  7.5 0.0 copy-done
  7.5 1.9 %collective-permute-start.5 = (bf16[2,64,8,256]{3,2,1,0:T(8,128)(2,1)S(1)}, bf16[2,64,8,256]{3,2,1,0:T(8,128)(2,1)S(1)}, u32[]{:S(2)}, u32[]{:S(2)}) collective-permute-start(bf16[2,64,8,256]{3,2,1,0:T(8,128)(2,1)S(1)} %copy-done), channel_id=1, source_target_pairs={{112,128},{128,112},{113,129},{129,113},{114,130},{130,114},{115,1... | collective-permute-start | bytes 1572872 | tf_op jit(solution)/shard_map/ppermute | solution.py:34
  9.5 0.7 %collective-permute-start.4 = (bf16[2,64,8,256]{3,2,1,0:T(8,128)(2,1)S(1)}, bf16[2,64,8,256]{3,2,1,0:T(8,128)(2,1)S(1)}, u32[]{:S(2)}, u32[]{:S(2)}) collective-permute-start(bf16[2,64,8,256]{3,2,1,0:T(8,128)(2,1)S(1)} %copy-done), channel_id=1, source_target_pairs={{16,32},{32,16},{48,64},{64,48},{80,96},{96,80},{144,160},{160,144... | collective-permute-start | bytes 1572872 | tf_op jit(solution)/shard_map/ppermute | solution.py:29
  10.2 0.0 copy-start.1
  10.2 0.0 copy-start.2
  10.2 0.0 copy-start.3
  10.2 0.4 %rest_kernel.1.part_late_ref = f32[1,192,256]{2,1,0:T(8,128)S(1)} custom-call(bf16[8,128,256]{2,1,0:T(8,128)(2,1)S(1)} %get-tuple-element.30.own_ref, bf16[8,128,256]{2,1,0:T(8,128)(2,1)S(1)} %get-tuple-element.35.partner_rows_ref, bf16[8,2,256,256]{3,2,1,0:T(8,128)(2,1)S(1)} %get-tuple-element.36.sides_ref.near_ref, ...), custom_call_target="tpu_custom_call" | custom-call | bytes 1048576 | tf_op jit(solution)/shard_map/rest_kernel/pallas_call | solution.py:370
  10.6 2.2 %collective-permute-done.1.rows_a_ref = bf16[2,256,256]{2,1,0:T(8,128)(2,1)S(1)} collective-permute-done((bf16[2,256,256]{2,1,0:T(8,128)(2,1)S(1)}, bf16[2,256,256]{2,1,0:T(8,128)(2,1)S(1)}, u32[]{:S(2)}, u32[]{:S(2)}) %collective-permute-start.1) | collective-permute-done | bytes 262176 | tf_op jit(solution)/shard_map/ppermute | solution.py:44
  12.9 0.0 collective-permute-start.2
  14.2 0.2 collective-permute-done.2.rows_b_ref
  14.5 1.8 %collective-permute-start.3 = (bf16[4,128,256]{2,1,0:T(8,128)(2,1)S(1)}, bf16[4,128,256]{2,1,0:T(8,128)(2,1)S(1)}, u32[]{:S(2)}, u32[]{:S(2)}) collective-permute-start(bf16[4,128,256]{2,1,0:T(8,128)(2,1)S(1)} %corner_kernel.1), channel_id=1, source_target_pairs={{0,240},{16,32},{32,16},{48,64},{64,48},{80,96},{96,80},{112,128},... | collective-permute-start | bytes 786440 | tf_op jit(solution)/shard_map/ppermute | solution.py:24
  16.2 0.0 copy-done.1
  16.3 0.0 copy-done.2
  16.3 0.0 copy-done.3
  16.3 0.3 %base_kernel.1 = (f32[2,2,64,8,128]{4,3,2,1,0:T(8,128)S(1)}, f32[2,8,256]{2,1,0:T(8,128)S(1)}) custom-call(f32[1]{0:T(128)S(6)} %copy.14.now_ref, f32[1]{0:T(128)S(6)} %copy.15.next_ref, s32[2,8,256]{2,1,0:T(8,128)S(1)} %copy-done.3, bf16[2,64,8,256]{3,2,1,0:T(8,128)(2,1)S(1)} %copy-done, bf16[2,64,8,256]{3,2,1,0:T(8,128)(2,1)S(1)} %copy-done.2, ...), custom_call_target="tpu_custom_call" | custom-call | flops 100000000 | bytes 1048576 | tf_op jit(solution)/shard_map/base_kernel/pallas_call | solution.py:370
  16.6 0.9 %rim_kernel.1.rim_part_ref = f32[4,192,256]{2,1,0:T(8,128)S(1)} custom-call(bf16[2,256,256]{2,1,0:T(8,128)(2,1)S(1)} %collective-permute-done.1.rows_a_ref, bf16[2,256,256]{2,1,0:T(8,128)(2,1)S(1)} %collective-permute-done.2.rows_b_ref, bf16[8,128,256]{2,1,0:T(8,128)(2,1)S(1)} %get-tuple-element.30.own_ref, ...), custom_call_target="tpu_custom_call" | custom-call | flops 1000000000 | bytes 1048576 | tf_op jit(solution)/shard_map/rim_kernel/pallas_call | solution.py:370
  17.5 2.7 %collective-permute-done.5.middle_ref = bf16[2,64,8,256]{3,2,1,0:T(8,128)(2,1)S(1)} collective-permute-done((bf16[2,64,8,256]{3,2,1,0:T(8,128)(2,1)S(1)}, bf16[2,64,8,256]{3,2,1,0:T(8,128)(2,1)S(1)}, u32[]{:S(2)}, u32[]{:S(2)}) %collective-permute-start.5) | collective-permute-done | bytes 524320 | tf_op jit(solution)/shard_map/ppermute | solution.py:34
  20.2 0.0 collective-permute-done.4.most_ref
  20.2 1.5 %far_kernel.1 = (bf16[6,3,192,256]{3,2,1,0:T(8,128)(2,1)S(1)}, f32[4,192,256]{2,1,0:T(8,128)S(1)}) custom-call(bf16[2,64,8,256]{3,2,1,0:T(8,128)(2,1)S(1)} %collective-permute-done.4.most_ref, bf16[2,64,8,256]{3,2,1,0:T(8,128)(2,1)S(1)} %collective-permute-done.5.middle_ref, f32[5,192,256]{2,1,0:T(8,128)S(1)} %get-tuple-element.41.part_ref, ...), custom_call_target="tpu_custom_call" | custom-call | flops 1000000000 | bytes 1048576 | tf_op jit(solution)/shard_map/far_kernel/pallas_call | solution.py:370
  21.7 1.2 %middle_kernel.1 = (f32[2,2,192,256]{3,2,1,0:T(8,128)S(1)}, f32[2,2,64,8,128]{4,3,2,1,0:T(8,128)S(1)}) custom-call(bf16[6,3,192,256]{3,2,1,0:T(8,128)(2,1)S(1)} %get-tuple-element.50.hid_ref, bf16[192,1152]{1,0:T(8,128)(2,1)S(1)} %get-tuple-element.48.w_two_ref, bf16[128,192]{1,0:T(8,128)(2,1)S(1)} %get-tuple-element.49.proj_ref, ...), custom_call_target="tpu_custom_call", output_to_operand_aliasing={{1}: (4, {})} | custom-call | flops 1000000000 | bytes 1048576 | tf_op jit(solution)/shard_map/middle_kernel/pallas_call | solution.py:370
  22.9 0.1 collective-permute-done.3.corner_ref
  23.0 2.2 %outer_kernel.1 = (f32[2,64,8,256]{3,2,1,0:T(8,128)}, f32[2,2,64,8,128]{4,3,2,1,0:T(8,128)S(1)}) custom-call(bf16[4,128,256]{2,1,0:T(8,128)(2,1)S(1)} %collective-permute-done.3.corner_ref, f32[4,192,256]{2,1,0:T(8,128)S(1)} %get-tuple-element.47.part_ref, bf16[192,1152]{1,0:T(8,128)(2,1)S(1)} %get-tuple-element.44.w_far_ref, ...), custom_call_target="tpu_custom_call", output_to_operand_aliasing={{1}: (7, {})} | custom-call | flops 1000000000 | bytes 1048576 | tf_op jit(solution)/shard_map/outer_kernel/pallas_call | solution.py:370
  (1 shorter events, 0.0 us)
Async XLA Ops:
  0.0 2.6 %collective-permute-start = (bf16[2,64,8,256]{3,2,1,0:T(8,128)(2,1)}, bf16[2,64,8,256]{3,2,1,0:T(8,128)(2,1)S(1)}, u32[]{:S(2)}, u32[]{:S(2)}) collective-permute-start(bf16[2,64,8,256]{3,2,1,0:T(8,128)(2,1)} %states_ref.3), channel_id=1, source_target_pairs={{0,16},{16,0},{32,48},{48,32},{64,80},{80,64},{96,112},{112,96},{1... | collective-permute-start | bytes 1572872 | tf_op jit(solution)/shard_map/ppermute | solution.py:20
  2.7 10.2 %collective-permute-start.1 = (bf16[2,256,256]{2,1,0:T(8,128)(2,1)S(1)}, bf16[2,256,256]{2,1,0:T(8,128)(2,1)S(1)}, u32[]{:S(2)}, u32[]{:S(2)}) collective-permute-start(bf16[2,256,256]{2,1,0:T(8,128)(2,1)S(1)} %edge_kernel.1), channel_id=1, source_target_pairs={{0,32},{1,16},{2,17},{3,18},{4,19},{5,20},{6,21},{7,22},{8,23},{9,... | collective-permute-start | bytes 786440 | tf_op jit(solution)/shard_map/ppermute | solution.py:44
  5.8 1.7 %copy-start = (bf16[2,64,8,256]{3,2,1,0:T(8,128)(2,1)S(1)}, bf16[2,64,8,256]{3,2,1,0:T(8,128)(2,1)}, u32[]{:S(2)}) copy-start(bf16[2,64,8,256]{3,2,1,0:T(8,128)(2,1)} %states_ref.3) | copy-start | bytes 1572868
  7.5 12.6 %collective-permute-start.5 = (bf16[2,64,8,256]{3,2,1,0:T(8,128)(2,1)S(1)}, bf16[2,64,8,256]{3,2,1,0:T(8,128)(2,1)S(1)}, u32[]{:S(2)}, u32[]{:S(2)}) collective-permute-start(bf16[2,64,8,256]{3,2,1,0:T(8,128)(2,1)S(1)} %copy-done), channel_id=1, source_target_pairs={{112,128},{128,112},{113,129},{129,113},{114,130},{130,114},{115,1... | collective-permute-start | bytes 1572872 | tf_op jit(solution)/shard_map/ppermute | solution.py:34
  9.5 10.7 %collective-permute-start.4 = (bf16[2,64,8,256]{3,2,1,0:T(8,128)(2,1)S(1)}, bf16[2,64,8,256]{3,2,1,0:T(8,128)(2,1)S(1)}, u32[]{:S(2)}, u32[]{:S(2)}) collective-permute-start(bf16[2,64,8,256]{3,2,1,0:T(8,128)(2,1)S(1)} %copy-done), channel_id=1, source_target_pairs={{16,32},{32,16},{48,64},{64,48},{80,96},{96,80},{144,160},{160,144... | collective-permute-start | bytes 1572872 | tf_op jit(solution)/shard_map/ppermute | solution.py:29
  10.2 6.1 %copy-start.1 = (f32[2,64,8,256]{3,2,1,0:T(8,128)S(1)}, f32[2,64,8,256]{3,2,1,0:T(8,128)}, u32[]{:S(2)}) copy-start(f32[2,64,8,256]{3,2,1,0:T(8,128)} %noise_ref) | copy-start | bytes 3145732
  10.2 6.0 %copy-start.2 = (bf16[2,64,8,256]{3,2,1,0:T(8,128)(2,1)S(1)}, bf16[2,64,8,256]{3,2,1,0:T(8,128)(2,1)}, u32[]{:S(2)}) copy-start(bf16[2,64,8,256]{3,2,1,0:T(8,128)(2,1)} %observed_ref.1) | copy-start | bytes 1572868
  10.2 6.0 %copy-start.3 = (s32[2,8,256]{2,1,0:T(8,128)S(1)}, s32[2,8,256]{2,1,0:T(8,128)}, u32[]{:S(2)}) copy-start(s32[2,8,256]{2,1,0:T(8,128)} %mask_ref.1) | copy-start | bytes 49156
  12.9 1.5 %collective-permute-start.2 = (bf16[2,256,256]{2,1,0:T(8,128)(2,1)S(1)}, bf16[2,256,256]{2,1,0:T(8,128)(2,1)S(1)}, u32[]{:S(2)}, u32[]{:S(2)}) collective-permute-start(bf16[2,256,256]{2,1,0:T(8,128)(2,1)S(1)} %collective-permute-done.1.rows_a_ref), channel_id=1, source_target_pairs={{0,16},{16,0},{32,48},{48,32},{64,80},{80,64},{96,112},{112,96},{1... | collective-permute-start | bytes 786440 | tf_op jit(solution)/shard_map/ppermute | solution.py:20
  14.5 8.5 %collective-permute-start.3 = (bf16[4,128,256]{2,1,0:T(8,128)(2,1)S(1)}, bf16[4,128,256]{2,1,0:T(8,128)(2,1)S(1)}, u32[]{:S(2)}, u32[]{:S(2)}) collective-permute-start(bf16[4,128,256]{2,1,0:T(8,128)(2,1)S(1)} %corner_kernel.1), channel_id=1, source_target_pairs={{0,240},{16,32},{32,16},{48,64},{64,48},{80,96},{96,80},{112,128},... | collective-permute-start | bytes 786440 | tf_op jit(solution)/shard_map/ppermute | solution.py:24
